TPU v7x, 32 devices: a whole 2x2x4 slice. The times are simulated.
32 devices in a mesh: dp: 2 (over core), expert: 4 (over z), shard: 4 (over y, x).
Axes of the slice: x: 2, y: 2, z: 4, core: 2. Of those that a mesh axis runs over, the one named last changes fastest.
Arguments:
- hidden_in: bfloat16 [6144, 2048], P(('dp', 'expert', 'shard')), may hold values from -6 to 6
- grad_out: bfloat16 [6144, 2048], P(('dp', 'expert', 'shard')), may hold values from -6 to 6
- doc_lengths: int32 [8, 4], P(('dp', 'expert')), may hold values from 1 to 576, as said below
- expert_ids: int32 [6144, 8], P(('dp', 'expert', 'shard')), may hold values from 0 to 15, all different within a row; in each aligned block of 192 rows (0 to 191, 192 to 383, ...) at most 120 rows name the same one
- attn_gain: bfloat16 [2048], P('shard'), may hold values from 0.099609375 to 1.8984375
- query_gain: bfloat16 [2048], P('shard'), may hold values from 0.099609375 to 1.8984375
- key_gain: bfloat16 [2048], P('shard'), may hold values from 0.099609375 to 1.8984375
- mlp_gain: bfloat16 [2048], P('shard'), may hold values from 0.099609375 to 1.8984375
- w_query: bfloat16 [2048, 2048], P('shard'), may hold values from -0.125 to 0.125
- w_key: bfloat16 [2048, 2048], P('shard'), may hold values from -0.125 to 0.125
- w_value: bfloat16 [2048, 2048], P('shard'), may hold values from -0.125 to 0.125
- w_output: bfloat16 [2048, 2048], P('shard'), may hold values from -0.75 to 0.75
- w_router: bfloat16 [2048, 16], P('shard'), may hold values from -0.0625 to 0.0625
- w_gate: bfloat16 [16, 2048, 1024], P(('expert', 'shard'), 'dp'), may hold values from -0.125 to 0.125
- w_up: bfloat16 [16, 2048, 1024], P(('expert', 'shard'), 'dp'), may hold values from -0.125 to 0.125
- w_down: bfloat16 [16, 1024, 2048], P(('expert', 'shard'), None, 'dp'), may hold values from -1 to 1
Outputs:
- block_out: bfloat16 [6144, 2048], P(('dp', 'expert', 'shard'))
- grad_in: float32 [6144, 2048], P(('dp', 'expert', 'shard'))
- grad_attn_gain: float32 [2048], P('shard')
- grad_query_gain: float32 [2048], P('shard')
- grad_key_gain: float32 [2048], P('shard')
- grad_mlp_gain: float32 [2048], P('shard')
- grad_query: float32 [2048, 2048], P('shard')
- grad_key: float32 [2048, 2048], P('shard')
- grad_value: float32 [2048, 2048], P('shard')
- grad_output: float32 [2048, 2048], P('shard')
- grad_router: float32 [2048, 16], P('shard')
- grad_gate: float32 [16, 2048, 1024], P(('expert', 'shard'), 'dp')
- grad_up: float32 [16, 2048, 1024], P(('expert', 'shard'), 'dp')
- grad_down: float32 [16, 1024, 2048], P(('expert', 'shard'), None, 'dp')
Inputs may be any that keep to these rules, and one draw needn't show every extreme that they name: `doc_lengths`: each row holds a document, then one of 576 tokens, then another document, then the padding; the lengths of a row sum to 768; the first document has 48 to 96 tokens and the padding 192//16 to 24. `expert_ids`: each token names 8 different experts; among the 192 tokens of one device no expert is named more than 120 times, a bound that some block reaches.
All inputs are finite; a program needn't handle non-finite values.
Results may differ from a plain program's by a relative error of at most 0.024.
Values may be sent and summed in bfloat16 or wider, within the bound.
No kernel may reach another device: no remote copies, remote signals or barrier semaphores. Data moves between devices by JAX's collectives and lax.ppermute only.
A program may use at most 320 MiB of HBM per device.

v0:
```python
import math

import jax
import jax.numpy as jnp
from jax import lax
from jax.sharding import PartitionSpec as P

D = 2048
HEADS = 16
HD = 128
TOP = 8
DOCS = 4


EPSILON = 1e-05
ROPE_BASE = 10000.0
NEG_FILL = -1e30


def rms(values, scale_gain):
    return (
        values * lax.rsqrt(jnp.mean(values * values, axis=-1, keepdims=True) + EPSILON) * scale_gain
    )


def softmax_rows(values):
    row_max = jnp.max(values, axis=-1, keepdims=True)
    exp_terms = jnp.exp(values - row_max)
    return exp_terms / jnp.sum(exp_terms, axis=-1, keepdims=True)


def doc_layout(doc_lengths, total):
    doc_ends = jnp.cumsum(doc_lengths, axis=1)
    doc_starts = doc_ends - doc_lengths
    places = jnp.arange(total, dtype=jnp.int32)
    doc_ids = jnp.sum((places[None, :, None] >= doc_ends[:, None, :]).astype(jnp.int32), axis=2)
    owner = doc_ids[:, :, None] == jnp.arange(DOCS, dtype=jnp.int32)[None, None, :]
    begins = jnp.sum(jnp.where(owner, doc_starts[:, None, :], 0), axis=2)
    return (doc_ids, places[None, :] - begins)


def rope_tables(doc_place):
    half_size = HD // 2
    freqs = jnp.exp(-math.log(ROPE_BASE) * 2.0 * jnp.arange(half_size, dtype=jnp.float32) / HD)
    angles = doc_place.astype(jnp.float32)[..., None] * freqs
    angles = jnp.concatenate([angles, angles], axis=-1)
    return (jnp.cos(angles), jnp.sin(angles))


def rotate(values, cosine, sine_part):
    half_size = HD // 2
    turned = jnp.concatenate([-values[..., half_size:], values[..., :half_size]], axis=-1)
    return values * cosine[..., None, :] + turned * sine_part[..., None, :]


def shards(
    hidden_in,
    grad_out,
    doc_lengths,
    expert_ids,
    attn_gain,
    query_gain,
    key_gain,
    mlp_gain,
    w_query,
    w_key,
    w_value,
    w_output,
    w_router,
    w_gate,
    w_up,
    w_down,
):
    gathered = (
        lax.all_gather(attn_gain, "shard", axis=0, tiled=True),
        lax.all_gather(query_gain, "shard", axis=0, tiled=True),
        lax.all_gather(key_gain, "shard", axis=0, tiled=True),
        lax.all_gather(mlp_gain, "shard", axis=0, tiled=True),
        lax.all_gather(w_query, "shard", axis=0, tiled=True),
        lax.all_gather(w_key, "shard", axis=0, tiled=True),
        lax.all_gather(w_value, "shard", axis=0, tiled=True),
        lax.all_gather(w_output, "shard", axis=0, tiled=True),
        lax.all_gather(w_router, "shard", axis=0, tiled=True),
    )
    gain_attn = gathered[0].astype(jnp.float32)
    gain_query = gathered[1].astype(jnp.float32)
    gain_key = gathered[2].astype(jnp.float32)
    gain_mlp = gathered[3].astype(jnp.float32)
    query_full, key_full, value_full, output_full, router_full = (
        gathered[4],
        gathered[5],
        gathered[6],
        gathered[7],
        gathered[8],
    )
    expert_full = (
        lax.all_gather(w_gate, "dp", axis=1, tiled=True),
        lax.all_gather(w_up, "dp", axis=1, tiled=True),
        lax.all_gather(w_down, "dp", axis=2, tiled=True),
    )
    gate_full = expert_full[0][0]
    up_full = expert_full[1][0]
    down_full = expert_full[2][0]
    length = hidden_in.shape[0]
    members = lax.axis_size("shard")
    seq_len = length * members
    offset = lax.axis_index("shard") * length
    experts = lax.axis_size(("expert", "shard"))
    capacity = 5 * length * TOP // (4 * experts)
    score_scale = HD ** (-0.5)
    inputs = hidden_in.astype(jnp.float32)
    doc_ids, doc_place = doc_layout(doc_lengths, seq_len)
    doc_row = doc_ids[0]
    query_doc = lax.dynamic_slice_in_dim(doc_row, offset, length)
    query_place = lax.dynamic_slice_in_dim(doc_place[0], offset, length)
    cosine, sine_part = rope_tables(query_place)
    query_pos = offset + jnp.arange(length, dtype=jnp.int32)
    key_pos = jnp.arange(seq_len, dtype=jnp.int32)
    allowed = (
        (query_doc[:, None] == doc_row[None, :])
        & (key_pos[None, :] <= query_pos[:, None])
        & ((doc_row[None, :] < DOCS - 1) | (key_pos[None, :] == query_pos[:, None]))
    )[None]
    attn_normed, pull_attn = jax.vjp(rms, inputs, gain_attn)
    attn_input = attn_normed.astype(jnp.bfloat16)
    query_raw = jnp.dot(attn_input, query_full, preferred_element_type=jnp.float32)
    key_raw = jnp.dot(attn_input, key_full, preferred_element_type=jnp.float32)
    value_heads = (
        jnp.dot(attn_input, value_full, preferred_element_type=jnp.float32)
        .astype(jnp.bfloat16)
        .reshape(length, HEADS, HD)
    )

    def turn_heads(raw_rows, scale_gain):
        return rotate(rms(raw_rows, scale_gain).reshape(length, HEADS, HD), cosine, sine_part)

    query_rot, pull_query = jax.vjp(turn_heads, query_raw, gain_query)
    key_rot, pull_key = jax.vjp(turn_heads, key_raw, gain_key)
    query_heads = query_rot.astype(jnp.bfloat16)
    key_heads = key_rot.astype(jnp.bfloat16)
    key_all, value_all = (
        lax.all_gather(key_heads, "shard", axis=0, tiled=True),
        lax.all_gather(value_heads, "shard", axis=0, tiled=True),
    )

    def masked_scores():
        raw_scores = (
            jnp.einsum("qhd,khd->hqk", query_heads, key_all, preferred_element_type=jnp.float32)
            * score_scale
        )
        return jnp.where(allowed, raw_scores, NEG_FILL)

    scores = masked_scores()
    row_max = jnp.max(scores, axis=-1, keepdims=True)
    exp_terms = jnp.exp(scores - row_max)
    row_total = jnp.sum(exp_terms, axis=-1, keepdims=True)
    log_total = row_max + jnp.log(row_total)
    attn_probs = (exp_terms / row_total).astype(jnp.bfloat16)
    mixed = jnp.einsum("hqk,khd->qhd", attn_probs, value_all, preferred_element_type=jnp.float32)
    mixed_rows = mixed.reshape(length, HEADS * HD).astype(jnp.bfloat16)
    residual = inputs + jnp.dot(mixed_rows, output_full, preferred_element_type=jnp.float32)
    mlp_normed, pull_mlp = jax.vjp(rms, residual, gain_mlp)
    mlp_input = mlp_normed.astype(jnp.bfloat16)
    logits = jnp.dot(mlp_input, router_full, preferred_element_type=jnp.float32)
    route_probs = softmax_rows(logits)
    choose = (expert_ids[:, :, None] == jnp.arange(experts, dtype=jnp.int32)[None, None, :]).astype(
        jnp.float32
    )
    gates = jnp.einsum("tke,te->tk", choose, route_probs, preferred_element_type=jnp.float32)
    flat_ids = expert_ids.reshape(-1)
    expert_hits = (flat_ids[:, None] == jnp.arange(experts, dtype=jnp.int32)[None, :]).astype(
        jnp.int32
    )
    slot_place = jnp.sum(expert_hits * jnp.cumsum(expert_hits, axis=0), axis=1) - 1
    slot_index = flat_ids * capacity + slot_place
    spread = jnp.repeat(mlp_input, TOP, axis=0)
    send_buffer = (
        jnp.zeros((experts * capacity, D), jnp.bfloat16)
        .at[slot_index]
        .set(spread)
        .reshape(experts, capacity, D)
    )
    slot_rows = lax.all_to_all(
        send_buffer, ("expert", "shard"), split_axis=0, concat_axis=0, tiled=True
    )
    gate_pre = jnp.einsum("scd,df->scf", slot_rows, gate_full, preferred_element_type=jnp.float32)
    up_pre = jnp.einsum("scd,df->scf", slot_rows, up_full, preferred_element_type=jnp.float32)
    hidden_mid = (gate_pre * jax.nn.sigmoid(gate_pre) * up_pre).astype(jnp.bfloat16)
    result = jnp.einsum(
        "scf,fd->scd", hidden_mid, down_full, preferred_element_type=jnp.float32
    ).astype(jnp.bfloat16)
    returned_rows = lax.all_to_all(
        result, ("expert", "shard"), split_axis=0, concat_axis=0, tiled=True
    )
    picked = returned_rows.reshape(experts * capacity, D)[slot_index].reshape(length, TOP, D)
    expert_sum = jnp.sum(gates[:, :, None] * picked, axis=1)
    block_out = (residual + expert_sum).astype(jnp.bfloat16)
    upstream = grad_out.astype(jnp.float32)
    gate_grads = jnp.sum(upstream[:, None, :] * picked, axis=2)
    weighted_grads = (
        (gates[:, :, None] * upstream[:, None, :]).astype(jnp.bfloat16).reshape(length * TOP, D)
    )
    grad_buffer = (
        jnp.zeros((experts * capacity, D), jnp.bfloat16)
        .at[slot_index]
        .set(weighted_grads)
        .reshape(experts, capacity, D)
    )
    grad_slots, slot_rows = (
        lax.all_to_all(grad_buffer, ("expert", "shard"), split_axis=0, concat_axis=0, tiled=True),
        lax.all_to_all(send_buffer, ("expert", "shard"), split_axis=0, concat_axis=0, tiled=True),
    )
    gate_pre = jnp.einsum("scd,df->scf", slot_rows, gate_full, preferred_element_type=jnp.float32)
    up_pre = jnp.einsum("scd,df->scf", slot_rows, up_full, preferred_element_type=jnp.float32)
    sigmoid_gate = jax.nn.sigmoid(gate_pre)
    silu_gate = gate_pre * sigmoid_gate
    hidden_mid = (silu_gate * up_pre).astype(jnp.bfloat16)
    grad_hidden = jnp.einsum(
        "scd,fd->scf", grad_slots, down_full, preferred_element_type=jnp.float32
    )
    grad_down_full = jnp.einsum(
        "scf,scd->fd", hidden_mid, grad_slots, preferred_element_type=jnp.float32
    )
    grad_gate_pre = (
        grad_hidden * up_pre * sigmoid_gate * (1.0 + gate_pre * (1.0 - sigmoid_gate))
    ).astype(jnp.bfloat16)
    grad_up_pre = (grad_hidden * silu_gate).astype(jnp.bfloat16)
    grad_gate_full = jnp.einsum(
        "scd,scf->df", slot_rows, grad_gate_pre, preferred_element_type=jnp.float32
    )
    grad_up_full = jnp.einsum(
        "scd,scf->df", slot_rows, grad_up_pre, preferred_element_type=jnp.float32
    )
    grad_rows = (
        jnp.einsum("scf,df->scd", grad_gate_pre, gate_full, preferred_element_type=jnp.float32)
        + jnp.einsum("scf,df->scd", grad_up_pre, up_full, preferred_element_type=jnp.float32)
    ).astype(jnp.bfloat16)
    returned_grads = lax.all_to_all(
        grad_rows, ("expert", "shard"), split_axis=0, concat_axis=0, tiled=True
    )
    grad_mlp_in = jnp.sum(
        returned_grads.reshape(experts * capacity, D)[slot_index].reshape(length, TOP, D),
        axis=1,
        dtype=jnp.float32,
    )
    grad_probs = jnp.einsum("tke,tk->te", choose, gate_grads, preferred_element_type=jnp.float32)
    grad_logits = (
        route_probs * (grad_probs - jnp.sum(route_probs * grad_probs, axis=-1, keepdims=True))
    ).astype(jnp.bfloat16)
    grad_mlp_in = grad_mlp_in + jnp.einsum(
        "te,de->td", grad_logits, router_full, preferred_element_type=jnp.float32
    )
    grad_mlp_norm, grad_gain_mlp = pull_mlp(grad_mlp_in)
    grad_residual = upstream + grad_mlp_norm
    grad_attn_out = grad_residual.astype(jnp.bfloat16)
    grad_mixed = (
        jnp.einsum("te,de->td", grad_attn_out, output_full, preferred_element_type=jnp.float32)
        .astype(jnp.bfloat16)
        .reshape(length, HEADS, HD)
    )
    again_probs = jnp.exp(masked_scores() - log_total)
    grad_value_part = jnp.einsum(
        "hqk,qhd->khd",
        again_probs.astype(jnp.bfloat16),
        grad_mixed,
        preferred_element_type=jnp.float32,
    )
    grad_attn_probs = jnp.einsum(
        "qhd,khd->hqk", grad_mixed, value_all, preferred_element_type=jnp.float32
    )
    row_delta = jnp.sum(again_probs * grad_attn_probs, axis=-1, keepdims=True)
    grad_scores = (again_probs * (grad_attn_probs - row_delta)).astype(jnp.bfloat16)
    grad_query_rot = (
        jnp.einsum("hqk,khd->qhd", grad_scores, key_all, preferred_element_type=jnp.float32)
        * score_scale
    )
    grad_key_part = (
        jnp.einsum("hqk,qhd->khd", grad_scores, query_heads, preferred_element_type=jnp.float32)
        * score_scale
    )
    key_value_sums = (
        lax.psum_scatter(
            grad_key_part.astype(jnp.bfloat16), "shard", scatter_dimension=0, tiled=True
        ).astype(jnp.float32),
        lax.psum_scatter(
            grad_value_part.astype(jnp.bfloat16), "shard", scatter_dimension=0, tiled=True
        ).astype(jnp.float32),
    )
    grad_key_rot = key_value_sums[0]
    grad_value_heads = key_value_sums[1].astype(jnp.bfloat16)
    grad_query_raw, grad_gain_query = pull_query(grad_query_rot)
    grad_key_raw, grad_gain_key = pull_key(grad_key_rot)
    grad_query_low = grad_query_raw.astype(jnp.bfloat16)
    grad_key_low = grad_key_raw.astype(jnp.bfloat16)
    grad_value_low = grad_value_heads.reshape(length, HEADS * HD)
    grad_attn_in = (
        jnp.einsum("te,de->td", grad_query_low, query_full, preferred_element_type=jnp.float32)
        + jnp.einsum("te,de->td", grad_key_low, key_full, preferred_element_type=jnp.float32)
        + jnp.einsum("te,de->td", grad_value_low, value_full, preferred_element_type=jnp.float32)
    )
    grad_attn_norm, grad_gain_attn = pull_attn(grad_attn_in)
    grad_in = grad_residual + grad_attn_norm
    grad_query_full = jnp.einsum(
        "td,te->de", attn_input, grad_query_low, preferred_element_type=jnp.float32
    )
    grad_key_full = jnp.einsum(
        "td,te->de", attn_input, grad_key_low, preferred_element_type=jnp.float32
    )
    grad_value_full = jnp.einsum(
        "td,te->de", attn_input, grad_value_low, preferred_element_type=jnp.float32
    )
    grad_output_full = jnp.einsum(
        "td,te->de", mixed_rows, grad_attn_out, preferred_element_type=jnp.float32
    )
    grad_router_full = jnp.einsum(
        "td,te->de", mlp_input, grad_logits, preferred_element_type=jnp.float32
    )
    local_sums = (
        lax.psum_scatter(
            grad_gain_attn.astype(jnp.bfloat16), "shard", scatter_dimension=0, tiled=True
        ).astype(jnp.float32),
        lax.psum_scatter(
            grad_gain_query.astype(jnp.bfloat16), "shard", scatter_dimension=0, tiled=True
        ).astype(jnp.float32),
        lax.psum_scatter(
            grad_gain_key.astype(jnp.bfloat16), "shard", scatter_dimension=0, tiled=True
        ).astype(jnp.float32),
        lax.psum_scatter(
            grad_gain_mlp.astype(jnp.bfloat16), "shard", scatter_dimension=0, tiled=True
        ).astype(jnp.float32),
        lax.psum_scatter(
            grad_query_full.astype(jnp.bfloat16), "shard", scatter_dimension=0, tiled=True
        ).astype(jnp.float32),
        lax.psum_scatter(
            grad_key_full.astype(jnp.bfloat16), "shard", scatter_dimension=0, tiled=True
        ).astype(jnp.float32),
        lax.psum_scatter(
            grad_value_full.astype(jnp.bfloat16), "shard", scatter_dimension=0, tiled=True
        ).astype(jnp.float32),
        lax.psum_scatter(
            grad_output_full.astype(jnp.bfloat16), "shard", scatter_dimension=0, tiled=True
        ).astype(jnp.float32),
        lax.psum_scatter(
            grad_router_full.astype(jnp.bfloat16), "shard", scatter_dimension=0, tiled=True
        ).astype(jnp.float32),
    )
    mixer_sums = (
        lax.psum(local_sums[0].astype(jnp.bfloat16), ("dp", "expert")).astype(jnp.float32),
        lax.psum(local_sums[1].astype(jnp.bfloat16), ("dp", "expert")).astype(jnp.float32),
        lax.psum(local_sums[2].astype(jnp.bfloat16), ("dp", "expert")).astype(jnp.float32),
        lax.psum(local_sums[3].astype(jnp.bfloat16), ("dp", "expert")).astype(jnp.float32),
        lax.psum(local_sums[4].astype(jnp.bfloat16), ("dp", "expert")).astype(jnp.float32),
        lax.psum(local_sums[5].astype(jnp.bfloat16), ("dp", "expert")).astype(jnp.float32),
        lax.psum(local_sums[6].astype(jnp.bfloat16), ("dp", "expert")).astype(jnp.float32),
        lax.psum(local_sums[7].astype(jnp.bfloat16), ("dp", "expert")).astype(jnp.float32),
        lax.psum(local_sums[8].astype(jnp.bfloat16), ("dp", "expert")).astype(jnp.float32),
    )
    expert_sums = (
        lax.psum_scatter(
            grad_gate_full[None].astype(jnp.bfloat16), "dp", scatter_dimension=1, tiled=True
        ).astype(jnp.float32),
        lax.psum_scatter(
            grad_up_full[None].astype(jnp.bfloat16), "dp", scatter_dimension=1, tiled=True
        ).astype(jnp.float32),
        lax.psum_scatter(
            grad_down_full[None].astype(jnp.bfloat16), "dp", scatter_dimension=2, tiled=True
        ).astype(jnp.float32),
    )
    return (
        block_out,
        grad_in,
        mixer_sums[0],
        mixer_sums[1],
        mixer_sums[2],
        mixer_sums[3],
        mixer_sums[4],
        mixer_sums[5],
        mixer_sums[6],
        mixer_sums[7],
        mixer_sums[8],
        expert_sums[0],
        expert_sums[1],
        expert_sums[2],
    )


def solution(mesh):
    return jax.shard_map(
        shards,
        mesh=mesh,
        in_specs=(
            P(("dp", "expert", "shard"), None),
            P(("dp", "expert", "shard"), None),
            P(("dp", "expert"), None),
            P(("dp", "expert", "shard"), None),
            P("shard"),
            P("shard"),
            P("shard"),
            P("shard"),
            P("shard", None),
            P("shard", None),
            P("shard", None),
            P("shard", None),
            P("shard", None),
            P(("expert", "shard"), "dp", None),
            P(("expert", "shard"), "dp", None),
            P(("expert", "shard"), None, "dp"),
        ),
        out_specs=(
            P(("dp", "expert", "shard"), None),
            P(("dp", "expert", "shard"), None),
            P("shard"),
            P("shard"),
            P("shard"),
            P("shard"),
            P("shard", None),
            P("shard", None),
            P("shard", None),
            P("shard", None),
            P("shard", None),
            P(("expert", "shard"), "dp", None),
            P(("expert", "shard"), "dp", None),
            P(("expert", "shard"), None, "dp"),
        ),
        check_vma=False,
    )
```

profile of v0, /device:TPU:9, one launch (start us, length us, event | category | flops | bytes accessed | tf_op | source)
XLA Modules:
  0.0 1926.0 jit_solution(7718172443508998707)
XLA Ops:
  30.2 69.4 %all-gather.18.cloned.1.call-done = bf16[2048,2048]{1,0:T(8,128)(2,1)} async-done(((bf16[512,2048]{1,0:T(8,128)(2,1)}), bf16[2048,2048]{1,0:T(8,128)(2,1)}) %all-gather.18.cloned.1.call-update) | async-done | bytes 8388624 | tf_op jit(solution)/shard_map/all_gather | solution.py:79
  105.0 84.1 %all-gather.20.cloned.1.call-done = bf16[2048,2048]{1,0:T(8,128)(2,1)} async-done(((bf16[512,2048]{1,0:T(8,128)(2,1)}), bf16[2048,2048]{1,0:T(8,128)(2,1)}) %all-gather.20.cloned.1.call-update) | async-done | bytes 8388624 | tf_op jit(solution)/shard_map/all_gather | solution.py:80
  198.3 80.3 %all-gather.14.cloned.1.call-done = bf16[2048,2048]{1,0:T(8,128)(2,1)} async-done(((bf16[512,2048]{1,0:T(8,128)(2,1)}), bf16[2048,2048]{1,0:T(8,128)(2,1)}) %all-gather.14.cloned.1.call-update) | async-done | bytes 8388624 | tf_op jit(solution)/shard_map/all_gather | solution.py:81
  298.8 26.1 %all-gather.22.cloned.1.call-done = bf16[768,16,128]{2,0,1:T(8,128)(2,1)} async-done(((bf16[192,16,128]{2,0,1:T(8,128)(2,1)}), bf16[768,16,128]{2,0,1:T(8,128)(2,1)}) %all-gather.22.cloned.1.call-update) | async-done | bytes 3145744 | tf_op jit(solution)/shard_map/all_gather | solution.py:142
  334.8 36.4 %all-gather.16.cloned.1.call-done = bf16[768,16,128]{2,0,1:T(8,128)(2,1)} async-done(((bf16[192,16,128]{2,0,1:T(8,128)(2,1)}), bf16[768,16,128]{2,0,1:T(8,128)(2,1)}) %all-gather.16.cloned.1.call-update) | async-done | bytes 3145744 | tf_op jit(solution)/shard_map/all_gather | solution.py:143
  377.9 82.6 %all-gather.24.cloned.1.call-done = bf16[2048,2048]{1,0:T(8,128)(2,1)} async-done(((bf16[512,2048]{1,0:T(8,128)(2,1)}), bf16[2048,2048]{1,0:T(8,128)(2,1)}) %all-gather.24.cloned.1.call-update) | async-done | bytes 8388624 | tf_op jit(solution)/shard_map/all_gather | solution.py:82
  467.2 14.0 scatter_custom_fusion
  487.1 35.1 %all_gather.52 = bf16[2048,16]{0,1:T(8,128)(2,1)S(1)} all-gather(bf16[512,16]{0,1:T(8,128)(2,1)S(1)} %copy-done.71), channel_id=1, replica_groups=mesh['dp'=2,'expert'=4,'shard'=4] {'shard'}, dimensions={0}, use_global_device_ids=true | all-gather | bytes 81920 | tf_op jit(solution)/shard_map/all_gather | solution.py:83
  523.8 14.5 scatter_custom_fusion.1
  538.4 117.4 %all-to-all-done = bf16[16,120,2048]{2,1,0:T(8,128)(2,1)} async-done(((bf16[16,120,2048]{2,1,0:T(8,128)(2,1)}), bf16[16,120,2048]{2,1,0:T(8,128)(2,1)}, u32[]{:S(2)}, u32[]{:S(2)}) %all-to-all-start) | async-done | bytes 7864352 | tf_op jit(solution)/shard_map/all_to_all | solution.py:183
  655.8 14.1 all-to-all-start.2
  671.6 17.2 all-gather.28.cloned.1.call-done
  688.8 13.8 fusion.20
  705.0 13.8 fusion.24
  721.2 116.3 %all-to-all-done.2 = bf16[16,120,2048]{2,1,0:T(8,128)(2,1)} async-done(((bf16[16,120,2048]{2,1,0:T(8,128)(2,1)}), bf16[16,120,2048]{2,1,0:T(8,128)(2,1)}, u32[]{:S(2)}, u32[]{:S(2)}) %all-to-all-start.2) | async-done | bytes 7864352 | tf_op jit(solution)/shard_map/all_to_all | solution.py:210
  837.5 22.0 %multiply_convert_fusion.1 = (bf16[16,120,1024]{2,1,0:T(8,128)(2,1)}, bf16[16,120,1024]{2,1,0:T(8,128)(2,1)}, bf16[16,120,1024]{2,1,0:T(8,128)(2,1)}) fusion(f32[16,120,1024]{2,1,0:T(8,128)} %fusion.24, f32[16,120,1024]{2,1,0:T(8,128)} %fusion.20, bf16[16,120,2048]{2,1,0:T(8,128)(2,1)} %all-to-all-done.2, ...), kind=kOutput, calls=%fused_computation.22 | convolution fusion | flops 8082554880 | bytes 39583744 | tf_op jit(solution)/shard_map/scd,fd->scf/dot_general | solution.py:218
  884.8 14.7 fusion.22
  912.9 138.3 %all-to-all-done.1 = bf16[16,120,2048]{2,1,0:T(8,128)(2,1)} async-done(((bf16[16,120,2048]{2,1,0:T(8,128)(2,1)}), bf16[16,120,2048]{2,1,0:T(8,128)(2,1)}, u32[]{:S(2)}, u32[]{:S(2)}) %all-to-all-start.1) | async-done | bytes 7864352 | tf_op jit(solution)/shard_map/all_to_all | solution.py:192
  1062.4 17.1 gather_fusion
  1086.6 143.3 %all-to-all-done.3 = bf16[16,120,2048]{2,1,0:T(8,128)(2,1)} async-done(((bf16[16,120,2048]{2,1,0:T(8,128)(2,1)}), bf16[16,120,2048]{2,1,0:T(8,128)(2,1)}, u32[]{:S(2)}, u32[]{:S(2)}) %all-to-all-start.3) | async-done | bytes 7864352 | tf_op jit(solution)/shard_map/all_to_all | solution.py:238
  1229.9 17.2 gather_fusion.1
  1295.8 27.5 %reduce-scatter.13.cloned.1.call-done = bf16[192,16,128]{2,1,0:T(8,128)(2,1)} async-done(((bf16[768,16,128]{2,1,0:T(8,128)(2,1)}), bf16[192,16,128]{2,1,0:T(8,128)(2,1)}) %reduce-scatter.13.cloned.1.call-update) | async-done | bytes 786448 | tf_op jit(solution)/shard_map/reduce_scatter | solution.py:285
  1338.9 32.0 %reduce-scatter.11.cloned.1.call-done = bf16[192,16,128]{2,0,1:T(8,128)(2,1)} async-done(((bf16[768,16,128]{2,0,1:T(8,128)(2,1)}), bf16[192,16,128]{2,0,1:T(8,128)(2,1)}) %reduce-scatter.11.cloned.1.call-update) | async-done | bytes 786448 | tf_op jit(solution)/shard_map/reduce_scatter | solution.py:282
  1394.0 14.1 fusion.31
  1408.2 14.1 fusion.30
  1422.3 13.9 fusion.29
  1438.5 21.8 %reduce-scatter.21.cloned.1.call-done = bf16[512,2048]{1,0:T(8,128)(2,1)} async-done(((bf16[2048,2048]{1,0:T(8,128)(2,1)}), bf16[512,2048]{1,0:T(8,128)(2,1)}) %reduce-scatter.21.cloned.1.call-update) | async-done | bytes 2097168 | tf_op jit(solution)/shard_map/reduce_scatter | solution.py:340
  1460.3 89.6 %reduce-scatter.19.cloned.1.call-done = bf16[512,2048]{1,0:T(8,128)(2,1)} async-done(((bf16[2048,2048]{1,0:T(8,128)(2,1)}), bf16[512,2048]{1,0:T(8,128)(2,1)}) %reduce-scatter.19.cloned.1.call-update) | async-done | bytes 2097168 | tf_op jit(solution)/shard_map/reduce_scatter | solution.py:337
  1549.9 89.5 %reduce-scatter.17.cloned.1.call-done = bf16[512,2048]{1,0:T(8,128)(2,1)} async-done(((bf16[2048,2048]{1,0:T(8,128)(2,1)}), bf16[512,2048]{1,0:T(8,128)(2,1)}) %reduce-scatter.17.cloned.1.call-update) | async-done | bytes 2097168 | tf_op jit(solution)/shard_map/reduce_scatter | solution.py:334
  1639.4 89.6 %reduce-scatter.15.cloned.1.call-done = bf16[512,2048]{1,0:T(8,128)(2,1)} async-done(((bf16[2048,2048]{1,0:T(8,128)(2,1)}), bf16[512,2048]{1,0:T(8,128)(2,1)}) %reduce-scatter.15.cloned.1.call-update) | async-done | bytes 2097168 | tf_op jit(solution)/shard_map/reduce_scatter | solution.py:331
  1807.6 31.0 %all-reduce.8 = (bf16[512]{0:T(512)(128)(2,1)S(1)}, bf16[512]{0:T(512)(128)(2,1)S(1)}, bf16[512]{0:T(512)(128)(2,1)S(1)}, bf16[512]{0:T(512)(128)(2,1)S(1)}, bf16[512,16]{0,1:T(8,128)(2,1)S(1)}) all-reduce(bf16[512]{0:T(512)(128)(2,1)S(1)} %dynamic-slice.7, ...), channel_id=1, replica_groups=mesh['dp'=2,'expert'=4,'shard'=4] {'dp','expert'}, use_global_device_ids=true, to_apply=%region_29.30 | all-reduce | flops 10240 | bytes 40960 | tf_op jit(solution)/shard_map/psum | solution.py:348
  1844.6 61.7 %all-reduce.13.cloned.1.call-done = (bf16[512,2048]{1,0:T(8,128)(2,1)}, bf16[512,2048]{1,0:T(8,128)(2,1)}, bf16[512,2048]{1,0:T(8,128)(2,1)}, bf16[512,2048]{1,0:T(8,128)(2,1)}) async-done(((bf16[512,2048]{1,0:T(8,128)(2,1)}, bf16[512,2048]{1,0:T(8,128)(2,1)}, bf16[512,2048]{1,0:T(8,128)(2,1)}, bf16[512,2048]{1,0:T(8,128)(2,1)}), (bf16[512,2048]{1,0:T(8,128)(2,1)}, bf16[512,2048]{1,0:T(8,128)(2,1)}, ...) | async-done | bytes 8388624 | tf_op jit(solution)/shard_map/psum | solution.py:352
  (374 shorter events, 335.3 us)
Async XLA Ops:
  8.0 91.6 %all-gather.18.cloned.1.call-start = ((), (), s32[]{:S(2)}) async-start(), calls=%async_computation.16 | async-start | bytes 10485760 | tf_op jit(solution)/shard_map/all_gather | solution.py:79
  8.7 180.3 %all-gather.20.cloned.1.call-start = ((), (), s32[]{:S(2)}) async-start(), calls=%async_computation.17 | async-start | bytes 10485760 | tf_op jit(solution)/shard_map/all_gather | solution.py:80
  9.5 269.1 %all-gather.14.cloned.1.call-start = ((), (), s32[]{:S(2)}) async-start(), calls=%async_computation.14 | async-start | bytes 10485760 | tf_op jit(solution)/shard_map/all_gather | solution.py:81
  10.2 314.7 %all-gather.22.cloned.1.call-start = ((), (), s32[]{:S(2)}) async-start(), calls=%async_computation.18 | async-start | bytes 3932160 | tf_op jit(solution)/shard_map/all_gather | solution.py:142
  16.8 179.4 %copy-start.52 = (f32[4,1,512]{2,1,0:T(1,128)}, f32[4,1,512]{2,1,0:T(1,128)S(1)}, u32[]{:S(2)}) copy-start(f32[4,1,512]{2,1,0:T(1,128)S(1)} %convert_element_type.322) | copy-start | bytes 24580
  22.8 173.3 %copy-start.50 = (f32[4,1,512]{2,1,0:T(1,128)}, f32[4,1,512]{2,1,0:T(1,128)S(1)}, u32[]{:S(2)}) copy-start(f32[4,1,512]{2,1,0:T(1,128)S(1)} %convert_element_type.321) | copy-start | bytes 24580
  28.6 250.0 %copy-start.33 = (f32[4,1,512]{2,1,0:T(1,128)}, f32[4,1,512]{2,1,0:T(1,128)S(1)}, u32[]{:S(2)}) copy-start(f32[4,1,512]{2,1,0:T(1,128)S(1)} %convert_element_type.320) | copy-start | bytes 24580
  30.0 166.2 %copy-start.35 = (f32[192,128]{1,0:T(8,128)}, f32[192,128]{1,0:T(8,128)S(1)}, u32[]{:S(2)}) copy-start(f32[192,128]{1,0:T(8,128)S(1)} %get-tuple-element.55) | copy-start | bytes 294916
  30.0 166.2 %copy-start.37 = (f32[192,128]{1,0:T(8,128)}, f32[192,128]{1,0:T(8,128)S(1)}, u32[]{:S(2)}) copy-start(f32[192,128]{1,0:T(8,128)S(1)} %get-tuple-element.54) | copy-start | bytes 294916
  30.2 248.4 %copy-start.58 = (f32[192]{0:T(256)}, f32[192]{0:T(256)S(1)}, u32[]{:S(2)}) copy-start(f32[192]{0:T(256)S(1)} %fusion.96) | copy-start | bytes 2308
  198.3 172.9 %all-gather.16.cloned.1.call-start = ((), (), s32[]{:S(2)}) async-start(), calls=%async_computation.15 | async-start | bytes 3932160 | tf_op jit(solution)/shard_map/all_gather | solution.py:143
  284.9 175.6 %all-gather.24.cloned.1.call-start = ((), (), s32[]{:S(2)}) async-start(), calls=%async_computation.19 | async-start | bytes 10485760 | tf_op jit(solution)/shard_map/all_gather | solution.py:82
  285.7 237.5 %copy-start.39 = (s32[192,8]{1,0:T(8,128)}, s32[192,8]{1,0:T(8,128)S(1)}, u32[]{:S(2)}) copy-start(s32[192,8]{1,0:T(8,128)S(1)} %copy.86) | copy-start | bytes 18436
  292.8 173.1 %copy-start.56 = (f32[4,1,512]{2,1,0:T(1,128)}, f32[4,1,512]{2,1,0:T(1,128)S(1)}, u32[]{:S(2)}) copy-start(f32[4,1,512]{2,1,0:T(1,128)S(1)} %convert_element_type.323) | copy-start | bytes 24580
  481.2 174.6 %all-to-all-start = ((bf16[16,120,2048]{2,1,0:T(8,128)(2,1)}), bf16[16,120,2048]{2,1,0:T(8,128)(2,1)}, u32[]{:S(2)}, u32[]{:S(2)}) async-start(bf16[16,120,2048]{2,1,0:T(8,128)(2,1)} %bitcast.224), calls=%async_computation | async-start | bytes 15728640 | tf_op jit(solution)/shard_map/all_to_all | solution.py:183
  655.8 181.8 %all-to-all-start.2 = ((bf16[16,120,2048]{2,1,0:T(8,128)(2,1)}), bf16[16,120,2048]{2,1,0:T(8,128)(2,1)}, u32[]{:S(2)}, u32[]{:S(2)}) async-start(bf16[16,120,2048]{2,1,0:T(8,128)(2,1)} %bitcast.223), calls=%async_computation.2 | async-start | bytes 15728640 | tf_op jit(solution)/shard_map/all_to_all | solution.py:210
  669.9 18.9 all-gather.28.cloned.1.call-start
  670.4 34.6 %all-gather.26.cloned.1.call-start = ((), (), s32[]{:S(2)}) async-start(), calls=%async_computation.20 | async-start | bytes 6291456 | tf_op jit(solution)/shard_map/all_gather | solution.py:97
  671.0 50.2 %all-gather.30.cloned.1.call-start = ((), (), s32[]{:S(2)}) async-start(), calls=%async_computation.22 | async-start | bytes 6291456 | tf_op jit(solution)/shard_map/all_gather | solution.py:99
  873.3 177.9 %all-to-all-start.1 = ((bf16[16,120,2048]{2,1,0:T(8,128)(2,1)}), bf16[16,120,2048]{2,1,0:T(8,128)(2,1)}, u32[]{:S(2)}, u32[]{:S(2)}) async-start(bf16[16,120,2048]{2,1,0:T(8,128)(2,1)} %convolution_convert_fusion.4), calls=%async_computation.1 | async-start | bytes 15728640 | tf_op jit(solution)/shard_map/all_to_all | solution.py:192
  1051.2 178.7 %all-to-all-start.3 = ((bf16[16,120,2048]{2,1,0:T(8,128)(2,1)}), bf16[16,120,2048]{2,1,0:T(8,128)(2,1)}, u32[]{:S(2)}, u32[]{:S(2)}) async-start(bf16[16,120,2048]{2,1,0:T(8,128)(2,1)} %add_convert_fusion), calls=%async_computation.3 | async-start | bytes 15728640 | tf_op jit(solution)/shard_map/all_to_all | solution.py:238
  1062.1 261.2 %reduce-scatter.13.cloned.1.call-start = ((), (), s32[]{:S(2)}) async-start(), calls=%async_computation.24 | async-start | bytes 3932160 | tf_op jit(solution)/shard_map/reduce_scatter | solution.py:285
  1270.3 100.6 %reduce-scatter.11.cloned.1.call-start = ((), (), s32[]{:S(2)}) async-start(), calls=%async_computation.23 | async-start | bytes 3932160 | tf_op jit(solution)/shard_map/reduce_scatter | solution.py:282
  1288.9 171.4 %reduce-scatter.21.cloned.1.call-start = ((), (), s32[]{:S(2)}) async-start(), calls=%async_computation.28 | async-start | bytes 10485760 | tf_op jit(solution)/shard_map/reduce_scatter | solution.py:340
  1295.8 254.2 %reduce-scatter.19.cloned.1.call-start = ((), (), s32[]{:S(2)}) async-start(), calls=%async_computation.27 | async-start | bytes 10485760 | tf_op jit(solution)/shard_map/reduce_scatter | solution.py:337
  1330.3 309.2 %reduce-scatter.17.cloned.1.call-start = ((), (), s32[]{:S(2)}) async-start(), calls=%async_computation.26 | async-start | bytes 10485760 | tf_op jit(solution)/shard_map/reduce_scatter | solution.py:334
  1383.5 345.6 %reduce-scatter.15.cloned.1.call-start = ((), (), s32[]{:S(2)}) async-start(), calls=%async_computation.25 | async-start | bytes 10485760 | tf_op jit(solution)/shard_map/reduce_scatter | solution.py:331
  1393.7 351.1 %reduce-scatter.29.cloned.1.call-start = ((), (), s32[]{:S(2)}) async-start(), calls=%async_computation.32 | async-start | bytes 6291456 | tf_op jit(solution)/shard_map/reduce_scatter | solution.py:365
  1408.1 352.9 %reduce-scatter.27.cloned.1.call-start = ((), (), s32[]{:S(2)}) async-start(), calls=%async_computation.31 | async-start | bytes 6291456 | tf_op jit(solution)/shard_map/reduce_scatter | solution.py:362
  1422.3 354.8 %reduce-scatter.25.cloned.1.call-start = ((), (), s32[]{:S(2)}) async-start(), calls=%async_computation.30 | async-start | bytes 6291456 | tf_op jit(solution)/shard_map/reduce_scatter | solution.py:359
  1436.3 371.4 %reduce-scatter.23.cloned.1.call-start = ((), (), s32[]{:S(2)}) async-start(), calls=%async_computation.29 | async-start | bytes 81920 | tf_op jit(solution)/shard_map/reduce_scatter | solution.py:343
  1438.2 468.0 %all-reduce.13.cloned.1.call-start = ((), (), s32[]{:S(2)}) async-start(), calls=%async_computation.33 | async-start | bytes 16777216 | tf_op jit(solution)/shard_map/psum | solution.py:352
  (91 other events, 1757.1 us)
Sparse Core Ops, SparseCore 0:
  10.7 88.8 all-gather.17
  101.4 87.5 all-gather.19
  190.9 87.5 all-gather.13
  280.8 44.0 all-gather.21
  327.2 43.9 all-gather.15
  372.9 87.5 all-gather.23
  1270.4 52.8 reduce-scatter.12
  1326.9 43.9 reduce-scatter.10
  1373.9 86.3 reduce-scatter.20
  1463.5 86.3 reduce-scatter.18
  1553.0 86.3 reduce-scatter.16
  1642.7 86.3 reduce-scatter.14
  1731.9 12.7 reduce-scatter.28
  1747.6 13.3 reduce-scatter.26
  1763.7 13.3 reduce-scatter.24
  1780.4 24.1 reduce-scatter.22
Sparse Core Ops, SparseCore 1:
  671.9 16.9 all-gather.27
  690.2 14.7 all-gather.25
  706.4 14.7 all-gather.29
  1729.2 177.0 all-reduce.12
where the time goes:
time: 1940 us; the launch traced here: 1930 us
  waiting for transfers between devices  1370 us (71%)
  matrix products  230 us (12%)
  blocking collectives  103 us (5%)
  other arithmetic  88.9 us (5%)
  local copies, waits for them, and re-layouts  72.5 us (4%)
  starting transfers between devices  43.9 us (2%)
    all_to_all x1, waiting for transfers between devices, shards(): lax.all_to_all(grad_rows, ('expert', 'shard'), split_axis=0, concat_axis=...  143 us
    all_to_all x1, waiting for transfers between devices, shards(): lax.all_to_all(result, ('expert', 'shard'), split_axis=0, concat_axis=0,...  138 us
    all_to_all x1, waiting for transfers between devices, shards(): lax.all_to_all(send_buffer, ('expert', 'shard'), split_axis=0, concat_axi...  117 us
    all_to_all x1, waiting for transfers between devices, shards(): lax.all_to_all(grad_buffer, ('expert', 'shard'), split_axis=0, concat_axi...  116 us
    reduce_scatter x1, waiting for transfers between devices, shards(): lax.psum_scatter(grad_query_full.astype(jnp.bfloat16), 'shard', scatter_d...  89.6 us
    reduce_scatter x1, waiting for transfers between devices, shards(): lax.psum_scatter(grad_value_full.astype(jnp.bfloat16), 'shard', scatter_d...  89.6 us
    reduce_scatter x1, waiting for transfers between devices, shards(): lax.psum_scatter(grad_key_full.astype(jnp.bfloat16), 'shard', scatter_dim...  89.5 us
    all_gather x1, waiting for transfers between devices, shards(): lax.all_gather(w_key, 'shard', axis=0, tiled=True)  84.1 us
  transfers between devices with their start and end apart: 24, of which 23 were waited for; matrix products, arithmetic and copies ran while one was open for 14% of the time, Pallas kernels for 0%

commit v1 on v0

v1 whole, which is shorter than its diff:
```python
import math

import jax
import jax.numpy as jnp
from jax import lax
from jax.sharding import PartitionSpec as P

D = 2048
HEADS = 16
HD = 128
TOP = 8
DOCS = 4

EPSILON = 1e-05
ROPE_BASE = 10000.0
NEG_FILL = -1e30

F32 = jnp.float32
BF16 = jnp.bfloat16


def dot(a, b):
    return jnp.dot(a, b, preferred_element_type=F32)


def dot_nt(a, b):
    return lax.dot_general(a, b, (((1,), (1,)), ((), ())), preferred_element_type=F32)


def dot_tn(a, b):
    return lax.dot_general(a, b, (((0,), (0,)), ((), ())), preferred_element_type=F32)


def at(stack, index):
    return lax.dynamic_index_in_dim(stack, index, 0, keepdims=False)


def doc_layout(lengths, total):
    doc_ends = jnp.cumsum(lengths)
    doc_starts = doc_ends - lengths
    places = jnp.arange(total, dtype=jnp.int32)
    doc_ids = jnp.sum((places[:, None] >= doc_ends[None, :]).astype(jnp.int32), axis=1)
    owner = doc_ids[:, None] == jnp.arange(DOCS, dtype=jnp.int32)[None, :]
    begins = jnp.sum(jnp.where(owner, doc_starts[None, :], 0), axis=1)
    return doc_ids, places - begins


def rope_tables(doc_place):
    half_size = HD // 2
    freqs = jnp.exp(-math.log(ROPE_BASE) * 2.0 * jnp.arange(half_size, dtype=F32) / HD)
    angles = doc_place.astype(F32)[:, None] * freqs
    angles = jnp.concatenate([angles, angles], axis=-1)
    return jnp.cos(angles), jnp.sin(angles)


def turn(values):
    half_size = HD // 2
    return jnp.concatenate([-values[..., half_size:], values[..., :half_size]], axis=-1)


def turn_back(values):
    half_size = HD // 2
    return jnp.concatenate([values[..., half_size:], -values[..., :half_size]], axis=-1)


def shards(
    hidden_in,
    grad_out,
    doc_lengths,
    expert_ids,
    attn_gain,
    query_gain,
    key_gain,
    mlp_gain,
    w_query,
    w_key,
    w_value,
    w_output,
    w_router,
    w_gate,
    w_up,
    w_down,
):
    length = hidden_in.shape[0]
    members = lax.axis_size("shard")
    planes = lax.axis_size("expert")
    me = lax.axis_index("shard")
    mz = lax.axis_index("expert")
    md = lax.axis_index("dp")
    total = length * members
    experts = planes * members
    capacity = 5 * length * TOP // (4 * experts)
    own = D // members
    local_heads = HEADS // members
    scale = HD ** (-0.5)
    others = range(1, members)

    def swap(value, k):
        return lax.ppermute(value, "shard", [(i, i ^ k) for i in range(members)])

    def fetch_z(value, j):
        return lax.ppermute(value, "expert", [(i, (i - j) % planes) for i in range(planes)])

    def return_z(value, j):
        return lax.ppermute(value, "expert", [(i, (i + j) % planes) for i in range(planes)])

    def swap_dp(value):
        return lax.ppermute(value, "dp", [(0, 1), (1, 0)])

    def plane_gather(value):
        relative = jnp.stack([value] + [swap(value, k) for k in others])
        return jnp.concatenate([at(relative, me ^ j) for j in range(members)], axis=0)

    def plane_sum(value):
        result = value
        for k in others:
            result = result + swap(value, k)
        return result

    def plane_scatter(partial, rows):
        pieces = partial.reshape(members, rows, partial.shape[1])
        result = at(pieces, me)
        low = pieces.astype(BF16)
        for k in others:
            result = result + swap(at(low, me ^ k), k).astype(F32)
        return result

    def order_z(values):
        stack = jnp.stack(values)
        return [at(stack, (z - mz) % planes) for z in range(planes)]

    small = jnp.concatenate([w_router.T, attn_gain[None], mlp_gain[None]], axis=0)
    small_all = jnp.stack([small] + [swap(small, k) for k in others])
    small_all = jnp.concatenate([at(small_all, me ^ j) for j in range(members)], axis=1)
    router_t = small_all[:experts]
    gain_attn = small_all[experts].astype(F32)
    gain_mlp = small_all[experts + 1].astype(F32)
    gain_query = query_gain.astype(F32)
    gain_key = key_gain.astype(F32)

    hidden_all = plane_gather(hidden_in).astype(F32)

    half = own // 2

    def column_blocks(dest):
        return jnp.concatenate(
            [lax.dynamic_slice_in_dim(w, dest * own, own, 1) for w in (w_query, w_key, w_value)],
            axis=1,
        )

    got = []
    for k in others:
        block = column_blocks(me ^ k)
        got.append(swap(lax.dynamic_slice_in_dim(block, md * half, half, 0), k))
    got = jnp.stack(got)
    peer = swap_dp(got)
    first = jnp.where(md == 0, got, peer)
    second = jnp.where(md == 0, peer, got)
    blocks = jnp.concatenate([first, second], axis=1)
    blocks = jnp.concatenate([column_blocks(me)[None], blocks], axis=0)
    w_qkv = jnp.concatenate([at(blocks, me ^ j) for j in range(members)], axis=0)

    doc_ids, doc_place = doc_layout(doc_lengths[0], total)
    cosine, sine = rope_tables(doc_place)
    cosine, sine = cosine[:, None, :], sine[:, None, :]
    places = jnp.arange(total, dtype=jnp.int32)
    allowed = (
        (doc_ids[:, None] == doc_ids[None, :])
        & (places[None, :] <= places[:, None])
        & ((doc_ids[None, :] < DOCS - 1) | (places[None, :] == places[:, None]))
    )[None]

    ids_z = [expert_ids] + [fetch_z(expert_ids, j) for j in range(1, planes)]
    plane_experts = mz * members + jnp.arange(members, dtype=jnp.int32)
    slot_axis = jnp.arange(capacity, dtype=jnp.int32)

    def slots_of(ids):
        hit = jnp.any(ids[:, :, None] == plane_experts[None, None, :], axis=1)
        rank = jnp.cumsum(hit.astype(jnp.int32), axis=0) - 1
        place = jnp.where(hit, rank, -1).T
        return place[:, None, :] == slot_axis[None, :, None]

    picks = [slots_of(ids) for ids in ids_z]
    picks_low = [p.astype(BF16) for p in picks]

    def dispatch(blocks_z):
        received = []
        for j in range(planes):
            rows = lax.dot_general(
                picks_low[j], blocks_z[j], (((2,), (0,)), ((), ())), preferred_element_type=F32
            ).astype(BF16)
            received.append(
                jnp.stack([at(rows, me)] + [swap(at(rows, me ^ k), k) for k in others])
            )
        return jnp.stack(received).reshape(planes * members * capacity, D)

    def collect(rows):
        rows = rows.reshape(planes, members, capacity, D)
        sums = []
        for j in range(planes):
            relative = [rows[j, 0]] + [swap(rows[j, k], k) for k in others]
            relative = jnp.stack(relative)
            expert_rows = jnp.concatenate([at(relative, me ^ s) for s in range(members)], axis=0)
            pick = picks_low[j].reshape(members * capacity, length)
            sums.append(dot_tn(pick, expert_rows))
        result = sums[0]
        for j in range(1, planes):
            result = result + return_z(sums[j].astype(BF16), j).astype(F32)
        return result

    def whole(weight, axis):
        mine = weight[0]
        peer_half = swap_dp(mine)
        low_half = jnp.where(md == 0, mine, peer_half)
        high_half = jnp.where(md == 0, peer_half, mine)
        return jnp.concatenate([low_half, high_half], axis=axis)

    gate_full = whole(w_gate, 0)
    up_full = whole(w_up, 0)
    down_full = whole(w_down, 1)

    inv_in = lax.rsqrt(jnp.mean(hidden_all * hidden_all, axis=-1, keepdims=True) + EPSILON)
    attn_input = (hidden_all * inv_in * gain_attn).astype(BF16)
    raw = dot(attn_input, w_qkv)
    query_raw = raw[:, :own]
    key_raw = raw[:, own : 2 * own]
    value_rows = raw[:, 2 * own :].astype(BF16)
    squares = jnp.stack([jnp.sum(query_raw * query_raw, axis=-1), jnp.sum(key_raw * key_raw, axis=-1)])
    squares = plane_sum(squares)
    inverse = lax.rsqrt(squares / D + EPSILON)
    inv_query, inv_key = inverse[0][:, None], inverse[1][:, None]

    def to_heads(rows):
        return rows.reshape(total, local_heads, HD)

    def rope(rows):
        v = to_heads(rows)
        return v * cosine + turn(v) * sine

    query_heads = rope(query_raw * inv_query * gain_query).astype(BF16)
    key_heads = rope(key_raw * inv_key * gain_key).astype(BF16)
    value_heads = to_heads(value_rows)
    scores = jnp.einsum("qhd,khd->hqk", query_heads, key_heads, preferred_element_type=F32) * scale
    scores = jnp.where(allowed, scores, NEG_FILL)
    row_max = jnp.max(scores, axis=-1, keepdims=True)
    exp_terms = jnp.exp(scores - row_max)
    probs = exp_terms / jnp.sum(exp_terms, axis=-1, keepdims=True)
    probs_low = probs.astype(BF16)
    mixed = jnp.einsum("hqk,khd->qhd", probs_low, value_heads, preferred_element_type=F32)
    mixed = mixed.astype(BF16).reshape(total, own)
    residual = hidden_in.astype(F32) + plane_scatter(dot(mixed, w_output), length)

    inv_mlp = lax.rsqrt(jnp.mean(residual * residual, axis=-1, keepdims=True) + EPSILON)
    unit_mlp = residual * inv_mlp
    mlp_input = (unit_mlp * gain_mlp).astype(BF16)
    logits = dot_nt(mlp_input, router_t)
    top_logit = jnp.max(logits, axis=-1, keepdims=True)
    exp_logits = jnp.exp(logits - top_logit)
    route = exp_logits / jnp.sum(exp_logits, axis=-1, keepdims=True)

    input_z = [mlp_input] + [fetch_z(mlp_input, j) for j in range(1, planes)]
    route_z = [route] + [fetch_z(route, j) for j in range(1, planes)]
    grads_z = [grad_out] + [fetch_z(grad_out, j) for j in range(1, planes)]
    gate_parts = []
    for j in range(planes):
        local_route = lax.dynamic_slice_in_dim(route_z[j], mz * members, members, 1).T
        gate_parts.append(jnp.sum(jnp.where(picks[j], local_route[:, None, :], 0.0), axis=-1))
    gate_slots = jnp.stack(gate_parts, axis=1)
    gate_rows = jnp.stack(
        [at(gate_slots, me)] + [swap(at(gate_slots, me ^ k), k) for k in others], axis=1
    ).reshape(planes * members * capacity)[:, None]
    slot_rows = dispatch(input_z)
    slot_grads = dispatch(grads_z)

    gate_pre = dot(slot_rows, gate_full)
    up_pre = dot(slot_rows, up_full)
    sig = jax.nn.sigmoid(gate_pre)
    silu = gate_pre * sig
    middle = (silu * up_pre).astype(BF16)
    raw_grad = dot_nt(slot_grads, down_full)
    gate_grad = jnp.sum(raw_grad * middle.astype(F32), axis=-1)
    grad_middle = raw_grad * gate_rows
    grad_gate_pre = (grad_middle * up_pre * sig * (1.0 + gate_pre * (1.0 - sig))).astype(BF16)
    grad_up_pre = (grad_middle * silu).astype(BF16)
    grad_rows = (dot_nt(grad_gate_pre, gate_full) + dot_nt(grad_up_pre, up_full)).astype(BF16)
    grad_mlp_in = collect(grad_rows)
    weighted = (dot(middle, down_full) * gate_rows).astype(BF16)
    block_out = (residual + collect(weighted)).astype(BF16)
    slot_dy = (slot_grads.astype(F32) * gate_rows).astype(BF16)
    grad_down_full = dot_tn(middle, slot_dy)
    grad_gate_full = dot_tn(slot_rows, grad_gate_pre)
    grad_up_full = dot_tn(slot_rows, grad_up_pre)

    def halves_sum(full, axis):
        size = full.shape[axis] // 2
        mine = lax.dynamic_slice_in_dim(full, md * size, size, axis)
        away = lax.dynamic_slice_in_dim(full, (1 - md) * size, size, axis)
        return mine + swap_dp(away.astype(BF16)).astype(F32)

    grad_gate = halves_sum(grad_gate_full, 0)[None]
    grad_up = halves_sum(grad_up_full, 0)[None]
    grad_down = halves_sum(grad_down_full, 1)[None]

    gate_grad = gate_grad.reshape(planes, members, capacity)
    relative = jnp.stack([gate_grad[:, 0]] + [swap(gate_grad[:, k], k) for k in others])
    by_expert = jnp.stack([at(relative, me ^ s) for s in range(members)])
    parts = []
    for j in range(planes):
        parts.append(jnp.sum(jnp.where(picks[j], by_expert[:, j, :, None], 0.0), axis=1))
    parts = [parts[0]] + [return_z(parts[j], j) for j in range(1, planes)]
    parts = jnp.stack(parts)
    grad_route = jnp.concatenate([at(parts, (mz - z) % planes) for z in range(planes)], axis=0).T
    grad_logits = (
        route * (grad_route - jnp.sum(route * grad_route, axis=-1, keepdims=True))
    ).astype(BF16)
    grad_mlp_in = grad_mlp_in + dot(grad_logits, router_t)
    grad_router_part = dot_tn(grad_logits, mlp_input)
    grad_gain_mlp_part = jnp.sum(grad_mlp_in * unit_mlp, axis=0)
    upstream = grad_out.astype(F32)
    scaled = grad_mlp_in * gain_mlp
    grad_residual = (
        upstream
        + (scaled - unit_mlp * jnp.mean(scaled * unit_mlp, axis=-1, keepdims=True)) * inv_mlp
    )
    grad_attn_all = plane_gather(grad_residual.astype(BF16))

    grad_output_part = dot_tn(mixed, grad_attn_all)
    grad_mixed = to_heads(dot_nt(grad_attn_all, w_output).astype(BF16))
    grad_value = jnp.einsum("hqk,qhd->khd", probs_low, grad_mixed, preferred_element_type=F32)
    grad_probs = jnp.einsum("qhd,khd->hqk", grad_mixed, value_heads, preferred_element_type=F32)
    row_delta = jnp.sum(probs * grad_probs, axis=-1, keepdims=True)
    grad_scores = (probs * (grad_probs - row_delta)).astype(BF16)
    grad_query_rot = (
        jnp.einsum("hqk,khd->qhd", grad_scores, key_heads, preferred_element_type=F32) * scale
    )
    grad_key_rot = (
        jnp.einsum("hqk,qhd->khd", grad_scores, query_heads, preferred_element_type=F32) * scale
    )

    def unrope(rows):
        return (rows * cosine + turn_back(rows * sine)).reshape(total, own)

    grad_query_normed = unrope(grad_query_rot)
    grad_key_normed = unrope(grad_key_rot)
    unit_query = query_raw * inv_query
    unit_key = key_raw * inv_key
    grad_gain_query = jnp.sum(grad_query_normed * unit_query, axis=0)
    grad_gain_key = jnp.sum(grad_key_normed * unit_key, axis=0)
    scaled_query = grad_query_normed * gain_query
    scaled_key = grad_key_normed * gain_key
    means = jnp.stack(
        [jnp.sum(scaled_query * unit_query, axis=-1), jnp.sum(scaled_key * unit_key, axis=-1)]
    )
    means = plane_sum(means) / D
    grad_query_low = ((scaled_query - unit_query * means[0][:, None]) * inv_query).astype(BF16)
    grad_key_low = ((scaled_key - unit_key * means[1][:, None]) * inv_key).astype(BF16)
    grad_value_low = grad_value.astype(BF16).reshape(total, own)
    grad_raw = jnp.concatenate([grad_query_low, grad_key_low, grad_value_low], axis=1)
    grad_attn_in = plane_scatter(dot_nt(grad_raw, w_qkv), length)
    inputs = hidden_in.astype(F32)
    inv_own = lax.rsqrt(jnp.mean(inputs * inputs, axis=-1, keepdims=True) + EPSILON)
    unit_in = inputs * inv_own
    grad_gain_attn_part = jnp.sum(grad_attn_in * unit_in, axis=0)
    scaled_in = grad_attn_in * gain_attn
    grad_in = (
        grad_residual
        + (scaled_in - unit_in * jnp.mean(scaled_in * unit_in, axis=-1, keepdims=True)) * inv_own
    )

    grad_qkv = dot_tn(attn_input, grad_raw)
    slab = half // planes

    def scatter_sum(pieces):
        mine = at(pieces, md)
        mine = mine + swap_dp(at(pieces, 1 - md).astype(BF16)).astype(F32)
        result = at(mine, mz)
        low = mine.astype(BF16)
        for j in range(1, planes):
            result = result + return_z(at(low, (mz + j) % planes), j).astype(F32)
        return result

    def gather_back(piece):
        every = jnp.stack(order_z([piece] + [fetch_z(piece, j) for j in range(1, planes)]))
        peer_side = swap_dp(every)
        return jnp.stack([jnp.where(md == 0, every, peer_side), jnp.where(md == 0, peer_side, every)])

    pieces = grad_qkv.reshape(members, 2, planes, slab, 3 * own).transpose(1, 2, 0, 3, 4)
    piece = scatter_sum(pieces).astype(BF16)
    relative = jnp.stack([at(piece, me)] + [swap(at(piece, me ^ k), k) for k in others])
    piece = jnp.stack([at(relative, me ^ s) for s in range(members)])
    full = gather_back(piece)
    full = full.reshape(2, planes, members, slab, 3, own).transpose(4, 0, 1, 3, 2, 5)
    full = full.reshape(3, own, D).astype(F32)
    grad_query, grad_key, grad_value_w = full[0], full[1], full[2]

    piece = scatter_sum(grad_output_part.reshape(2, planes, slab, D)).astype(BF16)
    grad_output = gather_back(piece).reshape(own, D).astype(F32)

    small_part = jnp.concatenate(
        [grad_router_part, grad_gain_attn_part[None], grad_gain_mlp_part[None]], axis=0
    )
    small_pieces = small_part.reshape(experts + 2, members, own).transpose(1, 0, 2)
    small_sum = at(small_pieces, me)
    for k in others:
        small_sum = small_sum + swap(at(small_pieces, me ^ k), k)
    small_sum = jnp.concatenate([small_sum, grad_gain_query[None], grad_gain_key[None]], axis=0)
    small_sum = small_sum + swap_dp(small_sum)
    small_sum = order_z([small_sum] + [fetch_z(small_sum, j) for j in range(1, planes)])
    small_total = small_sum[0]
    for z in range(1, planes):
        small_total = small_total + small_sum[z]
    return (
        block_out,
        grad_in,
        small_total[experts],
        small_total[experts + 2],
        small_total[experts + 3],
        small_total[experts + 1],
        grad_query,
        grad_key,
        grad_value_w,
        grad_output,
        small_total[:experts].T,
        grad_gate,
        grad_up,
        grad_down,
    )


def solution(mesh):
    return jax.shard_map(
        shards,
        mesh=mesh,
        in_specs=(
            P(("dp", "expert", "shard"), None),
            P(("dp", "expert", "shard"), None),
            P(("dp", "expert"), None),
            P(("dp", "expert", "shard"), None),
            P("shard"),
            P("shard"),
            P("shard"),
            P("shard"),
            P("shard", None),
            P("shard", None),
            P("shard", None),
            P("shard", None),
            P("shard", None),
            P(("expert", "shard"), "dp", None),
            P(("expert", "shard"), "dp", None),
            P(("expert", "shard"), None, "dp"),
        ),
        out_specs=(
            P(("dp", "expert", "shard"), None),
            P(("dp", "expert", "shard"), None),
            P("shard"),
            P("shard"),
            P("shard"),
            P("shard"),
            P("shard", None),
            P("shard", None),
            P("shard", None),
            P("shard", None),
            P("shard", None),
            P(("expert", "shard"), "dp", None),
            P(("expert", "shard"), "dp", None),
            P(("expert", "shard"), None, "dp"),
        ),
        check_vma=False,
    )
```

time: 1940 us -> 1260 us (0.65)
  waiting for transfers between devices: 1370 us -> 606 us
  starting transfers between devices: 43.9 us -> 153 us
  blocking collectives: 103 us -> 0 us
  local copies, waits for them, and re-layouts: 72.5 us -> 145 us
  other arithmetic: 88.9 us -> 131 us
  matrix products: 230 us -> 207 us
    ppermute x0 -> x132, waiting for transfers between devices: none -> 606 us  [the longest x84 290 us: swap(): return lax.ppermute(value, 'shard', [(i, i ^ k) for i in range(members)])]
    all_to_all x4 -> x0, waiting for transfers between devices: 515 us -> none  [the longest x1 143 us: shards(): lax.all_to_all(grad_rows, ('expert', 'shard'), split_axis=0, concat_axis=...]
    all_gather x9 -> x0, waiting for transfers between devices: 401 us -> none  [the longest x1 84.1 us: shards(): lax.all_gather(w_key, 'shard', axis=0, tiled=True)]
    reduce_scatter x10 -> x0, waiting for transfers between devices: 388 us -> none  [the longest x1 89.6 us: shards(): lax.psum_scatter(grad_query_full.astype(jnp.bfloat16), 'shard', scatter_d...]
    ppermute x0 -> x132, starting transfers between devices: none -> 153 us  [the longest x84 77.3 us: swap(): return lax.ppermute(value, 'shard', [(i, i ^ k) for i in range(members)])]
    psum x1 -> x0, waiting for transfers between devices: 61.7 us -> none  [shards(): lax.psum(local_sums[4].astype(jnp.bfloat16), ('dp', 'expert'))]
    all_gather x5 -> x0, blocking collectives: 59.7 us -> none  [the longest x1 35.1 us: shards(): lax.all_gather(w_router, 'shard', axis=0, tiled=True)]
    all_to_all x4 -> x0, starting transfers between devices: 42.1 us -> none  [the longest x1 14.1 us: shards(): lax.all_to_all(grad_buffer, ('expert', 'shard'), split_axis=0, concat_axi...]
  transfers between devices with their start and end apart: 24 -> 132, of which waited for: 23 -> 52; matrix products, arithmetic and copies ran while one was open for 14% -> 32% of each run, Pallas kernels for 0% -> 0%
where the time goes in v1:
time: 1260 us; the launch traced here: 1250 us
  waiting for transfers between devices  606 us (48%)
  matrix products  207 us (16%)
  starting transfers between devices  153 us (12%)
  local copies, waits for them, and re-layouts  145 us (12%)
  other arithmetic  131 us (10%)
    ppermute x84, waiting for transfers between devices, swap(): return lax.ppermute(value, 'shard', [(i, i ^ k) for i in range(members)])  290 us
    ppermute x15, waiting for transfers between devices, return_z(): lax.ppermute(value, 'expert', [(i, (i + j) % planes) for i in range(plane...  167 us
    ppermute x21, waiting for transfers between devices, fetch_z(): lax.ppermute(value, 'expert', [(i, (i - j) % planes) for i in range(plane...  146 us
    ppermute x84, starting transfers between devices, swap(): return lax.ppermute(value, 'shard', [(i, i ^ k) for i in range(members)])  77.3 us
    dot_general x14, matrix products, dot_tn(): lax.dot_general(a, b, (((0,), (0,)), ((), ())), preferred_element_type=F32)  59 us
    dot_general x6, matrix products, dot_nt(): lax.dot_general(a, b, (((1,), (1,)), ((), ())), preferred_element_type=F32)  58.4 us
    dot_general x6, matrix products, dot(): return jnp.dot(a, b, preferred_element_type=F32)  50.6 us
    unnamed x344, local copies, waits for them, and re-layouts  30.7 us
  transfers between devices with their start and end apart: 132, of which 52 were waited for; matrix products, arithmetic and copies ran while one was open for 32% of the time, Pallas kernels for 0%

profile of v1, /device:TPU:9, one launch (start us, length us, event | category | flops | bytes accessed | tf_op | source)
XLA Modules:
  0.0 1245.5 jit_solution(17244905151812232685)
XLA Ops:
  61.6 10.8 collective-permute-done.59
  72.5 31.1 %collective-permute-done.58 = bf16[120,2048]{1,0:T(8,128)(2,1)S(1)} collective-permute-done((bf16[120,2048]{1,0:T(8,128)(2,1)S(1)}, bf16[120,2048]{1,0:T(8,128)(2,1)S(1)}, u32[]{:S(2)}, u32[]{:S(2)}) %collective-permute-start.58) | collective-permute-done | bytes 491552 | tf_op jit(solution)/shard_map/ppermute | solution.py:99
  108.4 12.4 collective-permute-done.65
  123.4 16.9 %collective-permute-done.7 = bf16[256,1536]{1,0:T(8,128)(2,1)S(1)} collective-permute-done((bf16[256,1536]{1,0:T(8,128)(2,1)S(1)}, bf16[256,1536]{1,0:T(8,128)(2,1)S(1)}, u32[]{:S(2)}, u32[]{:S(2)}) %collective-permute-start.7) | collective-permute-done | bytes 786464 | tf_op jit(solution)/shard_map/ppermute | solution.py:99
  154.4 12.9 %collective-permute-done.67 = bf16[120,2048]{1,0:T(8,128)(2,1)S(1)} collective-permute-done((bf16[120,2048]{1,0:T(8,128)(2,1)S(1)}, bf16[120,2048]{1,0:T(8,128)(2,1)S(1)}, u32[]{:S(2)}, u32[]{:S(2)}) %collective-permute-start.67) | collective-permute-done | bytes 491552 | tf_op jit(solution)/shard_map/ppermute | solution.py:99
  174.5 13.7 %collective-permute-done.71 = bf16[120,2048]{1,0:T(8,128)(2,1)S(1)} collective-permute-done((bf16[120,2048]{1,0:T(8,128)(2,1)S(1)}, bf16[120,2048]{1,0:T(8,128)(2,1)S(1)}, u32[]{:S(2)}, u32[]{:S(2)}) %collective-permute-start.71) | collective-permute-done | bytes 491552 | tf_op jit(solution)/shard_map/ppermute | solution.py:99
  283.8 17.4 %collective-permute-done.15 = bf16[192,2048]{1,0:T(8,128)(2,1)S(1)} collective-permute-done((bf16[192,2048]{1,0:T(8,128)(2,1)S(1)}, bf16[192,2048]{1,0:T(8,128)(2,1)S(1)}, u32[]{:S(2)}, u32[]{:S(2)}) %collective-permute-start.15) | collective-permute-done | bytes 786464 | tf_op jit(solution)/shard_map/ppermute | solution.py:99
  311.0 12.5 %collective-permute-done.39 = f32[192,16]{0,1:T(8,128)S(1)} collective-permute-done((f32[192,16]{0,1:T(8,128)S(1)}, f32[192,16]{0,1:T(8,128)S(1)}, u32[]{:S(2)}, u32[]{:S(2)}) %collective-permute-start.39) | collective-permute-done | bytes 12320 | tf_op jit(solution)/shard_map/ppermute | solution.py:102
  336.9 39.1 %collective-permute-done.25 = bf16[192,2048]{1,0:T(8,128)(2,1)S(1)} collective-permute-done((bf16[192,2048]{1,0:T(8,128)(2,1)S(1)}, bf16[192,2048]{1,0:T(8,128)(2,1)S(1)}, u32[]{:S(2)}, u32[]{:S(2)}) %collective-permute-start.25) | collective-permute-done | bytes 786464 | tf_op jit(solution)/shard_map/ppermute | solution.py:102
  388.2 17.8 %collective-permute-done.27 = bf16[120,2048]{1,0:T(8,128)(2,1)S(1)} collective-permute-done((bf16[120,2048]{1,0:T(8,128)(2,1)S(1)}, bf16[120,2048]{1,0:T(8,128)(2,1)S(1)}, u32[]{:S(2)}, u32[]{:S(2)}) %collective-permute-start.27) | collective-permute-done | bytes 491552 | tf_op jit(solution)/shard_map/ppermute | solution.py:99
  408.9 13.8 %collective-permute-done.32 = bf16[120,2048]{1,0:T(8,128)(2,1)S(1)} collective-permute-done((bf16[120,2048]{1,0:T(8,128)(2,1)S(1)}, bf16[120,2048]{1,0:T(8,128)(2,1)S(1)}, u32[]{:S(2)}, u32[]{:S(2)}) %collective-permute-start.32) | collective-permute-done | bytes 491552 | tf_op jit(solution)/shard_map/ppermute | solution.py:99
  425.6 11.6 fusion.18
  437.2 13.3 %fusion.19 = f32[1920,1024]{0,1:T(8,128)} fusion(bf16[1920,2048]{1,0:T(8,128)(2,1)S(1)} %bitcast.705, bf16[1024,1024]{1,0:T(8,128)(2,1)} %get-tuple-element.101, bf16[1024,1024]{1,0:T(8,128)(2,1)} %get-tuple-element.100), kind=kOutput, calls=%fused_computation.65 | convolution fusion | flops 8061452288 | bytes 19922944 | tf_op jit(solution)/shard_map/dot_general | solution.py:23
  450.5 17.4 %multiply_reduce_fusion.1 = (f32[1920]{0:T(1024)S(1)}, bf16[1920,1024]{0,1:T(8,128)(2,1)}, f32[1920,1024]{0,1:T(8,128)}) fusion(f32[1920,1024]{0,1:T(8,128)} %fusion.18, f32[1920,1024]{0,1:T(8,128)} %fusion.19, bf16[1920,2048]{1,0:T(8,128)(2,1)} %bitcast.702, bf16[1024,1024]{1,0:T(8,128)(2,1)S(1)} %copy-done.47, bf16[1024,1024]{1,0:T(8,128)(2,1)S(1)} %copy-done.45), kind=kOutput, calls=%fused_computation.12 | convolution fusion | flops 8079144960 | bytes 39591424 | tf_op jit(solution)/shard_map/dot_general | solution.py:27
  489.4 15.1 %fusion.1 = f32[1024,2048]{1,0:T(8,128)} fusion(bf16[1920,1024]{0,1:T(8,128)(2,1)} %get-tuple-element.48, bf16[1920,2048]{1,0:T(8,128)(2,1)} %bitcast.703, f32[1920]{0:T(1024)S(1)} %mul.457), kind=kOutput, calls=%fused_computation.9 | convolution fusion | flops 8064860160 | bytes 20192768 | tf_op jit(solution)/shard_map/dot_general | solution.py:31
  504.6 13.1 %multiply_convert_fusion.1 = bf16[1920,2048]{1,0:T(8,128)(2,1)} fusion(bf16[1920,1024]{0,1:T(8,128)(2,1)} %get-tuple-element.48, f32[1920]{0:T(1024)S(1)} %mul.457, bf16[1024,1024]{1,0:T(8,128)(2,1)S(1)} %copy-done.48, bf16[1024,1024]{1,0:T(8,128)(2,1)S(1)} %copy-done.46), kind=kOutput, calls=%fused_computation.4 | convolution fusion | flops 8069316608 | bytes 15998464 | tf_op jit(solution)/shard_map/dot_general | solution.py:23
  527.3 13.6 %fusion.250 = f32[2048,1024]{1,0:T(8,128)} fusion(bf16[1920,2048]{1,0:T(8,128)(2,1)S(1)} %bitcast.708, bf16[1920,1024]{0,1:T(8,128)(2,1)} %get-tuple-element.55), kind=kOutput, calls=%fused_computation.622 | convolution fusion | flops 8053063680 | bytes 20185088 | tf_op jit(solution)/shard_map/dot_general | solution.py:31
  540.9 15.1 %fusion.17 = f32[1920,2048]{1,0:T(8,128)} fusion(bf16[1920,1024]{0,1:T(8,128)(2,1)} %get-tuple-element.55, bf16[1024,1024]{1,0:T(8,128)(2,1)S(1)} %copy-done.42, bf16[1024,1024]{1,0:T(8,128)(2,1)S(1)} %copy-done.44), kind=kOutput, calls=%fused_computation.63 | convolution fusion | flops 8061452288 | bytes 23855104 | tf_op jit(solution)/shard_map/dot_general | solution.py:27
  561.4 11.7 fusion.249
  581.2 14.2 %add_convert_fusion = bf16[1920,2048]{1,0:T(8,128)(2,1)} fusion(f32[1920,2048]{1,0:T(8,128)} %fusion.17, bf16[1920,1024]{0,1:T(8,128)(2,1)S(1)} %copy-done.24, bf16[1024,1024]{1,0:T(8,128)(2,1)} %get-tuple-element.101, bf16[1024,1024]{1,0:T(8,128)(2,1)S(1)} %copy-done.49), kind=kOutput, calls=%fused_computation.3 | convolution fusion | flops 8069316608 | bytes 31719424 | tf_op jit(solution)/shard_map/dot_general | solution.py:27
  638.3 19.1 %collective-permute-done.82 = bf16[120,2048]{1,0:T(8,128)(2,1)S(1)} collective-permute-done((bf16[120,2048]{1,0:T(8,128)(2,1)S(1)}, bf16[120,2048]{1,0:T(8,128)(2,1)S(1)}, u32[]{:S(2)}, u32[]{:S(2)}) %collective-permute-start.82) | collective-permute-done | bytes 491552 | tf_op jit(solution)/shard_map/ppermute | solution.py:99
  658.5 18.0 %collective-permute-done.81 = bf16[120,2048]{1,0:T(8,128)(2,1)S(1)} collective-permute-done((bf16[120,2048]{1,0:T(8,128)(2,1)S(1)}, bf16[120,2048]{1,0:T(8,128)(2,1)S(1)}, u32[]{:S(2)}, u32[]{:S(2)}) %collective-permute-start.81) | collective-permute-done | bytes 491552 | tf_op jit(solution)/shard_map/ppermute | solution.py:99
  679.6 11.9 collective-permute-done.77
  739.2 29.6 %collective-permute-done.83 = bf16[192,2048]{1,0:T(8,128)(2,1)S(1)} collective-permute-done((bf16[192,2048]{1,0:T(8,128)(2,1)S(1)}, bf16[192,2048]{1,0:T(8,128)(2,1)S(1)}, u32[]{:S(2)}, u32[]{:S(2)}) %collective-permute-start.83) | collective-permute-done | bytes 786464 | tf_op jit(solution)/shard_map/ppermute | solution.py:105
  776.5 26.6 %collective-permute-done.49 = bf16[192,2048]{1,0:T(8,128)(2,1)S(1)} collective-permute-done((bf16[192,2048]{1,0:T(8,128)(2,1)S(1)}, bf16[192,2048]{1,0:T(8,128)(2,1)S(1)}, u32[]{:S(2)}, u32[]{:S(2)}) %collective-permute-start.49) | collective-permute-done | bytes 786464 | tf_op jit(solution)/shard_map/ppermute | solution.py:105
  804.9 30.9 %collective-permute-done.53 = bf16[192,2048]{1,0:T(8,128)(2,1)} collective-permute-done((bf16[192,2048]{1,0:T(8,128)(2,1)}, bf16[192,2048]{1,0:T(8,128)(2,1)}, u32[]{:S(2)}, u32[]{:S(2)}) %collective-permute-start.53) | collective-permute-done | bytes 786464 | tf_op jit(solution)/shard_map/ppermute | solution.py:105
  835.8 10.7 collective-permute-start.131
  948.3 15.6 %collective-permute-done.102 = bf16[192,2048]{1,0:T(8,128)(2,1)S(1)} collective-permute-done((bf16[192,2048]{1,0:T(8,128)(2,1)S(1)}, bf16[192,2048]{1,0:T(8,128)(2,1)S(1)}, u32[]{:S(2)}, u32[]{:S(2)}) %collective-permute-start.102) | collective-permute-done | bytes 786464 | tf_op jit(solution)/shard_map/ppermute | solution.py:99
  989.3 12.3 collective-permute-done.111
  1002.0 18.3 %collective-permute-done.113 = bf16[4,64,1536]{2,1,0:T(8,128)(2,1)S(1)} collective-permute-done((bf16[4,64,1536]{2,1,0:T(8,128)(2,1)S(1)}, bf16[4,64,1536]{2,1,0:T(8,128)(2,1)S(1)}, u32[]{:S(2)}, u32[]{:S(2)}) %collective-permute-start.113) | collective-permute-done | bytes 786464 | tf_op jit(solution)/shard_map/ppermute | solution.py:105
  1020.4 35.4 %collective-permute-done.112 = bf16[4,64,1536]{2,1,0:T(8,128)(2,1)S(1)} collective-permute-done((bf16[4,64,1536]{2,1,0:T(8,128)(2,1)S(1)}, bf16[4,64,1536]{2,1,0:T(8,128)(2,1)S(1)}, u32[]{:S(2)}, u32[]{:S(2)}) %collective-permute-start.112) | collective-permute-done | bytes 786464 | tf_op jit(solution)/shard_map/ppermute | solution.py:105
  1091.8 73.7 %collective-permute-done.126 = bf16[64,2048]{1,0:T(8,128)(2,1)S(1)} collective-permute-done((bf16[64,2048]{1,0:T(8,128)(2,1)S(1)}, bf16[64,2048]{1,0:T(8,128)(2,1)S(1)}, u32[]{:S(2)}, u32[]{:S(2)}) %collective-permute-start.126) | collective-permute-done | bytes 262176 | tf_op jit(solution)/shard_map/ppermute | solution.py:102
  (873 shorter events, 615.9 us)
Async XLA Ops:
  51.5 52.3 %collective-permute-start = (bf16[192,2048]{1,0:T(8,128)(2,1)S(1)}, bf16[192,2048]{1,0:T(8,128)(2,1)S(1)}, u32[]{:S(2)}, u32[]{:S(2)}) collective-permute-start(bf16[192,2048]{1,0:T(8,128)(2,1)S(1)} %copy-done.8), channel_id=1, source_target_pairs={{0,1},{1,0},{2,3},{3,2},{4,5},{5,4},{6,7},{7,6},{8,9},{9,8},{10,11... | collective-permute-start | bytes 2359304 | tf_op jit(solution)/shard_map/ppermute | solution.py:99
  51.8 53.7 %collective-permute-start.2 = (bf16[192,2048]{1,0:T(8,128)(2,1)S(1)}, bf16[192,2048]{1,0:T(8,128)(2,1)S(1)}, u32[]{:S(2)}, u32[]{:S(2)}) collective-permute-start(bf16[192,2048]{1,0:T(8,128)(2,1)S(1)} %copy-done.8), channel_id=1, source_target_pairs={{0,3},{1,2},{2,1},{3,0},{4,7},{5,6},{6,5},{7,4},{8,11},{9,10},{10,... | collective-permute-start | bytes 2359304 | tf_op jit(solution)/shard_map/ppermute | solution.py:99
  54.0 52.1 %collective-permute-start.1 = (bf16[192,2048]{1,0:T(8,128)(2,1)S(1)}, bf16[192,2048]{1,0:T(8,128)(2,1)S(1)}, u32[]{:S(2)}, u32[]{:S(2)}) collective-permute-start(bf16[192,2048]{1,0:T(8,128)(2,1)S(1)} %copy-done.8), channel_id=1, source_target_pairs={{0,2},{1,3},{2,0},{3,1},{4,6},{5,7},{6,4},{7,5},{8,10},{9,11},{10,... | collective-permute-start | bytes 2359304 | tf_op jit(solution)/shard_map/ppermute | solution.py:99
  143.2 64.0 %collective-permute-start.9 = (bf16[3,256,1536]{2,1,0:T(8,128)(2,1)S(1)}, bf16[3,256,1536]{2,1,0:T(8,128)(2,1)S(1)}, u32[]{:S(2)}, u32[]{:S(2)}) collective-permute-start(bf16[3,256,1536]{2,1,0:T(8,128)(2,1)S(1)} %pad_maximum_fusion.18), channel_id=1, source_target_pairs={{0,16},{16,0},{1,17},{17,1},{2,18},{18,2},{3,19},{19,3},{4,20},{20... | collective-permute-start | bytes 7077896 | tf_op jit(solution)/shard_map/ppermute | solution.py:108
  188.5 83.3 %collective-permute-start.36 = (bf16[1024,1024]{1,0:T(8,128)(2,1)}, bf16[1024,1024]{1,0:T(8,128)(2,1)}, u32[]{:S(2)}, u32[]{:S(2)}) collective-permute-start(bf16[1024,1024]{1,0:T(8,128)(2,1)} %bitcast.88), channel_id=1, source_target_pairs={{0,16},{16,0},{1,17},{17,1},{2,18},{18,2},{3,19},{19,3},{4,20},{20... | collective-permute-start | bytes 6291464 | tf_op jit(solution)/shard_map/ppermute | solution.py:108
  194.1 77.7 %collective-permute-start.35 = (bf16[1024,1024]{1,0:T(8,128)(2,1)}, bf16[1024,1024]{1,0:T(8,128)(2,1)}, u32[]{:S(2)}, u32[]{:S(2)}) collective-permute-start(bf16[1024,1024]{1,0:T(8,128)(2,1)} %bitcast.87), channel_id=1, source_target_pairs={{0,16},{16,0},{1,17},{17,1},{2,18},{18,2},{3,19},{19,3},{4,20},{20... | collective-permute-start | bytes 6291464 | tf_op jit(solution)/shard_map/ppermute | solution.py:108
  327.0 51.1 %collective-permute-start.30 = (bf16[192,2048]{1,0:T(8,128)(2,1)S(1)}, bf16[192,2048]{1,0:T(8,128)(2,1)S(1)}, u32[]{:S(2)}, u32[]{:S(2)}) collective-permute-start(bf16[192,2048]{1,0:T(8,128)(2,1)S(1)} %multiply_convert_fusion.9), channel_id=1, source_target_pairs={{0,4},{4,8},{8,12},{12,0},{1,5},{5,9},{9,13},{13,1},{2,6},{6,10},{... | collective-permute-start | bytes 2359304 | tf_op jit(solution)/shard_map/ppermute | solution.py:102
  406.0 64.8 %collective-permute-start.37 = (f32[192,16]{0,1:T(8,128)S(1)}, f32[192,16]{0,1:T(8,128)S(1)}, u32[]{:S(2)}, u32[]{:S(2)}) collective-permute-start(f32[192,16]{0,1:T(8,128)S(1)} %fusion.187), channel_id=1, source_target_pairs={{0,12},{4,0},{8,4},{12,8},{1,13},{5,1},{9,5},{13,9},{2,14},{6,2},{... | collective-permute-start | bytes 36872 | tf_op jit(solution)/shard_map/ppermute | solution.py:102
  481.7 123.7 %collective-permute-start.93 = (f32[4,192]{0,1:T(8,128)}, f32[4,192]{0,1:T(8,128)}, u32[]{:S(2)}, u32[]{:S(2)}) collective-permute-start(f32[4,192]{0,1:T(8,128)} %get-tuple-element.32), channel_id=1, source_target_pairs={{0,12},{4,0},{8,4},{12,8},{1,13},{5,1},{9,5},{13,9},{2,14},{6,2},{... | collective-permute-start | bytes 9224 | tf_op jit(solution)/shard_map/ppermute | solution.py:105
  488.0 119.6 %collective-permute-start.92 = (f32[4,192]{0,1:T(8,128)}, f32[4,192]{0,1:T(8,128)}, u32[]{:S(2)}, u32[]{:S(2)}) collective-permute-start(f32[4,192]{0,1:T(8,128)} %get-tuple-element.30), channel_id=1, source_target_pairs={{0,8},{4,12},{8,0},{12,4},{1,9},{5,13},{9,1},{13,5},{2,10},{6,14},... | collective-permute-start | bytes 9224 | tf_op jit(solution)/shard_map/ppermute | solution.py:105
  488.0 121.9 %collective-permute-start.91 = (f32[4,192]{0,1:T(8,128)}, f32[4,192]{0,1:T(8,128)S(1)}, u32[]{:S(2)}, u32[]{:S(2)}) collective-permute-start(f32[4,192]{0,1:T(8,128)} %get-tuple-element.28), channel_id=1, source_target_pairs={{0,4},{4,8},{8,12},{12,0},{1,5},{5,9},{9,13},{13,1},{2,6},{6,10},{... | collective-permute-start | bytes 9224 | tf_op jit(solution)/shard_map/ppermute | solution.py:105
  559.9 52.3 %collective-permute-start.56 = (bf16[120,2048]{1,0:T(8,128)(2,1)}, bf16[120,2048]{1,0:T(8,128)(2,1)}, u32[]{:S(2)}, u32[]{:S(2)}) collective-permute-start(bf16[120,2048]{1,0:T(8,128)(2,1)} %get-tuple-element.73), channel_id=1, source_target_pairs={{0,3},{1,2},{2,1},{3,0},{4,7},{5,6},{6,5},{7,4},{8,11},{9,10},{10,... | collective-permute-start | bytes 1474568 | tf_op jit(solution)/shard_map/ppermute | solution.py:99
  561.3 52.2 %collective-permute-start.55 = (bf16[120,2048]{1,0:T(8,128)(2,1)}, bf16[120,2048]{1,0:T(8,128)(2,1)}, u32[]{:S(2)}, u32[]{:S(2)}) collective-permute-start(bf16[120,2048]{1,0:T(8,128)(2,1)} %get-tuple-element.74), channel_id=1, source_target_pairs={{0,2},{1,3},{2,0},{3,1},{4,6},{5,7},{6,4},{7,5},{8,10},{9,11},{10,... | collective-permute-start | bytes 1474568 | tf_op jit(solution)/shard_map/ppermute | solution.py:99
  613.4 80.1 %collective-permute-start.48 = (bf16[120,2048]{1,0:T(8,128)(2,1)}, bf16[120,2048]{1,0:T(8,128)(2,1)S(1)}, u32[]{:S(2)}, u32[]{:S(2)}) collective-permute-start(bf16[120,2048]{1,0:T(8,128)(2,1)} %get-tuple-element.81), channel_id=1, source_target_pairs={{0,3},{1,2},{2,1},{3,0},{4,7},{5,6},{6,5},{7,4},{8,11},{9,10},{10,... | collective-permute-start | bytes 1474568 | tf_op jit(solution)/shard_map/ppermute | solution.py:99
  614.7 80.7 %collective-permute-start.47 = (bf16[120,2048]{1,0:T(8,128)(2,1)}, bf16[120,2048]{1,0:T(8,128)(2,1)S(1)}, u32[]{:S(2)}, u32[]{:S(2)}) collective-permute-start(bf16[120,2048]{1,0:T(8,128)(2,1)} %get-tuple-element.82), channel_id=1, source_target_pairs={{0,2},{1,3},{2,0},{3,1},{4,6},{5,7},{6,4},{7,5},{8,10},{9,11},{10,... | collective-permute-start | bytes 1474568 | tf_op jit(solution)/shard_map/ppermute | solution.py:99
  715.2 53.6 %collective-permute-start.83 = (bf16[192,2048]{1,0:T(8,128)(2,1)S(1)}, bf16[192,2048]{1,0:T(8,128)(2,1)S(1)}, u32[]{:S(2)}, u32[]{:S(2)}) collective-permute-start(bf16[192,2048]{1,0:T(8,128)(2,1)S(1)} %convolution_convert_fusion.9), channel_id=1, source_target_pairs={{0,8},{4,12},{8,0},{12,4},{1,9},{5,13},{9,1},{13,5},{2,10},{6,14},... | collective-permute-start | bytes 2359304 | tf_op jit(solution)/shard_map/ppermute | solution.py:105
  772.7 63.0 %collective-permute-start.53 = (bf16[192,2048]{1,0:T(8,128)(2,1)}, bf16[192,2048]{1,0:T(8,128)(2,1)}, u32[]{:S(2)}, u32[]{:S(2)}) collective-permute-start(bf16[192,2048]{1,0:T(8,128)(2,1)} %convolution_convert_fusion.12), channel_id=1, source_target_pairs={{0,8},{4,12},{8,0},{12,4},{1,9},{5,13},{9,1},{13,5},{2,10},{6,14},... | collective-permute-start | bytes 2359304 | tf_op jit(solution)/shard_map/ppermute | solution.py:105
  774.1 72.4 %collective-permute-start.57 = (bf16[192,2048]{1,0:T(8,128)(2,1)}, bf16[192,2048]{1,0:T(8,128)(2,1)}, u32[]{:S(2)}, u32[]{:S(2)}) collective-permute-start(bf16[192,2048]{1,0:T(8,128)(2,1)} %convolution_convert_fusion.11), channel_id=1, source_target_pairs={{0,12},{4,0},{8,4},{12,8},{1,13},{5,1},{9,5},{13,9},{2,14},{6,2},{... | collective-permute-start | bytes 2359304 | tf_op jit(solution)/shard_map/ppermute | solution.py:105
  775.2 77.2 %collective-permute-start.96 = (bf16[192,2048]{1,0:T(8,128)(2,1)S(1)}, bf16[192,2048]{1,0:T(8,128)(2,1)}, u32[]{:S(2)}, u32[]{:S(2)}) collective-permute-start(bf16[192,2048]{1,0:T(8,128)(2,1)S(1)} %fusion.234), channel_id=1, source_target_pairs={{0,3},{1,2},{2,1},{3,0},{4,7},{5,6},{6,5},{7,4},{8,11},{9,10},{10,... | collective-permute-start | bytes 2359304 | tf_op jit(solution)/shard_map/ppermute | solution.py:99
  776.1 76.2 %collective-permute-start.95 = (bf16[192,2048]{1,0:T(8,128)(2,1)S(1)}, bf16[192,2048]{1,0:T(8,128)(2,1)}, u32[]{:S(2)}, u32[]{:S(2)}) collective-permute-start(bf16[192,2048]{1,0:T(8,128)(2,1)S(1)} %fusion.234), channel_id=1, source_target_pairs={{0,2},{1,3},{2,0},{3,1},{4,6},{5,7},{6,4},{7,5},{8,10},{9,11},{10,... | collective-permute-start | bytes 2359304 | tf_op jit(solution)/shard_map/ppermute | solution.py:99
  835.8 93.6 %collective-permute-start.131 = (bf16[1024,1024]{1,0:T(8,128)(2,1)}, bf16[1024,1024]{1,0:T(8,128)(2,1)}, u32[]{:S(2)}, u32[]{:S(2)}) collective-permute-start(bf16[1024,1024]{1,0:T(8,128)(2,1)} %dynamic-slice_convert_fusion.1), channel_id=1, source_target_pairs={{0,16},{16,0},{1,17},{17,1},{2,18},{18,2},{3,19},{19,3},{4,20},{20... | collective-permute-start | bytes 6291464 | tf_op jit(solution)/shard_map/ppermute | solution.py:108
  846.4 121.9 %collective-permute-start.129 = (bf16[1024,1024]{1,0:T(8,128)(2,1)}, bf16[1024,1024]{1,0:T(8,128)(2,1)}, u32[]{:S(2)}, u32[]{:S(2)}) collective-permute-start(bf16[1024,1024]{1,0:T(8,128)(2,1)} %dynamic-slice_convert_fusion.3), channel_id=1, source_target_pairs={{0,16},{16,0},{1,17},{17,1},{2,18},{18,2},{3,19},{19,3},{4,20},{20... | collective-permute-start | bytes 6291464 | tf_op jit(solution)/shard_map/ppermute | solution.py:108
  919.4 58.4 %collective-permute-start.110 = (bf16[4,4,64,1536]{3,2,0,1:T(8,128)(2,1)}, bf16[4,4,64,1536]{3,2,0,1:T(8,128)(2,1)}, u32[]{:S(2)}, u32[]{:S(2)}) collective-permute-start(bf16[4,4,64,1536]{3,2,0,1:T(8,128)(2,1)} %fusion.13), channel_id=1, source_target_pairs={{0,16},{16,0},{1,17},{17,1},{2,18},{18,2},{3,19},{19,3},{4,20},{20... | collective-permute-start | bytes 9437192 | tf_op jit(solution)/shard_map/ppermute | solution.py:108
  947.1 136.4 %collective-permute-start.130 = (bf16[1024,1024]{1,0:T(8,128)(2,1)}, bf16[1024,1024]{1,0:T(8,128)(2,1)}, u32[]{:S(2)}, u32[]{:S(2)}) collective-permute-start(bf16[1024,1024]{1,0:T(8,128)(2,1)} %dynamic-slice_convert_fusion.2), channel_id=1, source_target_pairs={{0,16},{16,0},{1,17},{17,1},{2,18},{18,2},{3,19},{19,3},{4,20},{20... | collective-permute-start | bytes 6291464 | tf_op jit(solution)/shard_map/ppermute | solution.py:108
  977.7 111.4 %collective-permute-start.106 = (f32[20,512]{1,0:T(8,128)S(1)}, f32[20,512]{1,0:T(8,128)S(1)}, u32[]{:S(2)}, u32[]{:S(2)}) collective-permute-start(f32[20,512]{1,0:T(8,128)S(1)} %pad_maximum_fusion.45), channel_id=1, source_target_pairs={{0,16},{16,0},{1,17},{17,1},{2,18},{18,2},{3,19},{19,3},{4,20},{20... | collective-permute-start | bytes 122888 | tf_op jit(solution)/shard_map/ppermute | solution.py:108
  985.3 70.4 %collective-permute-start.112 = (bf16[4,64,1536]{2,1,0:T(8,128)(2,1)S(1)}, bf16[4,64,1536]{2,1,0:T(8,128)(2,1)S(1)}, u32[]{:S(2)}, u32[]{:S(2)}) collective-permute-start(bf16[4,64,1536]{2,1,0:T(8,128)(2,1)S(1)} %get-tuple-element.112), channel_id=1, source_target_pairs={{0,8},{4,12},{8,0},{12,4},{1,9},{5,13},{9,1},{13,5},{2,10},{6,14},... | collective-permute-start | bytes 2359304 | tf_op jit(solution)/shard_map/ppermute | solution.py:105
  1001.5 65.3 %collective-permute-start.122 = (bf16[64,2048]{1,0:T(8,128)(2,1)S(1)}, bf16[64,2048]{1,0:T(8,128)(2,1)S(1)}, u32[]{:S(2)}, u32[]{:S(2)}) collective-permute-start(bf16[64,2048]{1,0:T(8,128)(2,1)S(1)} %get-tuple-element.217), channel_id=1, source_target_pairs={{0,4},{4,8},{8,12},{12,0},{1,5},{5,9},{9,13},{13,1},{2,6},{6,10},{... | collective-permute-start | bytes 786440 | tf_op jit(solution)/shard_map/ppermute | solution.py:105
  1079.4 92.8 %collective-permute-start.118 = (bf16[4,64,1536]{2,1,0:T(8,128)(2,1)S(1)}, bf16[4,64,1536]{2,1,0:T(8,128)(2,1)S(1)}, u32[]{:S(2)}, u32[]{:S(2)}) collective-permute-start(bf16[4,64,1536]{2,1,0:T(8,128)(2,1)S(1)} %get-tuple-element.221), channel_id=1, source_target_pairs={{0,8},{4,12},{8,0},{12,4},{1,9},{5,13},{9,1},{13,5},{2,10},{6,14},... | collective-permute-start | bytes 2359304 | tf_op jit(solution)/shard_map/ppermute | solution.py:102
  1081.3 91.4 %collective-permute-start.117 = (bf16[4,64,1536]{2,1,0:T(8,128)(2,1)S(1)}, bf16[4,64,1536]{2,1,0:T(8,128)(2,1)S(1)}, u32[]{:S(2)}, u32[]{:S(2)}) collective-permute-start(bf16[4,64,1536]{2,1,0:T(8,128)(2,1)S(1)} %get-tuple-element.221), channel_id=1, source_target_pairs={{0,12},{4,0},{8,4},{12,8},{1,13},{5,1},{9,5},{13,9},{2,14},{6,2},{... | collective-permute-start | bytes 2359304 | tf_op jit(solution)/shard_map/ppermute | solution.py:102
  1083.6 89.2 %collective-permute-start.119 = (bf16[4,64,1536]{2,1,0:T(8,128)(2,1)S(1)}, bf16[4,64,1536]{2,1,0:T(8,128)(2,1)S(1)}, u32[]{:S(2)}, u32[]{:S(2)}) collective-permute-start(bf16[4,64,1536]{2,1,0:T(8,128)(2,1)S(1)} %get-tuple-element.221), channel_id=1, source_target_pairs={{0,4},{4,8},{8,12},{12,0},{1,5},{5,9},{9,13},{13,1},{2,6},{6,10},{... | collective-permute-start | bytes 2359304 | tf_op jit(solution)/shard_map/ppermute | solution.py:102
  1089.1 76.3 %collective-permute-start.126 = (bf16[64,2048]{1,0:T(8,128)(2,1)S(1)}, bf16[64,2048]{1,0:T(8,128)(2,1)S(1)}, u32[]{:S(2)}, u32[]{:S(2)}) collective-permute-start(bf16[64,2048]{1,0:T(8,128)(2,1)S(1)} %fusion.170), channel_id=1, source_target_pairs={{0,8},{4,12},{8,0},{12,4},{1,9},{5,13},{9,1},{13,5},{2,10},{6,14},... | collective-permute-start | bytes 786440 | tf_op jit(solution)/shard_map/ppermute | solution.py:102
  1090.3 81.8 %collective-permute-start.125 = (bf16[64,2048]{1,0:T(8,128)(2,1)S(1)}, bf16[64,2048]{1,0:T(8,128)(2,1)S(1)}, u32[]{:S(2)}, u32[]{:S(2)}) collective-permute-start(bf16[64,2048]{1,0:T(8,128)(2,1)S(1)} %fusion.170), channel_id=1, source_target_pairs={{0,12},{4,0},{8,4},{12,8},{1,13},{5,1},{9,5},{13,9},{2,14},{6,2},{... | collective-permute-start | bytes 786440 | tf_op jit(solution)/shard_map/ppermute | solution.py:102
  (266 other events, 6323.1 us)

commit v2 on v1

v2 whole, which is shorter than its diff:
```python
import functools
import math

import jax
import jax.numpy as jnp
from jax import lax
from jax.experimental import pallas as pl
from jax.experimental.pallas import tpu as pltpu
from jax.sharding import PartitionSpec as P

D = 2048
HEADS = 16
HD = 128
TOP = 8
DOCS = 4

EPSILON = 1e-05
ROPE_BASE = 10000.0
NEG_FILL = -1e30

F32 = jnp.float32
BF16 = jnp.bfloat16


def dot(a, b):
    return jnp.dot(a, b, preferred_element_type=F32)


def dot_nt(a, b):
    return lax.dot_general(a, b, (((1,), (1,)), ((), ())), preferred_element_type=F32)


def dot_tn(a, b):
    return lax.dot_general(a, b, (((0,), (0,)), ((), ())), preferred_element_type=F32)


def at(stack, index):
    return lax.dynamic_index_in_dim(stack, index, 0, keepdims=False)


def doc_layout(lengths, total):
    doc_ends = jnp.cumsum(lengths)
    doc_starts = doc_ends - lengths
    places = jnp.arange(total, dtype=jnp.int32)
    doc_ids = jnp.sum((places[:, None] >= doc_ends[None, :]).astype(jnp.int32), axis=1)
    owner = doc_ids[:, None] == jnp.arange(DOCS, dtype=jnp.int32)[None, :]
    begins = jnp.sum(jnp.where(owner, doc_starts[None, :], 0), axis=1)
    return doc_ids, places - begins


def rope_tables(doc_place):
    half_size = HD // 2
    freqs = jnp.exp(-math.log(ROPE_BASE) * 2.0 * jnp.arange(half_size, dtype=F32) / HD)
    angles = doc_place.astype(F32)[:, None] * freqs
    angles = jnp.concatenate([angles, angles], axis=-1)
    return jnp.cos(angles), jnp.sin(angles)


PART = 256
MIB = 1024 * 1024


def call(body, args, kinds, outs, scratch=(), vmem=40, flops=0, moved=0, after=()):
    spaces = {"v": pltpu.VMEM, "s": pltpu.SMEM, "a": pl.ANY}
    count = len(args)

    def run(*refs):
        body(*refs[:count], *refs[count + len(after) :])

    return pl.pallas_call(
        run,
        out_shape=[jax.ShapeDtypeStruct(shape, dtype) for shape, dtype in outs],
        in_specs=[pl.BlockSpec(memory_space=spaces[kind]) for kind in kinds + "a" * len(after)],
        out_specs=[pl.BlockSpec(memory_space=pltpu.VMEM) for _ in outs],
        scratch_shapes=list(scratch),
        compiler_params=pltpu.CompilerParams(vmem_limit_bytes=vmem * MIB),
        cost_estimate=pl.CostEstimate(flops=flops, bytes_accessed=moved, transcendentals=0),
    )(*args, *after)


def copy_all(pairs, sems):
    copies = [pltpu.make_async_copy(a, b, sems.at[i]) for i, (a, b) in enumerate(pairs)]
    for c in copies:
        c.start()
    for c in copies:
        c.wait()


def iota(shape, axis):
    return lax.broadcasted_iota(jnp.int32, shape, axis)


def split3(x):
    hi = x.astype(BF16).astype(F32)
    mid = (x - hi).astype(BF16).astype(F32)
    lo = (x - hi - mid).astype(BF16).astype(F32)
    return hi, mid, lo


def pick_rows(place, slots):
    return jnp.where(iota((slots, place.shape[1]), 0) == place, 1.0, 0.0).astype(BF16)


def dispatch_body(gated, members, capacity, slots, idx, place, rows, *outs):
    length = place.shape[1]
    me, mz = idx[0], idx[1]
    source = rows[0:length, :]
    for k in range(members):
        expert = mz * members + (me ^ k)
        pick = pick_rows(place[pl.ds(expert, 1), :], slots)
        result = dot(pick, source)
        outs[k][...] = result.astype(BF16)
        if gated:
            experts = place.shape[0]
            head = result[:, 0:128]
            row = iota((slots, 128), 0)
            for part in range(3):
                table = rows[length : length + experts, part * PART : part * PART + length].astype(F32)
                gate = jnp.sum(jnp.where(iota(table.shape, 0) == expert, table, 0.0), axis=0, keepdims=True)
                gate = jnp.broadcast_to(gate, (8, length)).astype(BF16)
                slot = dot_nt(gate, pick)[0:1, :]
                if slots < 128:
                    slot = jnp.concatenate([slot, jnp.zeros((1, 128 - slots), F32)], axis=1)
                head = head + jnp.where(row == capacity + part, slot, 0.0)
            outs[k][:, 0:128] = head.astype(BF16)


def expert_body(members, capacity, slots, first, idx, *refs):
    xs, cs = refs[:members], refs[members : 2 * members]
    ga, gb, ua, ub, da, db = refs[2 * members : 2 * members + 6]
    rest = refs[2 * members + 6 :]
    ds, (gm, dz, du), (x, c, sems) = rest[:members], rest[members : members + 3], rest[members + 3 :]
    pairs = [(xs[k], x.at[pl.ds(k * slots, slots)]) for k in range(members)]
    pairs += [(cs[k].at[pl.ds(first, slots)], c.at[pl.ds(k * slots, slots)]) for k in range(members)]
    copy_all(pairs, sems)
    md = idx[2]
    half = ga.shape[0]
    inner = ga.shape[1]
    mine = pl.ds(pl.multiple_of(md * half, half), half)
    peer = pl.ds(pl.multiple_of((1 - md) * half, half), half)
    rows = members * slots
    eye = iota((slots, 128), 0) == iota((slots, 128), 1)
    row = iota((slots, 128), 0)
    gates = []
    for k in range(members):
        part = x[k * slots : (k + 1) * slots, 0:128].astype(F32)
        line = jnp.sum(
            jnp.where((row >= capacity) & (row < capacity + 3), part, 0.0), axis=0, keepdims=True
        )
        gates.append(jnp.sum(jnp.where(eye, line, 0.0), axis=1, keepdims=True))
    gate = jnp.concatenate(gates, axis=0)
    gate_grad = jnp.zeros((rows, 1), F32)
    step = 512
    for n in range(0, inner, step):
        cols = slice(n, n + step)
        z = dot(x[:, mine], ga[:, cols]) + dot(x[:, peer], gb[:, cols])
        u = dot(x[:, mine], ua[:, cols]) + dot(x[:, peer], ub[:, cols])
        raw = dot_nt(c[:, mine], da[cols, :]) + dot_nt(c[:, peer], db[cols, :])
        sig = 1.0 / (1.0 + jnp.exp(-z))
        silu = z * sig
        middle = silu * u
        gate_grad = gate_grad + jnp.sum(
            raw * middle.astype(BF16).astype(F32), axis=1, keepdims=True
        )
        gm[:, cols] = (gate * middle).astype(BF16)
        raw = raw * gate
        dz[:, cols] = (raw * u * sig * (1.0 + z * (1.0 - sig))).astype(BF16)
        du[:, cols] = (raw * silu).astype(BF16)
    lines = []
    for k in range(members):
        col = gate_grad[k * slots : (k + 1) * slots]
        lines.append(jnp.sum(jnp.where(eye, col, 0.0), axis=0, keepdims=True))
    for part, (wg, wu) in ((mine, (ga, ua)), (peer, (gb, ub))):
        result = dot_nt(dz[...], wg[...]) + dot_nt(du[...], wu[...])
        for k in range(members):
            ds[k][:, part] = result[k * slots : (k + 1) * slots].astype(BF16)
    for k in range(members):
        head = ds[k][:, 0:128].astype(F32)
        for i, value in enumerate(split3(lines[k])):
            head = head + jnp.where(row == capacity + i, value, 0.0)
        ds[k][:, 0:128] = head.astype(BF16)


def collect_body(graded, low, members, capacity, slots, idx, place, *refs):
    rows, outs, (stack, pick, sems) = refs[:members], refs[members:-3], refs[-3:]
    length = place.shape[1]
    me, mz = idx[0], idx[1]
    copies = [
        pltpu.make_async_copy(rows[k], stack.at[pl.ds(k * slots, slots)], sems.at[k])
        for k in range(members)
    ]
    for copy in copies:
        copy.start()
    for k in range(members):
        expert = mz * members + (me ^ k)
        pick[k * slots : (k + 1) * slots, :] = pick_rows(place[pl.ds(expert, 1), :], slots)
    for copy in copies:
        copy.wait()
    out = outs[0]
    result = dot_tn(pick[...], stack[...])
    out[0:length, :] = result.astype(out.dtype)
    if not graded:
        return
    slab = iota((16, length), 0)
    lines = jnp.zeros((16, length), F32)
    row = iota((slots, 128), 0)
    for k in range(members):
        head = stack[k * slots : (k + 1) * slots, 0:128].astype(F32)
        pieces = [
            jnp.sum(jnp.where(row == capacity + i, head, 0.0), axis=0, keepdims=True) for i in range(3)
        ]
        pieces = jnp.concatenate(pieces + [jnp.zeros((5, 128), F32)], axis=0).astype(BF16)
        line = jnp.sum(
            dot(pieces[:, 0:slots], pick[k * slots : (k + 1) * slots, :]), axis=0, keepdims=True
        )
        lines = lines + jnp.where(slab == (me ^ k), line, 0.0)
    if low:
        out[length : length + 16, :] = jnp.zeros((16, out.shape[1]), BF16)
        for i, value in enumerate(split3(lines)):
            out[length : length + 16, i * PART : i * PART + length] = value.astype(BF16)
    else:
        outs[1][...] = lines


def row_grad_body(count, slots, idx, *refs):
    pieces, blocks = refs[: count[0]], refs[count[0] : count[0] + count[1]]
    keep, away, a, b, sems = refs[count[0] + count[1] :]
    size = blocks[0].shape[0]
    pairs = [(p, a.at[pl.ds(i * slots, slots)]) for i, p in enumerate(pieces)]
    pairs += [(q, b.at[pl.ds(i * size, size)]) for i, q in enumerate(blocks)]
    copy_all(pairs, sems)
    md = idx[2]
    half = keep.shape[0]
    step = 256
    for n in range(0, half, step):
        other = pl.multiple_of((1 - md) * half + n, step)
        away[n : n + step, :] = dot_tn(a[:, pl.ds(other, step)], b[...]).astype(BF16)
    for n in range(0, half, step):
        this = pl.multiple_of(md * half + n, step)
        keep[n : n + step, :] = dot_tn(a[:, pl.ds(this, step)], b[...])


def col_grad_body(planes, members, slots, idx, *refs):
    blocks, arrays = refs[:planes], refs[planes:-5]
    keep, away, a, b, sems = refs[-5:]
    size = blocks[0].shape[0]
    pairs = [(q, a.at[pl.ds(i * size, size)]) for i, q in enumerate(blocks)]
    span = arrays[0].shape[0] // slots
    groups = len(arrays) // members
    for g in range(groups):
        for k in range(members):
            for i in range(span):
                at_row = ((g * span + i) * members + k) * slots
                pairs.append((arrays[g * members + k].at[pl.ds(i * slots, slots)], b.at[pl.ds(at_row, slots)]))
    copy_all(pairs, sems)
    md = idx[2]
    half = keep.shape[1]
    step = 256
    for n in range(0, keep.shape[0], step):
        lhs = a[:, n : n + step]
        other = pl.ds(pl.multiple_of((1 - md) * half, half), half)
        away[n : n + step, :] = dot_tn(lhs, b[:, other]).astype(BF16)
    for n in range(0, keep.shape[0], step):
        lhs = a[:, n : n + step]
        this = pl.ds(pl.multiple_of(md * half, half), half)
        keep[n : n + step, :] = dot_tn(lhs, b[:, this])


def down_body(planes, members, slots, idx, *refs):
    blocks, (da, db), outs = refs[:planes], refs[planes : planes + 2], refs[planes + 2 :]
    md = idx[2]
    half = da.shape[1]
    for j in range(planes):
        for part, w in ((md, da), (1 - md, db)):
            cols = pl.ds(pl.multiple_of(part * half, half), half)
            result = dot(blocks[j][...], w[...])
            for k in range(members):
                outs[k][j * slots : (j + 1) * slots, cols] = result[k * slots : (k + 1) * slots].astype(BF16)


def to_row(column):
    eye = iota((128, 128), 0) == iota((128, 128), 1)
    return jnp.concatenate(
        [
            jnp.sum(jnp.where(eye, column[i : i + 128], 0.0), axis=0, keepdims=True)
            for i in range(0, column.shape[0], 128)
        ],
        axis=1,
    )


def to_column(line):
    eye = iota((128, 128), 0) == iota((128, 128), 1)
    return jnp.sum(jnp.where(eye, line, 0.0), axis=1, keepdims=True)


def prepare_body(members, idx, wq, wk, wv, *outs):
    me, md = idx[0], idx[2]
    half = outs[0].shape[0]
    own = wq.shape[1] // members
    rows = pl.ds(pl.multiple_of(md * half, half), half)
    for k in range(1, members):
        cols = pl.ds(pl.multiple_of((me ^ k) * own, own), own)
        for i, w in enumerate((wq, wk, wv)):
            outs[k - 1][:, i * own : (i + 1) * own] = w[rows, cols]


def project_body(members, experts, idx, *refs):
    hs, sms = refs[:members], refs[members : 2 * members]
    refs = refs[2 * members :]
    ws, got, peer = refs[:3], refs[3 : 2 + members], refs[2 + members : 1 + 2 * members]
    q0, k0, v, a, w, squares, gain, sems = refs[1 + 2 * members :]
    me, md = idx[0], idx[2]
    length, total = hs[0].shape[0], a.shape[0]
    own = q0.shape[1]
    half = own // 2
    copies = []
    base = pl.multiple_of(me * own, own)
    for i in range(3):
        copies.append((ws[i].at[:, pl.ds(base, own)], w.at[pl.ds(base, own), i * own : (i + 1) * own]))
    for k in range(1, members):
        for side, source in ((md, got), (1 - md, peer)):
            row = pl.multiple_of((me ^ k) * own + side * half, half)
            copies.append((source[k - 1], w.at[pl.ds(row, half)]))
    copies = [pltpu.make_async_copy(s, d, sems.at[i]) for i, (s, d) in enumerate(copies)]
    for c in copies:
        c.start()
    for k in range(members):
        cols = pl.ds(pl.multiple_of((me ^ k) * own, own), own)
        gain[:, cols] = sms[k][experts : experts + 1, :].astype(F32)
    for k in range(members):
        h = hs[k][...].astype(F32)
        inv = lax.rsqrt(jnp.mean(h * h, axis=-1, keepdims=True) + EPSILON)
        rows = pl.ds(pl.multiple_of((me ^ k) * length, length), length)
        a[rows, :] = (h * inv * gain[...]).astype(BF16)
    for c in copies:
        c.wait()
    step = 256
    sums = [[], []]
    for n in range(0, total, step):
        rows = slice(n, n + step)
        for i, out in enumerate((q0, k0)):
            raw = dot(a[rows, :], w[:, i * own : (i + 1) * own])
            out[rows, :] = raw
            sums[i].append(jnp.sum(raw * raw, axis=1, keepdims=True))
        v[rows, :] = dot(a[rows, :], w[:, 2 * own :]).astype(BF16)
    lines = [to_row(jnp.concatenate(s, axis=0)) for s in sums]
    squares[...] = jnp.concatenate(lines + [jnp.zeros((6, total), F32)], axis=0)


def doc_start(lens, first, count):
    end0 = lens[0, 0]
    end1 = end0 + lens[0, 1]
    end2 = end1 + lens[0, 2]
    at_row = iota((count, 1), 0) + first
    later = jnp.where(at_row < end2, end1, at_row)
    start = jnp.where(at_row < end0, 0, jnp.where(at_row < end1, end0, later))
    return at_row, start


def inverse_rms(squares):
    total = squares[0][...]
    for s in squares[1:]:
        total = total + s[...]
    return lax.rsqrt(total / D + EPSILON)


def attend_body(members, scale, idx, lens, q0, k0, v, *refs):
    squares, (cosine, sine, gq, gk, wo) = refs[:members], refs[members : members + 5]
    refs = refs[members + 5 :]
    outs, (qr, kr, mixed, lse) = refs[:members], refs[members:]
    me = idx[0]
    total, own = q0.shape
    inv = inverse_rms(squares)
    for n in range(0, total, 128):
        rows = slice(n, n + 128)
        cos, sin = cosine[rows, :], sine[rows, :]
        for i, (raw, gain, out) in enumerate(((q0, gq, qr), (k0, gk, kr))):
            col = to_column(inv[i : i + 1, n : n + 128])
            for h in range(0, own, HD):
                x = raw[rows, h : h + HD] * col * gain[:, h : h + HD].astype(F32)
                out[rows, h : h + HD] = (x * cos + pltpu.roll(x, HD // 2, 1) * sin).astype(BF16)
    step = 256
    for n in range(0, total, step):
        rows = slice(n, n + step)
        at_row, start = doc_start(lens, n, step)
        at_key = iota((step, n + step), 1)
        allowed = (at_key <= at_row) & (at_key >= start)
        for h in range(0, own, HD):
            cols = slice(h, h + HD)
            s = dot_nt(qr[rows, cols], kr[0 : n + step, cols]) * scale
            s = jnp.where(allowed, s, NEG_FILL)
            top = jnp.max(s, axis=-1, keepdims=True)
            p = jnp.exp(s - top)
            norm = jnp.sum(p, axis=-1, keepdims=True)
            lse[rows, h // HD : h // HD + 1] = top + jnp.log(norm)
            p = (p * (1.0 / norm)).astype(BF16)
            mixed[rows, cols] = dot(p, v[0 : n + step, cols]).astype(BF16)
    length = outs[0].shape[0]
    for k in list(range(1, members)) + [0]:
        rows = pl.ds(pl.multiple_of((me ^ k) * length, length), length)
        outs[k][...] = dot(mixed[rows, :], wo[...]).astype(outs[k].dtype)


def place_pieces(members, row, idx, pieces, out):
    me = idx[0]
    own = pieces[0].shape[1]
    for k in range(members):
        cols = pl.ds(pl.multiple_of((me ^ k) * own, own), own)
        out[:, cols] = pieces[k][row, :].astype(out.dtype)


def route_body(members, experts, idx, hidden, own, *refs):
    got, sms = refs[: members - 1], refs[members - 1 : 2 * members - 1]
    h1, packed, route, router, gain = refs[2 * members - 1 :]
    place_pieces(members, slice(0, experts), idx, sms, router)
    place_pieces(members, slice(experts + 1, experts + 2), idx, sms, gain)
    length = hidden.shape[0]
    h = hidden[...].astype(F32) + own[...]
    for g in got:
        h = h + g[...].astype(F32)
    h1[...] = h
    inv = lax.rsqrt(jnp.mean(h * h, axis=-1, keepdims=True) + EPSILON)
    packed[0:length, :] = (h * inv * gain[...]).astype(BF16)
    logits = dot_nt(router[...], packed[0:length, :])
    e = jnp.exp(logits - jnp.max(logits, axis=0, keepdims=True))
    r = e / jnp.sum(e, axis=0, keepdims=True)
    route[...] = r
    packed[length:, :] = jnp.zeros((experts, packed.shape[1]), BF16)
    for i, value in enumerate(split3(r)):
        packed[length:, i * PART : i * PART + length] = value.astype(BF16)


def token_body(members, planes, experts, idx, own, lines, *refs):
    got, (route, h1, packed, grad_out) = refs[: planes - 1], refs[planes - 1 : planes + 3]
    sms = refs[planes + 3 : planes + 3 + members]
    grad, low, small, router, gain = refs[planes + 3 + members :]
    place_pieces(members, slice(0, experts), idx, sms, router)
    place_pieces(members, slice(experts + 1, experts + 2), idx, sms, gain)
    mz = idx[1]
    length = h1.shape[0]
    total = own[...]
    spread = iota((experts, length), 0)
    grad_route = jnp.zeros((experts, length), F32)
    for j in range(planes):
        if j == 0:
            part = lines[...]
        else:
            total = total + got[j - 1][0:length, :].astype(F32)
            part = sum(
                got[j - 1][length : length + 16, i * PART : i * PART + length].astype(F32) for i in range(3)
            )
        z = lax.rem(mz - j + planes, planes)
        for s in range(members):
            grad_route = grad_route + jnp.where(spread == z * members + s, part[s : s + 1], 0.0)
    r = route[...]
    dl = (r * (grad_route - jnp.sum(r * grad_route, axis=0, keepdims=True))).astype(BF16)
    total = total + dot_tn(dl, router[...])
    small[0:experts, :] = dot(dl, packed[0:length, :])
    h = h1[...]
    inv = lax.rsqrt(jnp.mean(h * h, axis=-1, keepdims=True) + EPSILON)
    unit = h * inv
    small[experts : experts + 8, :] = jnp.broadcast_to(
        jnp.sum(total * unit, axis=0, keepdims=True), (8, h.shape[1])
    )
    scaled = total * gain[...]
    back = (scaled - unit * jnp.mean(scaled * unit, axis=-1, keepdims=True)) * inv
    result = grad_out[...].astype(F32) + back
    grad[...] = result
    low[...] = result.astype(BF16)


def attend_back_body(members, scale, idx, lens, *refs):
    ds, squares = refs[:members], refs[members : 2 * members]
    wo, qr, kr, v, lse, q0, k0, cosine, sine, gq, gk = refs[2 * members : 2 * members + 11]
    grads, dv, sq, sk, dots, gains, do, dkt, dvt, sems = refs[2 * members + 11 :]
    me = idx[0]
    length = ds[0].shape[0]
    total, own = q0.shape
    pairs = []
    for k in range(members):
        rows = pl.ds(pl.multiple_of((me ^ k) * length, length), length)
        pairs.append((ds[k], grads.at[rows]))
    copy_all(pairs, sems)
    step = 256
    for n in range(0, total, step):
        do[n : n + step, :] = dot_nt(grads[n : n + step, :], wo[...]).astype(BF16)
    inv = inverse_rms(squares)
    dot_q, dot_k = [0.0] * (total // 128), [0.0] * (total // 128)
    gain_lines = []
    for h in range(0, own, HD):
        cols = slice(h, h + HD)
        for n in range(0, total, step):
            rows = slice(n, n + step)
            keys = slice(0, n + step)
            at_row, start = doc_start(lens, n, step)
            at_key = iota((step, n + step), 1)
            allowed = (at_key <= at_row) & (at_key >= start)
            s = dot_nt(qr[rows, cols], kr[keys, cols]) * scale
            p = jnp.exp(jnp.where(allowed, s - lse[rows, h // HD : h // HD + 1], NEG_FILL))
            dp = dot_nt(do[rows, cols], v[keys, cols])
            delta = jnp.sum(p * dp, axis=-1, keepdims=True)
            grad_s = (p * (dp - delta)).astype(BF16)
            part_v = dot_tn(p.astype(BF16), do[rows, cols])
            part_k = dot_tn(grad_s, qr[rows, cols])
            if n == 0:
                dkt[...] = jnp.zeros(dkt.shape, F32)
                dvt[...] = jnp.zeros(dvt.shape, F32)
            dvt[keys, :] = dvt[keys, :] + part_v
            dkt[keys, :] = dkt[keys, :] + part_k
            sq[rows, cols] = dot(grad_s, kr[keys, cols]) * scale
        dv[:, cols] = dvt[...].astype(BF16)
        gq_sum, gk_sum = jnp.zeros((1, HD), F32), jnp.zeros((1, HD), F32)
        for c in range(total // 128):
            rows = slice(c * 128, c * 128 + 128)
            cos, sin = cosine[rows, :], sine[rows, :]
            for i, raw in enumerate((q0, k0)):
                g = sq[rows, cols] if i == 0 else dkt[rows, :] * scale
                g = g * cos - pltpu.roll(g, HD // 2, 1) * sin
                unit = raw[rows, cols] * to_column(inv[i : i + 1, c * 128 : c * 128 + 128])
                line = jnp.sum(g * unit, axis=0, keepdims=True)
                scaled = g * (gq if i == 0 else gk)[:, cols].astype(F32)
                value = jnp.sum(scaled * unit, axis=1, keepdims=True)
                if i == 0:
                    gq_sum = gq_sum + line
                    sq[rows, cols] = scaled
                    dot_q[c] = dot_q[c] + value
                else:
                    gk_sum = gk_sum + line
                    sk[rows, cols] = scaled
                    dot_k[c] = dot_k[c] + value
        gain_lines.append(jnp.concatenate([gq_sum, gk_sum, jnp.zeros((6, HD), F32)], axis=0))
    gains[...] = jnp.concatenate(gain_lines, axis=1)
    lines = [to_row(jnp.concatenate(x, axis=0)) for x in (dot_q, dot_k)]
    dots[...] = jnp.concatenate(lines + [jnp.zeros((6, total), F32)], axis=0)


def project_back_body(members, planes, idx, sq, sk, dv, q0, k0, a, *refs):
    squares, dots = refs[:members], refs[members : 2 * members]
    d3, keep, away = refs[2 * members :]
    md = idx[2]
    total, own = q0.shape
    inv = inverse_rms(squares)
    mean = dots[0][...]
    for d in dots[1:]:
        mean = mean + d[...]
    mean = mean / D
    for c in range(0, total, 128):
        rows = slice(c, c + 128)
        for i, (scaled, raw) in enumerate(((sq, q0), (sk, k0))):
            col = to_column(inv[i : i + 1, c : c + 128])
            avg = to_column(mean[i : i + 1, c : c + 128])
            unit = raw[rows, :] * col
            d3[rows, i * own : (i + 1) * own] = ((scaled[rows, :] - unit * avg) * col).astype(BF16)
    d3[:, 2 * own :] = dv[...]
    half = own // 2
    for out, side in ((away, 1 - md), (keep, md)):
        for s in range(members):
            cols = pl.ds(pl.multiple_of(s * own + side * half, half), half)
            out[s * half : (s + 1) * half, :] = dot_tn(a[:, cols], d3[...]).astype(out.dtype)


def input_back_body(members, idx, d3, w, *outs):
    me = idx[0]
    length = outs[0].shape[0]
    for k in list(range(1, members)) + [0]:
        rows = pl.ds(pl.multiple_of((me ^ k) * length, length), length)
        outs[k][...] = dot_nt(d3[rows, :], w[...]).astype(outs[k].dtype)


def input_body(members, experts, idx, own, *refs):
    got, sms = refs[: members - 1], refs[members - 1 : 2 * members - 1]
    hidden, grad, out, line, gain = refs[2 * members - 1 :]
    place_pieces(members, slice(experts, experts + 1), idx, sms, gain)
    total = own[...]
    for g in got:
        total = total + g[...].astype(F32)
    h = hidden[...].astype(F32)
    inv = lax.rsqrt(jnp.mean(h * h, axis=-1, keepdims=True) + EPSILON)
    unit = h * inv
    line[...] = jnp.broadcast_to(jnp.sum(total * unit, axis=0, keepdims=True), line.shape)
    scaled = total * gain[...]
    out[...] = grad[...] + (scaled - unit * jnp.mean(scaled * unit, axis=-1, keepdims=True)) * inv


def output_grad_body(idx, mixed, grads, keep, away):
    md = idx[2]
    half = keep.shape[0]
    for out, side in ((away, 1 - md), (keep, md)):
        cols = pl.ds(pl.multiple_of(side * half, half), half)
        out[...] = dot_tn(mixed[:, cols], grads[...]).astype(out.dtype)


def split_body(planes, parts, idx, keep, peer, *outs):
    mz = idx[1]
    slab = keep.shape[0] // (parts * planes)
    for j in range(planes):
        z = lax.rem(mz + j, planes)
        for p in range(parts):
            rows = pl.ds(pl.multiple_of((p * planes + z) * slab, slab), slab)
            value = keep[rows, :] + peer[rows, :].astype(F32)
            outs[j][p * slab : (p + 1) * slab, :] = value.astype(outs[j].dtype)


def add_body(members, idx, *refs):
    values, outs = refs[: len(refs) - members], refs[len(refs) - members :]
    me = idx[0]
    slab = outs[0].shape[0]
    for k in range(members):
        rows = pl.ds(pl.multiple_of((me ^ k) * slab, slab), slab) if members > 1 else slice(0, slab)
        total = values[0][rows, :]
        for value in values[1:]:
            total = total + value[rows, :].astype(F32)
        outs[k][...] = total.astype(BF16)


def merge_body(members, idx, *refs):
    pieces, out = refs[:members], refs[members]
    me = idx[0]
    own = pieces[0].shape[1] // 3
    for k in range(members):
        for i in range(3):
            cols = pl.ds(pl.multiple_of(i * members * own + (me ^ k) * own, own), own)
            out[:, cols] = pieces[k][:, i * own : (i + 1) * own]


def spread_body(planes, idx, *refs):
    pieces, outs = refs[: 2 * planes], refs[2 * planes :]
    mz, md = idx[1], idx[2]
    slab = pieces[0].shape[0]
    width = outs[0].shape[1]
    for c in range(2):
        side = md if c == 0 else 1 - md
        for j in range(planes):
            row = side * (planes * slab) + lax.rem(mz + j, planes) * slab
            rows = pl.ds(pl.multiple_of(row, slab), slab)
            for i, out in enumerate(outs):
                out[rows, :] = pieces[c * planes + j][:, i * width : (i + 1) * width].astype(F32)


def shards(
    hidden_in,
    grad_out,
    doc_lengths,
    expert_ids,
    attn_gain,
    query_gain,
    key_gain,
    mlp_gain,
    w_query,
    w_key,
    w_value,
    w_output,
    w_router,
    w_gate,
    w_up,
    w_down,
):
    length = hidden_in.shape[0]
    members = lax.axis_size("shard")
    planes = lax.axis_size("expert")
    me = lax.axis_index("shard")
    mz = lax.axis_index("expert")
    md = lax.axis_index("dp")
    total = length * members
    experts = planes * members
    capacity = 5 * length * TOP // (4 * experts)
    own = D // members
    local_heads = HEADS // members
    scale = HD ** (-0.5)
    others = range(1, members)

    def swap(value, k):
        return lax.ppermute(value, "shard", [(i, i ^ k) for i in range(members)])

    def fetch_z(value, j):
        return lax.ppermute(value, "expert", [(i, (i - j) % planes) for i in range(planes)])

    def return_z(value, j):
        return lax.ppermute(value, "expert", [(i, (i + j) % planes) for i in range(planes)])

    def swap_dp(value):
        return lax.ppermute(value, "dp", [(0, 1), (1, 0)])

    def exchange(pieces):
        return [pieces[0]] + [swap(pieces[k], k) for k in others]

    def gather_plane(value):
        return exchange([value] * members)

    def gather_z(value):
        return [value] + [fetch_z(value, j) for j in range(1, planes)]

    idx = jnp.stack([me, mz, md]).astype(jnp.int32)
    half = own // 2
    slab = half // planes
    inner = w_gate.shape[2]
    slots = (capacity + 3 + 15) // 16 * 16
    rows = members * slots
    whole = planes * rows
    sms_rows = (experts + 2 + 15) // 16 * 16

    hidden_pieces = gather_plane(hidden_in)
    small = jnp.concatenate([w_router.T, attn_gain[None], mlp_gain[None]], axis=0)
    small = gather_plane(jnp.pad(small, ((0, sms_rows - experts - 2), (0, 0))))
    sent = call(
        functools.partial(prepare_body, members),
        (idx, w_query, w_key, w_value),
        "svvv",
        [((half, 3 * own), BF16)] * (members - 1),
        moved=9 * own * D,
    )
    got = [swap(sent[k - 1], k) for k in others]
    peers = [swap_dp(g) for g in got]

    doc_ids, doc_place = doc_layout(doc_lengths[0], total)
    cosine, sine = rope_tables(doc_place)
    sine = jnp.concatenate([-sine[:, : HD // 2], sine[:, HD // 2 :]], axis=1)
    gain_query, gain_key = query_gain[None], key_gain[None]

    hit = jnp.any(expert_ids[:, :, None] == jnp.arange(experts, dtype=jnp.int32), axis=1)
    before = jnp.triu(jnp.ones((length, length), BF16))
    rank = dot(hit.T.astype(BF16), before).astype(jnp.int32) - 1
    place_z = gather_z(jnp.where(hit.T, rank, -1))
    grads_z = gather_z(grad_out)

    gate_mine, up_mine, down_mine = w_gate[0], w_up[0], w_down[0]
    gate_peer, up_peer, down_peer = swap_dp(gate_mine), swap_dp(up_mine), swap_dp(down_mine)

    query_raw, key_raw, value_rows, attn_input, w_qkv, squares = call(
        functools.partial(project_body, members, experts),
        (idx, *hidden_pieces, *small, w_query, w_key, w_value, *got, *peers),
        "s" + "v" * (2 * members) + "a" * (1 + 2 * members),
        [
            ((total, own), F32),
            ((total, own), F32),
            ((total, own), BF16),
            ((total, D), BF16),
            ((D, 3 * own), BF16),
            ((8, total), F32),
        ],
        scratch=[pltpu.VMEM((1, D), F32), pltpu.SemaphoreType.DMA((1 + 2 * members,))],
        flops=6 * total * D * own,
    )
    squares = gather_plane(squares)
    result = call(
        functools.partial(attend_body, members, scale),
        (idx, doc_lengths, query_raw, key_raw, value_rows, *squares, cosine, sine, gain_query, gain_key, w_output),
        "ss" + "v" * (8 + members),
        [((length, D), F32)]
        + [((length, D), BF16)] * (members - 1)
        + [((total, own), BF16)] * 3
        + [((total, 128), F32)],
        flops=8 * total * total * own + 2 * total * own * D,
    )
    partial = exchange(result[:members])
    query_heads, key_heads, mixed, log_total = result[members:]
    residual, packed, route = call(
        functools.partial(route_body, members, experts),
        (idx, hidden_in, *partial, *small),
        "s" + "v" * (1 + 2 * members),
        [((length, D), F32), ((length + experts, D), BF16), ((experts, length), F32)],
        scratch=[pltpu.VMEM((experts, D), BF16), pltpu.VMEM((1, D), F32)],
    )

    def dispatch(source, j, gated, after=()):
        return call(
            functools.partial(dispatch_body, gated, members, capacity, slots),
            (idx, place_z[j], source),
            "svv",
            [((slots, D), BF16)] * members,
            flops=2 * members * slots * length * D,
            after=after,
        )

    input_z = gather_z(packed)
    grad_pieces, slot_pieces, blocks_gm, blocks_dz, blocks_du, back = [], [], [], [], [], []
    weights = (gate_mine, gate_peer, up_mine, up_peer, down_mine, down_peer)
    order = [squares[1:], [residual]]
    for j in range(planes):
        pieces = exchange(dispatch(input_z[j], j, True))
        slot_pieces += pieces
        after = order[j] if j < 2 else back[j - 2][1:2]
        grads = exchange(dispatch(grads_z[j], j, False, after))
        grad_pieces += grads
        result = call(
            functools.partial(expert_body, members, capacity, slots, 0),
            (idx, *pieces, *grads, *weights),
            "s" + "a" * (2 * members) + "v" * 6,
            [((slots, D), BF16)] * members + [((rows, inner), BF16)] * 3,
            scratch=[
                pltpu.VMEM((rows, D), BF16),
                pltpu.VMEM((rows, D), BF16),
                pltpu.SemaphoreType.DMA((2 * members,)),
            ],
            vmem=48,
            flops=10 * rows * D * inner,
        )
        back.append(exchange(result[:members]))
        blocks_gm.append(result[members])
        blocks_dz.append(result[members + 1])
        blocks_du.append(result[members + 2])

    def collect(pieces, j, graded):
        extra_rows = 16 if graded and j > 0 else 0
        outs = [((length + extra_rows, D), F32 if j == 0 else BF16)]
        if graded and j == 0:
            outs.append(((16, length), F32))
        return call(
            functools.partial(collect_body, graded, j > 0, members, capacity, slots),
            (idx, place_z[j], *pieces),
            "sv" + "a" * members,
            outs,
            scratch=[
                pltpu.VMEM((rows, D), BF16),
                pltpu.VMEM((rows, length), BF16),
                pltpu.SemaphoreType.DMA((members,)),
            ],
            flops=2 * rows * length * D,
        )

    sums = [collect(back[j], j, True) for j in range(planes)]
    returned = [return_z(sums[j][0], j) for j in range(1, planes)]
    grad_residual, grad_low, small_part = call(
        functools.partial(token_body, members, planes, experts),
        (idx, *sums[0], *returned, route, residual, packed, grad_out, *small),
        "s" + "v" * (2 + planes - 1 + 4 + members),
        [((length, D), F32), ((length, D), BF16), ((experts + 8, D), F32)],
        scratch=[pltpu.VMEM((experts, D), BF16), pltpu.VMEM((1, D), F32)],
    )
    grad_all = gather_plane(grad_low)

    expert_sum = residual
    for first, last, after in ((0, planes // 2, [s[0] for s in sums[1:]]), (planes // 2, planes, grad_all[1:])):
        span = last - first
        weighted = call(
            functools.partial(down_body, span, members, slots),
            (idx, *blocks_gm[first:last], down_mine, down_peer),
            "s" + "v" * (span + 2),
            [((span * slots, D), BF16)] * members,
            flops=2 * span * rows * D * inner,
            after=after,
        )
        weighted = exchange(weighted)
        for j in range(first, last):
            at_row = (j - first) * slots
            part = collect([w[at_row : at_row + slots] for w in weighted], j, False)[0]
            if j > 0:
                part = return_z(part, j).astype(F32)
            expert_sum = expert_sum + part
    block_out = expert_sum.astype(BF16)

    half_d = D // 2

    def row_grad(blocks):
        return call(
            functools.partial(row_grad_body, (len(slot_pieces), planes), slots),
            (idx, *slot_pieces, *blocks),
            "s" + "a" * (len(slot_pieces) + planes),
            [((half_d, inner), F32), ((half_d, inner), BF16)],
            scratch=[
                pltpu.VMEM((whole, D), BF16),
                pltpu.VMEM((whole, inner), BF16),
                pltpu.SemaphoreType.DMA((len(slot_pieces) + planes,)),
            ],
            vmem=48,
            flops=2 * whole * D * inner,
        )

    grad_gate, away = row_grad(blocks_dz)
    grad_gate = (grad_gate + swap_dp(away).astype(F32))[None]
    grad_up, away = row_grad(blocks_du)
    grad_up = (grad_up + swap_dp(away).astype(F32))[None]
    grad_down, away = call(
        functools.partial(col_grad_body, planes, members, slots),
        (idx, *blocks_gm, *grad_pieces),
        "s" + "a" * (planes + len(grad_pieces)),
        [((inner, half_d), F32), ((inner, half_d), BF16)],
        scratch=[
            pltpu.VMEM((whole, inner), BF16),
            pltpu.VMEM((whole, D), BF16),
            pltpu.SemaphoreType.DMA((planes + planes * members,)),
        ],
        vmem=48,
        flops=2 * whole * D * inner,
    )
    grad_down = (grad_down + swap_dp(away).astype(F32))[None]

    grads, grad_value, scaled_query, scaled_key, dots, grad_gains = call(
        functools.partial(attend_back_body, members, scale),
        (
            idx,
            doc_lengths,
            *grad_all,
            *squares,
            w_output,
            query_heads,
            key_heads,
            value_rows,
            log_total,
            query_raw,
            key_raw,
            cosine,
            sine,
            gain_query,
            gain_key,
        ),
        "ss" + "a" * members + "v" * (members + 11),
        [
            ((total, D), BF16),
            ((total, own), BF16),
            ((total, own), F32),
            ((total, own), F32),
            ((8, total), F32),
            ((8, own), F32),
        ],
        scratch=[
            pltpu.VMEM((total, own), BF16),
            pltpu.VMEM((total, HD), F32),
            pltpu.VMEM((total, HD), F32),
            pltpu.SemaphoreType.DMA((members,)),
        ],
        flops=20 * total * total * own // 2,
    )
    dots = gather_plane(dots)
    grad_raw, keep, away = call(
        functools.partial(project_back_body, members, planes),
        (idx, scaled_query, scaled_key, grad_value, query_raw, key_raw, attn_input, *squares, *dots),
        "s" + "v" * (6 + 2 * members),
        [((total, 3 * own), BF16), ((D // 2, 3 * own), F32), ((D // 2, 3 * own), BF16)],
        vmem=48,
        flops=6 * total * D * own,
    )

    def scatter_z(keep, away, parts, holders):
        height, width = keep.shape
        pieces = call(
            functools.partial(split_body, planes, parts),
            (idx, keep, swap_dp(away)),
            "svv",
            [((height // planes, width), F32)] + [((height // planes, width), BF16)] * (planes - 1),
        )
        pieces = [pieces[0]] + [return_z(pieces[j], j) for j in range(1, planes)]
        return call(
            functools.partial(add_body, holders),
            (idx, *pieces),
            "s" + "v" * planes,
            [((height // planes // holders, width), BF16)] * holders,
        )

    def spread_z(piece, count):
        pieces = gather_z(piece)
        pieces = pieces + [swap_dp(p) for p in pieces]
        return call(
            functools.partial(spread_body, planes),
            (idx, *pieces),
            "s" + "v" * (2 * planes),
            [((own, D), F32)] * count,
        )

    summed = exchange(scatter_z(keep, away, members, members))
    piece = call(
        functools.partial(merge_body, members),
        (idx, *summed),
        "s" + "v" * members,
        [((slab, 3 * D), BF16)],
    )[0]
    grad_query, grad_key, grad_value_w = spread_z(piece, 3)

    keep, away = call(
        output_grad_body,
        (idx, mixed, grads),
        "svv",
        [((half, D), F32), ((half, D), BF16)],
        flops=2 * total * own * D,
    )
    grad_output = spread_z(scatter_z(keep, away, 1, 1)[0], 1)[0]

    partial = call(
        functools.partial(input_back_body, members),
        (idx, grad_raw, w_qkv),
        "svv",
        [((length, D), F32)] + [((length, D), BF16)] * (members - 1),
        flops=6 * total * D * own,
    )
    partial = exchange(partial)
    grad_in, line = call(
        functools.partial(input_body, members, experts),
        (idx, *partial, *small, hidden_in, grad_residual),
        "s" + "v" * (2 * members + 2),
        [((length, D), F32), ((8, D), F32)],
        scratch=[pltpu.VMEM((1, D), F32)],
    )

    small_part = jnp.concatenate([small_part[: experts + 1], line[:1]], axis=0)
    small_pieces = small_part.reshape(experts + 2, members, own).transpose(1, 0, 2)
    small_sum = at(small_pieces, me)
    for k in others:
        small_sum = small_sum + swap(at(small_pieces, me ^ k), k)
    small_sum = jnp.concatenate([small_sum, grad_gains[:2]], axis=0)
    small_sum = small_sum + swap_dp(small_sum)
    stack = jnp.stack(gather_z(small_sum))
    small_total = at(stack, (0 - mz) % planes)
    for z in range(1, planes):
        small_total = small_total + at(stack, (z - mz) % planes)
    return (
        block_out,
        grad_in,
        small_total[experts + 1],
        small_total[experts + 2],
        small_total[experts + 3],
        small_total[experts],
        grad_query,
        grad_key,
        grad_value_w,
        grad_output,
        small_total[:experts].T,
        grad_gate,
        grad_up,
        grad_down,
    )


def solution(mesh):
    return jax.shard_map(
        shards,
        mesh=mesh,
        in_specs=(
            P(("dp", "expert", "shard"), None),
            P(("dp", "expert", "shard"), None),
            P(("dp", "expert"), None),
            P(("dp", "expert", "shard"), None),
            P("shard"),
            P("shard"),
            P("shard"),
            P("shard"),
            P("shard", None),
            P("shard", None),
            P("shard", None),
            P("shard", None),
            P("shard", None),
            P(("expert", "shard"), "dp", None),
            P(("expert", "shard"), "dp", None),
            P(("expert", "shard"), None, "dp"),
        ),
        out_specs=(
            P(("dp", "expert", "shard"), None),
            P(("dp", "expert", "shard"), None),
            P("shard"),
            P("shard"),
            P("shard"),
            P("shard"),
            P("shard", None),
            P("shard", None),
            P("shard", None),
            P("shard", None),
            P("shard", None),
            P(("expert", "shard"), "dp", None),
            P(("expert", "shard"), "dp", None),
            P(("expert", "shard"), None, "dp"),
        ),
        check_vma=False,
    )
```

time: 1260 us -> 1070 us (0.85)
  Pallas kernels: 0 us -> 260 us
  matrix products: 207 us -> 0.21 us
  other arithmetic: 131 us -> 17.4 us
  local copies, waits for them, and re-layouts: 145 us -> 60.8 us
  waiting for transfers between devices: 606 us -> 551 us
  starting transfers between devices: 153 us -> 175 us
    pallas_call x0 -> x42, Pallas kernels: none -> 260 us  [call(): pl.pallas_call(run, out_shape=[jax.ShapeDtypeStruct(shape, dtype) for sha...]
    dot_general x33 -> x0, matrix products: 148 us -> none  [the longest x14 59 us: dot_tn(): lax.dot_general(a, b, (((0,), (0,)), ((), ())), preferred_element_type=F32)]
    ppermute x15 -> x12, waiting for transfers between devices: 167 us -> 107 us  [return_z(): lax.ppermute(value, 'expert', [(i, (i + j) % planes) for i in range(plane...]
    dot_general x6 -> x1, matrix products: 50.6 us -> 0.21 us  [dot(): return jnp.dot(a, b, preferred_element_type=F32)]
    convert_element_type x15 -> x1, other arithmetic: 42.9 us -> 1.46 us  [shards(): block_out = expert_sum.astype(BF16)]
    another operation x31 -> x1, local copies, waits for them, and re-layouts: 33.4 us -> 0.13 us  [the longest x2 20.2 us: gather_back(): jnp.stack([jnp.where(md == 0, every, peer_side), jnp.where(md == 0, peer_...]
    another operation x52 -> x3, other arithmetic: 25.5 us -> 0.27 us  [the longest x10 8.55 us: dispatch(): return jnp.stack(received).reshape(planes * members * capacity, D)]
    ppermute x15 -> x12, starting transfers between devices: 17.9 us -> 39.4 us  [return_z(): lax.ppermute(value, 'expert', [(i, (i + j) % planes) for i in range(plane...]
  transfers between devices with their start and end apart: 132 -> 122, of which waited for: 52 -> 41; matrix products, arithmetic and copies ran while one was open for 32% -> 3% of each run, Pallas kernels for 0% -> 24%
where the time goes in v2:
time: 1070 us
  waiting for transfers between devices  551 us (51%)
  Pallas kernels  260 us (24%)
  starting transfers between devices  175 us (16%)
  local copies, waits for them, and re-layouts  60.8 us (6%)
  other arithmetic  17.4 us (2%)
    ppermute x72, waiting for transfers between devices, swap(): return lax.ppermute(value, 'shard', [(i, i ^ k) for i in range(members)])  287 us
    pallas_call x42, Pallas kernels, call(): pl.pallas_call(run, out_shape=[jax.ShapeDtypeStruct(shape, dtype) for sha...  260 us
    ppermute x18, waiting for transfers between devices, fetch_z(): lax.ppermute(value, 'expert', [(i, (i - j) % planes) for i in range(plane...  157 us
    ppermute x12, waiting for transfers between devices, return_z(): lax.ppermute(value, 'expert', [(i, (i + j) % planes) for i in range(plane...  107 us
    ppermute x72, starting transfers between devices, swap(): return lax.ppermute(value, 'shard', [(i, i ^ k) for i in range(members)])  79.4 us
    unnamed x297, local copies, waits for them, and re-layouts  50.3 us
    ppermute x12, starting transfers between devices, return_z(): lax.ppermute(value, 'expert', [(i, (i + j) % planes) for i in range(plane...  39.4 us
    ppermute x20, starting transfers between devices, swap_dp(): return lax.ppermute(value, 'dp', [(0, 1), (1, 0)])  28.6 us
  transfers between devices with their start and end apart: 122, of which 41 were waited for; matrix products, arithmetic and copies ran while one was open for 3% of the time, Pallas kernels for 24%

profile of v2, /device:TPU:9, one launch (start us, length us, event | category | flops | bytes accessed | tf_op | source)
XLA Modules:
  0.0 1067.9 jit_solution(16588214625441389089)
XLA Ops:
  12.9 41.9 %collective-permute-done.5.refs_8_.refs_9_.refs_13_ = bf16[32,512]{1,0:T(8,128)(2,1)S(1)} collective-permute-done((bf16[32,512]{1,0:T(8,128)(2,1)S(1)}, bf16[32,512]{1,0:T(8,128)(2,1)S(1)}, u32[]{:S(2)}, u32[]{:S(2)}) %collective-permute-start.5) | collective-permute-done | bytes 32800 | tf_op jit(solution)/shard_map/ppermute | solution.py:674
  81.6 10.2 shard_map.264
  97.2 10.3 shard_map.265
  115.2 12.4 %collective-permute-done.15.refs_3_ = bf16[192,2048]{1,0:T(8,128)(2,1)S(1)} collective-permute-done((bf16[192,2048]{1,0:T(8,128)(2,1)S(1)}, bf16[192,2048]{1,0:T(8,128)(2,1)S(1)}, u32[]{:S(2)}, u32[]{:S(2)}) %collective-permute-start.15) | collective-permute-done | bytes 786464 | tf_op jit(solution)/shard_map/ppermute | solution.py:674
  129.1 19.1 %collective-permute-done.16.refs_4_ = bf16[192,2048]{1,0:T(8,128)(2,1)S(1)} collective-permute-done((bf16[192,2048]{1,0:T(8,128)(2,1)S(1)}, bf16[192,2048]{1,0:T(8,128)(2,1)S(1)}, u32[]{:S(2)}, u32[]{:S(2)}) %collective-permute-start.16) | collective-permute-done | bytes 786464 | tf_op jit(solution)/shard_map/ppermute | solution.py:674
  153.2 11.0 %collective-permute-done.27.refs_1_ = s32[16,192]{1,0:T(8,128)S(1)} collective-permute-done((s32[16,192]{1,0:T(8,128)S(1)}, s32[16,192]{1,0:T(8,128)S(1)}, u32[]{:S(2)}, u32[]{:S(2)}) %collective-permute-start.27) | collective-permute-done | bytes 12320 | tf_op jit(solution)/shard_map/ppermute | solution.py:677
  196.2 11.2 %collective-permute-done.18.refs_2_ = bf16[128,2048]{1,0:T(8,128)(2,1)S(1)} collective-permute-done((bf16[128,2048]{1,0:T(8,128)(2,1)S(1)}, bf16[128,2048]{1,0:T(8,128)(2,1)S(1)}, u32[]{:S(2)}, u32[]{:S(2)}) %collective-permute-start.18) | collective-permute-done | bytes 524320 | tf_op jit(solution)/shard_map/ppermute | solution.py:674
  224.5 19.4 %shard_map.269 = (bf16[128,2048]{1,0:T(8,128)(2,1)S(1)}, bf16[128,2048]{1,0:T(8,128)(2,1)}, bf16[128,2048]{1,0:T(8,128)(2,1)}, bf16[128,2048]{1,0:T(8,128)(2,1)}...) custom-call(s32[3]{0:T(128)S(1)} %pad_add_fusion.refs_0_, ...), custom_call_target="tpu_custom_call" | custom-call | flops 10737418240 | tf_op jit(solution)/shard_map/pallas_call | solution.py:70
  261.1 19.5 %shard_map.272 = (bf16[128,2048]{1,0:T(8,128)(2,1)S(1)}, bf16[128,2048]{1,0:T(8,128)(2,1)S(1)}, bf16[128,2048]{1,0:T(8,128)(2,1)}, bf16[128,2048]{1,0:T(8,128)(2...) custom-call(s32[3]{0:T(128)S(1)} %pad_add_fusion.refs_0_, ...), custom_call_target="tpu_custom_call" | custom-call | flops 10737418240 | tf_op jit(solution)/shard_map/pallas_call | solution.py:70
  286.4 28.7 %collective-permute-done.53.refs_2_ = bf16[208,2048]{1,0:T(8,128)(2,1)S(1)} collective-permute-done((bf16[208,2048]{1,0:T(8,128)(2,1)S(1)}, bf16[208,2048]{1,0:T(8,128)(2,1)S(1)}, u32[]{:S(2)}, u32[]{:S(2)}) %collective-permute-start.53) | collective-permute-done | bytes 852000 | tf_op jit(solution)/shard_map/ppermute | solution.py:677
  337.6 9.9 collective-permute-done.54.refs_2_.refs_14_
  361.5 9.8 collective-permute-done.48.refs_8_.refs_16_
  372.1 19.7 %shard_map.276 = (bf16[128,2048]{1,0:T(8,128)(2,1)S(1)}, bf16[128,2048]{1,0:T(8,128)(2,1)}, bf16[128,2048]{1,0:T(8,128)(2,1)}, bf16[128,2048]{1,0:T(8,128)(2,1)}...) custom-call(s32[3]{0:T(128)S(1)} %pad_add_fusion.refs_0_, ...), custom_call_target="tpu_custom_call" | custom-call | flops 10737418240 | tf_op jit(solution)/shard_map/pallas_call | solution.py:70
  407.3 19.0 %shard_map.280 = (bf16[128,2048]{1,0:T(8,128)(2,1)S(1)}, bf16[128,2048]{1,0:T(8,128)(2,1)S(1)}, bf16[128,2048]{1,0:T(8,128)(2,1)S(1)}, bf16[128,2048]{1,0:T(8,12...) custom-call(s32[3]{0:T(128)S(1)} %pad_add_fusion.refs_0_, ...), custom_call_target="tpu_custom_call" | custom-call | flops 10737418240 | tf_op jit(solution)/shard_map/pallas_call | solution.py:70
  430.0 15.0 %collective-permute-done.50.refs_4_ = bf16[128,2048]{1,0:T(8,128)(2,1)S(1)} collective-permute-done((bf16[128,2048]{1,0:T(8,128)(2,1)}, bf16[128,2048]{1,0:T(8,128)(2,1)S(1)}, u32[]{:S(2)}, u32[]{:S(2)}) %collective-permute-start.50) | collective-permute-done | bytes 524320 | tf_op jit(solution)/shard_map/ppermute | solution.py:674
  453.0 15.2 %collective-permute-start.70 = (bf16[208,2048]{1,0:T(8,128)(2,1)}, bf16[208,2048]{1,0:T(8,128)(2,1)}, u32[]{:S(2)}, u32[]{:S(2)}) collective-permute-start(bf16[208,2048]{1,0:T(8,128)(2,1)} %shard_map.273.refs_5_), channel_id=1, source_target_pairs={{0,4},{4,8},{8,12},{12,0},{1,5},{5,9},{9,13},{13,1},{2,6},{6,10},{... | collective-permute-start | bytes 2555912 | tf_op jit(solution)/shard_map/ppermute | solution.py:680
  477.7 20.6 %collective-permute-start.72 = (bf16[208,2048]{1,0:T(8,128)(2,1)}, bf16[208,2048]{1,0:T(8,128)(2,1)}, u32[]{:S(2)}, u32[]{:S(2)}) collective-permute-start(bf16[208,2048]{1,0:T(8,128)(2,1)} %shard_map.281.refs_7_), channel_id=1, source_target_pairs={{0,12},{4,0},{8,4},{12,8},{1,13},{5,1},{9,5},{13,9},{2,14},{6,2},{... | collective-permute-start | bytes 2555912 | tf_op jit(solution)/shard_map/ppermute | solution.py:680
  510.4 15.0 %shard_map.303 = (f32[1024,1024]{1,0:T(8,128)}, bf16[1024,1024]{1,0:T(8,128)(2,1)}) custom-call(s32[3]{0:T(128)S(1)} %pad_add_fusion.refs_0_, bf16[128,2048]{1,0:T(8,128)(2,1)S(1)} %copy-done.113, bf16[128,2048]{1,0:T(8,128)(2,1)S(1)} %copy-done.52, bf16[128,2048]{1,0:T(8,128)(2,1)S(1)} %copy-done.55, bf16[128,2048]{1,0:T(8,128)(2,1)S(1)} %copy-done.58, ...), custom_call_target="tpu_custom_call" | custom-call | flops 8589934592 | tf_op jit(solution)/shard_map/pallas_call | solution.py:70
  526.3 22.7 %collective-permute-done.72.refs_5_ = bf16[208,2048]{1,0:T(8,128)(2,1)} collective-permute-done((bf16[208,2048]{1,0:T(8,128)(2,1)}, bf16[208,2048]{1,0:T(8,128)(2,1)}, u32[]{:S(2)}, u32[]{:S(2)}) %collective-permute-start.72) | collective-permute-done | bytes 852000 | tf_op jit(solution)/shard_map/ppermute | solution.py:680
  557.9 14.9 %shard_map.304 = (f32[1024,1024]{1,0:T(8,128)}, bf16[1024,1024]{1,0:T(8,128)(2,1)}) custom-call(s32[3]{0:T(128)S(1)} %pad_add_fusion.refs_0_, bf16[512,1024]{1,0:T(8,128)(2,1)} %get-tuple-element.166.refs_1_, bf16[512,1024]{1,0:T(8,128)(2,1)} %get-tuple-element.175.refs_2_, bf16[512,1024]{1,0:T(8,128)(2,1)} %get-tuple-element.209.refs_1_.refs_3_, ...), custom_call_target="tpu_custom_call" | custom-call | flops 8589934592 | tf_op jit(solution)/shard_map/pallas_call | solution.py:70
  573.0 16.6 %collective-permute-done.74.refs_6_.refs_4_ = bf16[192,2048]{1,0:T(8,128)(2,1)} collective-permute-done((bf16[192,2048]{1,0:T(8,128)(2,1)}, bf16[192,2048]{1,0:T(8,128)(2,1)}, u32[]{:S(2)}, u32[]{:S(2)}) %collective-permute-start.74) | collective-permute-done | bytes 786464 | tf_op jit(solution)/shard_map/ppermute | solution.py:674
  590.6 21.1 %shard_map.290 = (bf16[768,2048]{1,0:T(8,128)(2,1)}, bf16[768,512]{1,0:T(8,128)(2,1)S(1)}, f32[768,512]{1,0:T(8,128)S(1)}, f32[768,512]{1,0:T(8,128)S(1)}, f32[8,768]{1,0:T(8,128)S(1)}, /*index=5*/f32[8,512]{1,0:T(8,128)S(1)}) custom-call(s32[3]{0:T(128)S(1)} %pad_add_fusion.refs_0_, s32[1,4]{1,0:T(1,128)S(1)} %copy-done.41, ...), custom_call_target="tpu_custom_call" | custom-call | flops 3019898880 | tf_op jit(solution)/shard_map/pallas_call | solution.py:70
  629.6 11.9 %shard_map.291 = (bf16[768,1536]{1,0:T(8,128)(2,1)}, f32[1024,1536]{1,0:T(8,128)}, bf16[1024,1536]{1,0:T(8,128)(2,1)}) custom-call(s32[3]{0:T(128)S(1)} %pad_add_fusion.refs_0_, f32[768,512]{1,0:T(8,128)S(1)} %copy-done.44, f32[768,512]{1,0:T(8,128)S(1)} %copy-done.46, bf16[768,512]{1,0:T(8,128)(2,1)S(1)} %copy-done.50, f32[768,512]{1,0:T(8,128)S(1)} %copy-done.11, ...), custom_call_target="tpu_custom_call" | custom-call | flops 4831838208 | tf_op jit(solution)/shard_map/pallas_call | solution.py:70
  661.4 15.2 %shard_map.302 = (f32[1024,1024]{1,0:T(8,128)}, bf16[1024,1024]{1,0:T(8,128)(2,1)}) custom-call(s32[3]{0:T(128)S(1)} %pad_add_fusion.refs_0_, bf16[128,2048]{1,0:T(8,128)(2,1)S(1)} %copy-done.114, bf16[128,2048]{1,0:T(8,128)(2,1)S(1)} %copy-done.53, bf16[128,2048]{1,0:T(8,128)(2,1)S(1)} %copy-done.56, bf16[128,2048]{1,0:T(8,128)(2,1)S(1)} %copy-done.59, ...), custom_call_target="tpu_custom_call" | custom-call | flops 8589934592 | tf_op jit(solution)/shard_map/pallas_call | solution.py:70
  709.8 26.4 %collective-permute-done.65 = bf16[256,2048]{1,0:T(8,128)(2,1)} collective-permute-done((bf16[256,2048]{1,0:T(8,128)(2,1)}, bf16[256,2048]{1,0:T(8,128)(2,1)}, u32[]{:S(2)}, u32[]{:S(2)}) %collective-permute-start.65) | collective-permute-done | bytes 1048608 | tf_op jit(solution)/shard_map/ppermute | solution.py:674
  742.3 18.2 %collective-permute-done.87 = f32[18,512]{1,0:T(8,128)S(1)} collective-permute-done((f32[18,512]{1,0:T(8,128)S(1)}, f32[18,512]{1,0:T(8,128)S(1)}, u32[]{:S(2)}, u32[]{:S(2)}) %collective-permute-start.87) | collective-permute-done | bytes 36896 | tf_op jit(solution)/shard_map/ppermute | solution.py:674
  779.0 33.1 %collective-permute-done.77 = bf16[256,2048]{1,0:T(8,128)(2,1)} collective-permute-done((bf16[256,2048]{1,0:T(8,128)(2,1)}, bf16[256,2048]{1,0:T(8,128)(2,1)}, u32[]{:S(2)}, u32[]{:S(2)}) %collective-permute-start.77) | collective-permute-done | bytes 1048608 | tf_op jit(solution)/shard_map/ppermute | solution.py:674
  830.8 48.4 %collective-permute-done.96.refs_3_ = bf16[256,1536]{1,0:T(8,128)(2,1)S(1)} collective-permute-done((bf16[256,1536]{1,0:T(8,128)(2,1)S(1)}, bf16[256,1536]{1,0:T(8,128)(2,1)S(1)}, u32[]{:S(2)}, u32[]{:S(2)}) %collective-permute-start.96) | collective-permute-done | bytes 786464 | tf_op jit(solution)/shard_map/ppermute | solution.py:680
  882.3 22.4 %collective-permute-done.97.refs_4_ = bf16[256,1536]{1,0:T(8,128)(2,1)S(1)} collective-permute-done((bf16[256,1536]{1,0:T(8,128)(2,1)S(1)}, bf16[256,1536]{1,0:T(8,128)(2,1)S(1)}, u32[]{:S(2)}, u32[]{:S(2)}) %collective-permute-start.97) | collective-permute-done | bytes 786464 | tf_op jit(solution)/shard_map/ppermute | solution.py:680
  917.8 29.5 %collective-permute-done.114.refs_4_ = bf16[64,2048]{1,0:T(8,128)(2,1)S(1)} collective-permute-done((bf16[64,2048]{1,0:T(8,128)(2,1)S(1)}, bf16[64,2048]{1,0:T(8,128)(2,1)S(1)}, u32[]{:S(2)}, u32[]{:S(2)}) %collective-permute-start.114) | collective-permute-done | bytes 262176 | tf_op jit(solution)/shard_map/ppermute | solution.py:677
  960.3 23.5 %collective-permute-done.113.refs_3_ = bf16[64,2048]{1,0:T(8,128)(2,1)S(1)} collective-permute-done((bf16[64,2048]{1,0:T(8,128)(2,1)S(1)}, bf16[64,2048]{1,0:T(8,128)(2,1)S(1)}, u32[]{:S(2)}, u32[]{:S(2)}) %collective-permute-start.113) | collective-permute-done | bytes 262176 | tf_op jit(solution)/shard_map/ppermute | solution.py:677
  1004.7 47.4 %collective-permute-done.102.refs_3_ = bf16[64,6144]{1,0:T(8,128)(2,1)S(1)} collective-permute-done((bf16[64,6144]{1,0:T(8,128)(2,1)S(1)}, bf16[64,6144]{1,0:T(8,128)(2,1)S(1)}, u32[]{:S(2)}, u32[]{:S(2)}) %collective-permute-start.102) | collective-permute-done | bytes 786464 | tf_op jit(solution)/shard_map/ppermute | solution.py:677
  (595 shorter events, 405.9 us)
Async XLA Ops:
  0.6 60.9 %collective-permute-start.2 = (bf16[192,2048]{1,0:T(8,128)(2,1)}, bf16[192,2048]{1,0:T(8,128)(2,1)S(1)}, u32[]{:S(2)}, u32[]{:S(2)}) collective-permute-start(bf16[192,2048]{1,0:T(8,128)(2,1)} %refs_9_.5), channel_id=1, source_target_pairs={{0,3},{1,2},{2,1},{3,0},{4,7},{5,6},{6,5},{7,4},{8,11},{9,10},{10,... | collective-permute-start | bytes 2359304 | tf_op jit(solution)/shard_map/ppermute | solution.py:674
  9.6 53.2 %collective-permute-start.6 = (bf16[256,1536]{1,0:T(8,128)(2,1)}, bf16[256,1536]{1,0:T(8,128)(2,1)S(1)}, u32[]{:S(2)}, u32[]{:S(2)}) collective-permute-start(bf16[256,1536]{1,0:T(8,128)(2,1)} %get-tuple-element.145), channel_id=1, source_target_pairs={{0,1},{1,0},{2,3},{3,2},{4,5},{5,4},{6,7},{7,6},{8,9},{9,8},{10,11... | collective-permute-start | bytes 2359304 | tf_op jit(solution)/shard_map/ppermute | solution.py:674
  9.9 57.6 %collective-permute-start.7 = (bf16[256,1536]{1,0:T(8,128)(2,1)}, bf16[256,1536]{1,0:T(8,128)(2,1)}, u32[]{:S(2)}, u32[]{:S(2)}) collective-permute-start(bf16[256,1536]{1,0:T(8,128)(2,1)} %get-tuple-element.146), channel_id=1, source_target_pairs={{0,2},{1,3},{2,0},{3,1},{4,6},{5,7},{6,4},{7,5},{8,10},{9,11},{10,... | collective-permute-start | bytes 2359304 | tf_op jit(solution)/shard_map/ppermute | solution.py:674
  10.1 57.4 %collective-permute-start.8 = (bf16[256,1536]{1,0:T(8,128)(2,1)S(1)}, bf16[256,1536]{1,0:T(8,128)(2,1)}, u32[]{:S(2)}, u32[]{:S(2)}) collective-permute-start(bf16[256,1536]{1,0:T(8,128)(2,1)S(1)} %get-tuple-element.147), channel_id=1, source_target_pairs={{0,3},{1,2},{2,1},{3,0},{4,7},{5,6},{6,5},{7,4},{8,11},{9,10},{10,... | collective-permute-start | bytes 2359304 | tf_op jit(solution)/shard_map/ppermute | solution.py:674
  75.6 91.4 %collective-permute-start.24 = (bf16[1024,1024]{1,0:T(8,128)(2,1)}, bf16[1024,1024]{1,0:T(8,128)(2,1)}, u32[]{:S(2)}, u32[]{:S(2)}) collective-permute-start(bf16[1024,1024]{1,0:T(8,128)(2,1)} %bitcast.9.refs_9_), channel_id=1, source_target_pairs={{0,16},{16,0},{1,17},{17,1},{2,18},{18,2},{3,19},{19,3},{4,20},{20... | collective-permute-start | bytes 6291464 | tf_op jit(solution)/shard_map/ppermute | solution.py:683
  80.3 86.8 %collective-permute-start.25 = (bf16[1024,1024]{1,0:T(8,128)(2,1)}, bf16[1024,1024]{1,0:T(8,128)(2,1)}, u32[]{:S(2)}, u32[]{:S(2)}) collective-permute-start(bf16[1024,1024]{1,0:T(8,128)(2,1)} %bitcast.10.refs_11_), channel_id=1, source_target_pairs={{0,16},{16,0},{1,17},{17,1},{2,18},{18,2},{3,19},{19,3},{4,20},{20... | collective-permute-start | bytes 6291464 | tf_op jit(solution)/shard_map/ppermute | solution.py:683
  95.5 74.1 %collective-permute-start.26 = (bf16[1024,1024]{1,0:T(8,128)(2,1)}, bf16[1024,1024]{1,0:T(8,128)(2,1)}, u32[]{:S(2)}, u32[]{:S(2)}) collective-permute-start(bf16[1024,1024]{1,0:T(8,128)(2,1)} %bitcast.11.refs_13_.refs_3_), channel_id=1, source_target_pairs={{0,16},{16,0},{1,17},{17,1},{2,18},{18,2},{3,19},{19,3},{4,20},{20... | collective-permute-start | bytes 6291464 | tf_op jit(solution)/shard_map/ppermute | solution.py:683
  169.6 54.9 %collective-permute-start.40 = (bf16[208,2048]{1,0:T(8,128)(2,1)S(1)}, bf16[208,2048]{1,0:T(8,128)(2,1)S(1)}, u32[]{:S(2)}, u32[]{:S(2)}) collective-permute-start(bf16[208,2048]{1,0:T(8,128)(2,1)S(1)} %get-tuple-element.157.refs_2_.refs_8_), channel_id=1, source_target_pairs={{0,8},{4,12},{8,0},{12,4},{1,9},{5,13},{9,1},{13,5},{2,10},{6,14},... | collective-permute-start | bytes 2555912 | tf_op jit(solution)/shard_map/ppermute | solution.py:677
  196.2 51.7 %collective-permute-start.34 = (bf16[128,2048]{1,0:T(8,128)(2,1)}, bf16[128,2048]{1,0:T(8,128)(2,1)S(1)}, u32[]{:S(2)}, u32[]{:S(2)}) collective-permute-start(bf16[128,2048]{1,0:T(8,128)(2,1)} %get-tuple-element.173), channel_id=1, source_target_pairs={{0,2},{1,3},{2,0},{3,1},{4,6},{5,7},{6,4},{7,5},{8,10},{9,11},{10,... | collective-permute-start | bytes 1572872 | tf_op jit(solution)/shard_map/ppermute | solution.py:674
  251.9 71.7 %collective-permute-start.57 = (bf16[192,2048]{1,0:T(8,128)(2,1)S(1)}, bf16[192,2048]{1,0:T(8,128)(2,1)S(1)}, u32[]{:S(2)}, u32[]{:S(2)}) collective-permute-start(bf16[192,2048]{1,0:T(8,128)(2,1)S(1)} %copy-done.24), channel_id=1, source_target_pairs={{0,4},{4,8},{8,12},{12,0},{1,5},{5,9},{9,13},{13,1},{2,6},{6,10},{... | collective-permute-start | bytes 2359304 | tf_op jit(solution)/shard_map/ppermute | solution.py:677
  255.9 59.2 %collective-permute-start.53 = (bf16[208,2048]{1,0:T(8,128)(2,1)S(1)}, bf16[208,2048]{1,0:T(8,128)(2,1)S(1)}, u32[]{:S(2)}, u32[]{:S(2)}) collective-permute-start(bf16[208,2048]{1,0:T(8,128)(2,1)S(1)} %get-tuple-element.157.refs_2_.refs_8_), channel_id=1, source_target_pairs={{0,4},{4,8},{8,12},{12,0},{1,5},{5,9},{9,13},{13,1},{2,6},{6,10},{... | collective-permute-start | bytes 2555912 | tf_op jit(solution)/shard_map/ppermute | solution.py:677
  255.9 62.3 %collective-permute-start.45 = (bf16[128,2048]{1,0:T(8,128)(2,1)}, bf16[128,2048]{1,0:T(8,128)(2,1)S(1)}, u32[]{:S(2)}, u32[]{:S(2)}) collective-permute-start(bf16[128,2048]{1,0:T(8,128)(2,1)} %get-tuple-element.184), channel_id=1, source_target_pairs={{0,1},{1,0},{2,3},{3,2},{4,5},{5,4},{6,7},{7,6},{8,9},{9,8},{10,11... | collective-permute-start | bytes 1572872 | tf_op jit(solution)/shard_map/ppermute | solution.py:674
  337.6 54.2 %collective-permute-start.55 = (bf16[128,2048]{1,0:T(8,128)(2,1)}, bf16[128,2048]{1,0:T(8,128)(2,1)S(1)}, u32[]{:S(2)}, u32[]{:S(2)}) collective-permute-start(bf16[128,2048]{1,0:T(8,128)(2,1)} %get-tuple-element.195), channel_id=1, source_target_pairs={{0,2},{1,3},{2,0},{3,1},{4,6},{5,7},{6,4},{7,5},{8,10},{9,11},{10,... | collective-permute-start | bytes 1572872 | tf_op jit(solution)/shard_map/ppermute | solution.py:674
  445.0 53.2 %collective-permute-start.68 = (bf16[128,2048]{1,0:T(8,128)(2,1)}, bf16[128,2048]{1,0:T(8,128)(2,1)}, u32[]{:S(2)}, u32[]{:S(2)}) collective-permute-start(bf16[128,2048]{1,0:T(8,128)(2,1)} %get-tuple-element.212), channel_id=1, source_target_pairs={{0,2},{1,3},{2,0},{3,1},{4,6},{5,7},{6,4},{7,5},{8,10},{9,11},{10,... | collective-permute-start | bytes 1572872 | tf_op jit(solution)/shard_map/ppermute | solution.py:674
  447.0 51.3 %collective-permute-start.69 = (bf16[128,2048]{1,0:T(8,128)(2,1)}, bf16[128,2048]{1,0:T(8,128)(2,1)}, u32[]{:S(2)}, u32[]{:S(2)}) collective-permute-start(bf16[128,2048]{1,0:T(8,128)(2,1)} %get-tuple-element.213), channel_id=1, source_target_pairs={{0,3},{1,2},{2,1},{3,0},{4,7},{5,6},{6,5},{7,4},{8,11},{9,10},{10,... | collective-permute-start | bytes 1572872 | tf_op jit(solution)/shard_map/ppermute | solution.py:674
  453.0 73.3 %collective-permute-start.70 = (bf16[208,2048]{1,0:T(8,128)(2,1)}, bf16[208,2048]{1,0:T(8,128)(2,1)}, u32[]{:S(2)}, u32[]{:S(2)}) collective-permute-start(bf16[208,2048]{1,0:T(8,128)(2,1)} %shard_map.273.refs_5_), channel_id=1, source_target_pairs={{0,4},{4,8},{8,12},{12,0},{1,5},{5,9},{9,13},{13,1},{2,6},{6,10},{... | collective-permute-start | bytes 2555912 | tf_op jit(solution)/shard_map/ppermute | solution.py:680
  477.7 71.3 %collective-permute-start.72 = (bf16[208,2048]{1,0:T(8,128)(2,1)}, bf16[208,2048]{1,0:T(8,128)(2,1)}, u32[]{:S(2)}, u32[]{:S(2)}) collective-permute-start(bf16[208,2048]{1,0:T(8,128)(2,1)} %shard_map.281.refs_7_), channel_id=1, source_target_pairs={{0,12},{4,0},{8,4},{12,8},{1,13},{5,1},{9,5},{13,9},{2,14},{6,2},{... | collective-permute-start | bytes 2555912 | tf_op jit(solution)/shard_map/ppermute | solution.py:680
  525.4 213.9 %collective-permute-start.120 = (bf16[1024,1024]{1,0:T(8,128)(2,1)}, bf16[1024,1024]{1,0:T(8,128)(2,1)}, u32[]{:S(2)}, u32[]{:S(2)}) collective-permute-start(bf16[1024,1024]{1,0:T(8,128)(2,1)} %get-tuple-element.273), channel_id=1, source_target_pairs={{0,16},{16,0},{1,17},{17,1},{2,18},{18,2},{3,19},{19,3},{4,20},{20... | collective-permute-start | bytes 6291464 | tf_op jit(solution)/shard_map/ppermute | solution.py:683
  676.6 64.5 %collective-permute-start.119 = (bf16[1024,1024]{1,0:T(8,128)(2,1)}, bf16[1024,1024]{1,0:T(8,128)(2,1)}, u32[]{:S(2)}, u32[]{:S(2)}) collective-permute-start(bf16[1024,1024]{1,0:T(8,128)(2,1)} %get-tuple-element.267), channel_id=1, source_target_pairs={{0,16},{16,0},{1,17},{17,1},{2,18},{18,2},{3,19},{19,3},{4,20},{20... | collective-permute-start | bytes 6291464 | tf_op jit(solution)/shard_map/ppermute | solution.py:683
  679.4 95.9 %collective-permute-start.94 = (bf16[1024,1536]{1,0:T(8,128)(2,1)}, bf16[1024,1536]{1,0:T(8,128)(2,1)}, u32[]{:S(2)}, u32[]{:S(2)}) collective-permute-start(bf16[1024,1536]{1,0:T(8,128)(2,1)} %get-tuple-element.242), channel_id=1, source_target_pairs={{0,16},{16,0},{1,17},{17,1},{2,18},{18,2},{3,19},{19,3},{4,20},{20... | collective-permute-start | bytes 9437192 | tf_op jit(solution)/shard_map/ppermute | solution.py:683
  680.5 55.8 %collective-permute-start.65 = (bf16[256,2048]{1,0:T(8,128)(2,1)}, bf16[256,2048]{1,0:T(8,128)(2,1)}, u32[]{:S(2)}, u32[]{:S(2)}) collective-permute-start(bf16[256,2048]{1,0:T(8,128)(2,1)} %get-tuple-element.207), channel_id=1, source_target_pairs={{0,2},{1,3},{2,0},{3,1},{4,6},{5,7},{6,4},{7,5},{8,10},{9,11},{10,... | collective-permute-start | bytes 3145736 | tf_op jit(solution)/shard_map/ppermute | solution.py:674
  775.2 133.8 %collective-permute-start.121 = (bf16[1024,1024]{1,0:T(8,128)(2,1)}, bf16[1024,1024]{1,0:T(8,128)(2,1)}, u32[]{:S(2)}, u32[]{:S(2)}) collective-permute-start(bf16[1024,1024]{1,0:T(8,128)(2,1)} %get-tuple-element.275), channel_id=1, source_target_pairs={{0,16},{16,0},{1,17},{17,1},{2,18},{18,2},{3,19},{19,3},{4,20},{20... | collective-permute-start | bytes 6291464 | tf_op jit(solution)/shard_map/ppermute | solution.py:683
  813.6 65.6 %collective-permute-start.96 = (bf16[256,1536]{1,0:T(8,128)(2,1)S(1)}, bf16[256,1536]{1,0:T(8,128)(2,1)S(1)}, u32[]{:S(2)}, u32[]{:S(2)}) collective-permute-start(bf16[256,1536]{1,0:T(8,128)(2,1)S(1)} %get-tuple-element.245), channel_id=1, source_target_pairs={{0,8},{4,12},{8,0},{12,4},{1,9},{5,13},{9,1},{13,5},{2,10},{6,14},... | collective-permute-start | bytes 2359304 | tf_op jit(solution)/shard_map/ppermute | solution.py:680
  813.6 91.2 %collective-permute-start.97 = (bf16[256,1536]{1,0:T(8,128)(2,1)S(1)}, bf16[256,1536]{1,0:T(8,128)(2,1)S(1)}, u32[]{:S(2)}, u32[]{:S(2)}) collective-permute-start(bf16[256,1536]{1,0:T(8,128)(2,1)S(1)} %get-tuple-element.246), channel_id=1, source_target_pairs={{0,12},{4,0},{8,4},{12,8},{1,13},{5,1},{9,5},{13,9},{2,14},{6,2},{... | collective-permute-start | bytes 2359304 | tf_op jit(solution)/shard_map/ppermute | solution.py:680
  819.4 90.2 %collective-permute-start.67 = (bf16[192,2048]{1,0:T(8,128)(2,1)}, bf16[192,2048]{1,0:T(8,128)(2,1)S(1)}, u32[]{:S(2)}, u32[]{:S(2)}) collective-permute-start(bf16[192,2048]{1,0:T(8,128)(2,1)} %shard_map.284), channel_id=1, source_target_pairs={{0,4},{4,8},{8,12},{12,0},{1,5},{5,9},{9,13},{13,1},{2,6},{6,10},{... | collective-permute-start | bytes 2359304 | tf_op jit(solution)/shard_map/ppermute | solution.py:680
  829.6 81.0 %collective-permute-start.93 = (f32[20,512]{1,0:T(8,128)S(1)}, f32[20,512]{1,0:T(8,128)S(1)}, u32[]{:S(2)}, u32[]{:S(2)}) collective-permute-start(f32[20,512]{1,0:T(8,128)S(1)} %fusion.30), channel_id=1, source_target_pairs={{0,4},{4,8},{8,12},{12,0},{1,5},{5,9},{9,13},{13,1},{2,6},{6,10},{... | collective-permute-start | bytes 122888 | tf_op jit(solution)/shard_map/ppermute | solution.py:677
  909.0 75.4 %collective-permute-start.79 = (bf16[192,2048]{1,0:T(8,128)(2,1)S(1)}, bf16[192,2048]{1,0:T(8,128)(2,1)S(1)}, u32[]{:S(2)}, u32[]{:S(2)}) collective-permute-start(bf16[192,2048]{1,0:T(8,128)(2,1)S(1)} %shard_map.288), channel_id=1, source_target_pairs={{0,8},{4,12},{8,0},{12,4},{1,9},{5,13},{9,1},{13,5},{2,10},{6,14},... | collective-permute-start | bytes 2359304 | tf_op jit(solution)/shard_map/ppermute | solution.py:680
  960.1 99.9 %collective-permute-start.80 = (bf16[192,2048]{1,0:T(8,128)(2,1)S(1)}, bf16[192,2048]{1,0:T(8,128)(2,1)S(1)}, u32[]{:S(2)}, u32[]{:S(2)}) collective-permute-start(bf16[192,2048]{1,0:T(8,128)(2,1)S(1)} %shard_map.289), channel_id=1, source_target_pairs={{0,12},{4,0},{8,4},{12,8},{1,13},{5,1},{9,5},{13,9},{2,14},{6,2},{... | collective-permute-start | bytes 2359304 | tf_op jit(solution)/shard_map/ppermute | solution.py:680
  984.4 67.7 %collective-permute-start.102 = (bf16[64,6144]{1,0:T(8,128)(2,1)S(1)}, bf16[64,6144]{1,0:T(8,128)(2,1)S(1)}, u32[]{:S(2)}, u32[]{:S(2)}) collective-permute-start(bf16[64,6144]{1,0:T(8,128)(2,1)S(1)} %shard_map.296.refs_1_), channel_id=1, source_target_pairs={{0,8},{4,12},{8,0},{12,4},{1,9},{5,13},{9,1},{13,5},{2,10},{6,14},... | collective-permute-start | bytes 2359304 | tf_op jit(solution)/shard_map/ppermute | solution.py:677
  987.5 68.6 %collective-permute-start.101 = (bf16[64,6144]{1,0:T(8,128)(2,1)S(1)}, bf16[64,6144]{1,0:T(8,128)(2,1)S(1)}, u32[]{:S(2)}, u32[]{:S(2)}) collective-permute-start(bf16[64,6144]{1,0:T(8,128)(2,1)S(1)} %shard_map.296.refs_1_), channel_id=1, source_target_pairs={{0,12},{4,0},{8,4},{12,8},{1,13},{5,1},{9,5},{13,9},{2,14},{6,2},{... | collective-permute-start | bytes 2359304 | tf_op jit(solution)/shard_map/ppermute | solution.py:677
  995.7 65.8 %collective-permute-start.104 = (bf16[64,6144]{1,0:T(8,128)(2,1)S(1)}, bf16[64,6144]{1,0:T(8,128)(2,1)S(1)}, u32[]{:S(2)}, u32[]{:S(2)}) collective-permute-start(bf16[64,6144]{1,0:T(8,128)(2,1)S(1)} %shard_map.296.refs_1_), channel_id=1, source_target_pairs={{0,16},{16,0},{1,17},{17,1},{2,18},{18,2},{3,19},{19,3},{4,20},{20... | collective-permute-start | bytes 2359304 | tf_op jit(solution)/shard_map/ppermute | solution.py:683
  1003.5 57.9 %collective-permute-start.107 = (bf16[64,6144]{1,0:T(8,128)(2,1)S(1)}, bf16[64,6144]{1,0:T(8,128)(2,1)S(1)}, u32[]{:S(2)}, u32[]{:S(2)}) collective-permute-start(bf16[64,6144]{1,0:T(8,128)(2,1)S(1)} %collective-permute-done.103.refs_4_), channel_id=1, source_target_pairs={{0,16},{16,0},{1,17},{17,1},{2,18},{18,2},{3,19},{19,3},{4,20},{20... | collective-permute-start | bytes 2359304 | tf_op jit(solution)/shard_map/ppermute | solution.py:683
  (237 other events, 6089.9 us)

commit v3 on v2

--- a/solution.py
+++ b/solution.py
@@ -60,21 +60,31 @@
 MIB = 1024 * 1024
 
 
-def call(body, args, kinds, outs, scratch=(), vmem=40, flops=0, moved=0, after=()):
-    spaces = {"v": pltpu.VMEM, "s": pltpu.SMEM, "a": pl.ANY}
-    count = len(args)
+def call(body, args, kinds, outs, scratch=(), vmem=40, after=()):
+    spaces = {"v": pltpu.VMEM, "s": pltpu.SMEM, "a": pl.ANY, "d": pl.ANY}
+    count, moved = len(args), [i for i, kind in enumerate(kinds) if kind == "d"]
+    extra = [pltpu.VMEM(args[i].shape, args[i].dtype) for i in moved]
+    if moved:
+        extra.append(pltpu.SemaphoreType.DMA((len(moved),)))
 
     def run(*refs):
-        body(*refs[:count], *refs[count + len(after) :])
+        given, rest = list(refs[:count]), list(refs[count + len(after) :])
+        if moved:
+            held, sems = rest[-len(moved) - 1 : -1], rest[-1]
+            rest = rest[: -len(moved) - 1]
+            copy_all([(given[i], to) for i, to in zip(moved, held)], sems)
+            for i, to in zip(moved, held):
+                given[i] = to
+        body(*given, *rest)
 
     return pl.pallas_call(
         run,
         out_shape=[jax.ShapeDtypeStruct(shape, dtype) for shape, dtype in outs],
         in_specs=[pl.BlockSpec(memory_space=spaces[kind]) for kind in kinds + "a" * len(after)],
         out_specs=[pl.BlockSpec(memory_space=pltpu.VMEM) for _ in outs],
-        scratch_shapes=list(scratch),
+        scratch_shapes=[*scratch, *extra],
         compiler_params=pltpu.CompilerParams(vmem_limit_bytes=vmem * MIB),
-        cost_estimate=pl.CostEstimate(flops=flops, bytes_accessed=moved, transcendentals=0),
+        cost_estimate=pl.CostEstimate(flops=1000, bytes_accessed=1000, transcendentals=0),
     )(*args, *after)
 
 
@@ -98,64 +108,84 @@
 
 
 def pick_rows(place, slots):
-    return jnp.where(iota((slots, place.shape[1]), 0) == place, 1.0, 0.0).astype(BF16)
-
-
-def dispatch_body(gated, members, capacity, slots, idx, place, rows, *outs):
-    length = place.shape[1]
+    slot = iota((slots, place.shape[1]), 0).astype(F32)
+    return jnp.where(slot == place, 1.0, 0.0).astype(BF16)
+
+
+def dispatch_body(shifts, gated, members, planes, capacity, slots, idx, places, source, *refs):
+    outs, (rows, sems) = refs[:members], refs[members:]
+    experts, length = places.shape[1:]
     me, mz = idx[0], idx[1]
-    source = rows[0:length, :]
-    for k in range(members):
-        expert = mz * members + (me ^ k)
-        pick = pick_rows(place[pl.ds(expert, 1), :], slots)
-        result = dot(pick, source)
-        outs[k][...] = result.astype(BF16)
-        if gated:
-            experts = place.shape[0]
-            head = result[:, 0:128]
-            row = iota((slots, 128), 0)
-            for part in range(3):
-                table = rows[length : length + experts, part * PART : part * PART + length].astype(F32)
-                gate = jnp.sum(jnp.where(iota(table.shape, 0) == expert, table, 0.0), axis=0, keepdims=True)
-                gate = jnp.broadcast_to(gate, (8, length)).astype(BF16)
-                slot = dot_nt(gate, pick)[0:1, :]
-                if slots < 128:
-                    slot = jnp.concatenate([slot, jnp.zeros((1, 128 - slots), F32)], axis=1)
-                head = head + jnp.where(row == capacity + part, slot, 0.0)
-            outs[k][:, 0:128] = head.astype(BF16)
-
-
-def expert_body(members, capacity, slots, first, idx, *refs):
-    xs, cs = refs[:members], refs[members : 2 * members]
-    ga, gb, ua, ub, da, db = refs[2 * members : 2 * members + 6]
-    rest = refs[2 * members + 6 :]
-    ds, (gm, dz, du), (x, c, sems) = rest[:members], rest[members : members + 3], rest[members + 3 :]
-    pairs = [(xs[k], x.at[pl.ds(k * slots, slots)]) for k in range(members)]
-    pairs += [(cs[k].at[pl.ds(first, slots)], c.at[pl.ds(k * slots, slots)]) for k in range(members)]
+    copies = []
+    for n, shift in enumerate(shifts):
+        z = lax.rem(mz + shift, planes)
+        block = source.at[z] if len(source.shape) == 3 else source
+        copies.append(pltpu.make_async_copy(block, rows.at[n], sems.at[n]))
+    for copy in copies:
+        copy.start()
+    for n, shift in enumerate(shifts):
+        z = lax.rem(mz + shift, planes)
+        span = slice(n * slots, (n + 1) * slots)
+        copies[n].wait()
+        for k in range(members):
+            expert = mz * members + (me ^ k)
+            pick = pick_rows(places[z, pl.ds(expert, 1), :], slots)
+            result = dot(pick, rows[n, 0:length, :])
+            outs[k][span, :] = result.astype(BF16)
+            if gated:
+                head = result[:, 0:128]
+                row = iota((slots, 128), 0)
+                for part in range(3):
+                    table = rows[n, length : length + experts, part * PART : part * PART + length].astype(F32)
+                    gate = jnp.sum(jnp.where(iota(table.shape, 0) == expert, table, 0.0), axis=0, keepdims=True)
+                    gate = jnp.broadcast_to(gate, (8, length)).astype(BF16)
+                    slot = dot_nt(gate, pick)[0:1, :]
+                    if slots < 128:
+                        slot = jnp.concatenate([slot, jnp.zeros((1, 128 - slots), F32)], axis=1)
+                    head = head + jnp.where(row == capacity + part, slot, 0.0)
+                outs[k][span, 0:128] = head.astype(BF16)
+
+
+def expert_body(where, members, capacity, slots, idx, *refs):
+    groups = 1 + max(g for g, _ in where)
+    xs, cs = refs[:members], refs[members : members + groups * members]
+    refs = refs[members + groups * members :]
+    weights, rest = refs[:6], refs[6:]
+    ds, (gm, dz, du) = rest[:members], rest[members : members + 3]
+    x, c, wg, wu, wd, sems = rest[members + 3 :]
+    md = idx[2]
+    half = wd.shape[2]
+    pairs = []
+    pieces = [(i, k) for i in range(len(where)) for k in range(members)]
+    for n, (i, k) in enumerate(pieces):
+        g, first = where[i]
+        to = pl.ds(n * slots, slots)
+        pairs.append((xs[k].at[pl.ds(i * slots, slots)], x.at[to]))
+        pairs.append((cs[g * members + k].at[pl.ds(first, slots)], c.at[to]))
+    for n, side in ((0, md), (1, 1 - md)):
+        rows = pl.ds(pl.multiple_of(side * half, half), half)
+        pairs += [(weights[n], wg.at[rows]), (weights[2 + n], wu.at[rows])]
+        pairs.append((weights[4 + n], wd.at[side]))
     copy_all(pairs, sems)
-    md = idx[2]
-    half = ga.shape[0]
-    inner = ga.shape[1]
-    mine = pl.ds(pl.multiple_of(md * half, half), half)
-    peer = pl.ds(pl.multiple_of((1 - md) * half, half), half)
-    rows = members * slots
+    inner = wg.shape[1]
+    rows = len(pieces) * slots
     eye = iota((slots, 128), 0) == iota((slots, 128), 1)
     row = iota((slots, 128), 0)
     gates = []
-    for k in range(members):
-        part = x[k * slots : (k + 1) * slots, 0:128].astype(F32)
+    for n in range(len(pieces)):
+        part = x[n * slots : (n + 1) * slots, 0:128].astype(F32)
         line = jnp.sum(
             jnp.where((row >= capacity) & (row < capacity + 3), part, 0.0), axis=0, keepdims=True
         )
         gates.append(jnp.sum(jnp.where(eye, line, 0.0), axis=1, keepdims=True))
     gate = jnp.concatenate(gates, axis=0)
     gate_grad = jnp.zeros((rows, 1), F32)
-    step = 512
+    step = 256 if rows <= 1024 else 128
     for n in range(0, inner, step):
         cols = slice(n, n + step)
-        z = dot(x[:, mine], ga[:, cols]) + dot(x[:, peer], gb[:, cols])
-        u = dot(x[:, mine], ua[:, cols]) + dot(x[:, peer], ub[:, cols])
-        raw = dot_nt(c[:, mine], da[cols, :]) + dot_nt(c[:, peer], db[cols, :])
+        z = dot(x[...], wg[:, cols])
+        u = dot(x[...], wu[:, cols])
+        raw = dot_nt(c[:, 0:half], wd[0, cols, :]) + dot_nt(c[:, half:], wd[1, cols, :])
         sig = 1.0 / (1.0 + jnp.exp(-z))
         silu = z * sig
         middle = silu * u
@@ -166,34 +196,35 @@
         raw = raw * gate
         dz[:, cols] = (raw * u * sig * (1.0 + z * (1.0 - sig))).astype(BF16)
         du[:, cols] = (raw * silu).astype(BF16)
-    lines = []
-    for k in range(members):
-        col = gate_grad[k * slots : (k + 1) * slots]
-        lines.append(jnp.sum(jnp.where(eye, col, 0.0), axis=0, keepdims=True))
-    for part, (wg, wu) in ((mine, (ga, ua)), (peer, (gb, ub))):
-        result = dot_nt(dz[...], wg[...]) + dot_nt(du[...], wu[...])
-        for k in range(members):
-            ds[k][:, part] = result[k * slots : (k + 1) * slots].astype(BF16)
-    for k in range(members):
-        head = ds[k][:, 0:128].astype(F32)
-        for i, value in enumerate(split3(lines[k])):
-            head = head + jnp.where(row == capacity + i, value, 0.0)
-        ds[k][:, 0:128] = head.astype(BF16)
-
-
-def collect_body(graded, low, members, capacity, slots, idx, place, *refs):
+    for n in range(0, wg.shape[0], 2 * step):
+        cols = slice(n, n + 2 * step)
+        result = dot_nt(dz[...], wg[cols, :]) + dot_nt(du[...], wu[cols, :])
+        for m, (i, k) in enumerate(pieces):
+            ds[k][i * slots : (i + 1) * slots, cols] = result[m * slots : (m + 1) * slots].astype(BF16)
+    for m, (i, k) in enumerate(pieces):
+        span = slice(i * slots, (i + 1) * slots)
+        col = gate_grad[m * slots : (m + 1) * slots]
+        line = jnp.sum(jnp.where(eye, col, 0.0), axis=0, keepdims=True)
+        head = ds[k][span, 0:128].astype(F32)
+        for part, value in enumerate(split3(line)):
+            head = head + jnp.where(row == capacity + part, value, 0.0)
+        ds[k][span, 0:128] = head.astype(BF16)
+
+
+def collect_body(shift, first, graded, low, members, planes, capacity, slots, idx, places, *refs):
     rows, outs, (stack, pick, sems) = refs[:members], refs[members:-3], refs[-3:]
-    length = place.shape[1]
+    length = places.shape[2]
     me, mz = idx[0], idx[1]
+    z = lax.rem(mz + shift, planes)
     copies = [
-        pltpu.make_async_copy(rows[k], stack.at[pl.ds(k * slots, slots)], sems.at[k])
+        pltpu.make_async_copy(rows[k].at[pl.ds(first, slots)], stack.at[pl.ds(k * slots, slots)], sems.at[k])
         for k in range(members)
     ]
     for copy in copies:
         copy.start()
     for k in range(members):
         expert = mz * members + (me ^ k)
-        pick[k * slots : (k + 1) * slots, :] = pick_rows(place[pl.ds(expert, 1), :], slots)
+        pick[k * slots : (k + 1) * slots, :] = pick_rows(places[z, pl.ds(expert, 1), :], slots)
     for copy in copies:
         copy.wait()
     out = outs[0]
@@ -222,60 +253,60 @@
         outs[1][...] = lines
 
 
-def row_grad_body(count, slots, idx, *refs):
-    pieces, blocks = refs[: count[0]], refs[count[0] : count[0] + count[1]]
-    keep, away, a, b, sems = refs[count[0] + count[1] :]
-    size = blocks[0].shape[0]
-    pairs = [(p, a.at[pl.ds(i * slots, slots)]) for i, p in enumerate(pieces)]
-    pairs += [(q, b.at[pl.ds(i * size, size)]) for i, q in enumerate(blocks)]
-    copy_all(pairs, sems)
+def load_pieces(where, arrays, slots, out):
+    return [
+        (arrays[g].at[pl.ds(first, slots)], out.at[pl.ds(i * slots, slots)])
+        for i, (g, first) in enumerate(where)
+    ]
+
+
+def load_blocks(blocks, out):
+    pairs, first = [], 0
+    for block in blocks:
+        pairs.append((block, out.at[pl.ds(first, block.shape[0])]))
+        first += block.shape[0]
+    return pairs
+
+
+def row_grad_body(where, slots, idx, *refs):
+    count = 1 + max(g for g, _ in where)
+    pieces, blocks = refs[:count], refs[count:-5]
+    keep, away, a, b, sems = refs[-5:]
+    copy_all(load_pieces(where, pieces, slots, a) + load_blocks(blocks, b), sems)
     md = idx[2]
-    half = keep.shape[0]
-    step = 256
-    for n in range(0, half, step):
-        other = pl.multiple_of((1 - md) * half + n, step)
-        away[n : n + step, :] = dot_tn(a[:, pl.ds(other, step)], b[...]).astype(BF16)
-    for n in range(0, half, step):
-        this = pl.multiple_of(md * half + n, step)
-        keep[n : n + step, :] = dot_tn(a[:, pl.ds(this, step)], b[...])
-
-
-def col_grad_body(planes, members, slots, idx, *refs):
-    blocks, arrays = refs[:planes], refs[planes:-5]
-    keep, away, a, b, sems = refs[-5:]
-    size = blocks[0].shape[0]
-    pairs = [(q, a.at[pl.ds(i * size, size)]) for i, q in enumerate(blocks)]
-    span = arrays[0].shape[0] // slots
-    groups = len(arrays) // members
-    for g in range(groups):
-        for k in range(members):
-            for i in range(span):
-                at_row = ((g * span + i) * members + k) * slots
-                pairs.append((arrays[g * members + k].at[pl.ds(i * slots, slots)], b.at[pl.ds(at_row, slots)]))
-    copy_all(pairs, sems)
+    step, half = 256, keep.shape[0]
+    for out, side in ((away, 1 - md), (keep, md)):
+        for n in range(0, half, step):
+            cols = pl.ds(pl.multiple_of(side * half + n, step), step)
+            out[n : n + step, :] = dot_tn(a[:, cols], b[...]).astype(out.dtype)
+
+
+def col_grad_body(where, slots, idx, *refs):
+    count = 1 + max(g for g, _ in where)
+    pieces, blocks = refs[:count], refs[count:-5]
+    keep, away, b, a, sems = refs[-5:]
+    copy_all(load_pieces(where, pieces, slots, b) + load_blocks(blocks, a), sems)
     md = idx[2]
-    half = keep.shape[1]
-    step = 256
+    step, half = 256, keep.shape[1]
     for n in range(0, keep.shape[0], step):
         lhs = a[:, n : n + step]
-        other = pl.ds(pl.multiple_of((1 - md) * half, half), half)
-        away[n : n + step, :] = dot_tn(lhs, b[:, other]).astype(BF16)
-    for n in range(0, keep.shape[0], step):
-        lhs = a[:, n : n + step]
-        this = pl.ds(pl.multiple_of(md * half, half), half)
-        keep[n : n + step, :] = dot_tn(lhs, b[:, this])
-
-
-def down_body(planes, members, slots, idx, *refs):
-    blocks, (da, db), outs = refs[:planes], refs[planes : planes + 2], refs[planes + 2 :]
+        for out, side in ((away, 1 - md), (keep, md)):
+            cols = pl.ds(pl.multiple_of(side * half, half), half)
+            out[n : n + step, :] = dot_tn(lhs, b[:, cols]).astype(out.dtype)
+
+
+def down_body(where, members, slots, idx, *refs):
+    count = len(refs) - members - 2
+    blocks, (mine, peer), outs = refs[:count], refs[count : count + 2], refs[count + 2 :]
     md = idx[2]
-    half = da.shape[1]
-    for j in range(planes):
-        for part, w in ((md, da), (1 - md, db)):
-            cols = pl.ds(pl.multiple_of(part * half, half), half)
-            result = dot(blocks[j][...], w[...])
+    half = mine.shape[1]
+    rows = members * slots
+    for n, (g, first) in enumerate(where):
+        for w, side in ((mine, md), (peer, 1 - md)):
+            cols = pl.ds(pl.multiple_of(side * half, half), half)
+            result = dot(blocks[g][first : first + rows, :], w[...])
             for k in range(members):
-                outs[k][j * slots : (j + 1) * slots, cols] = result[k * slots : (k + 1) * slots].astype(BF16)
+                outs[k][n * slots : (n + 1) * slots, cols] = result[k * slots : (k + 1) * slots].astype(BF16)
 
 
 def to_row(column):
@@ -294,24 +325,25 @@
     return jnp.sum(jnp.where(eye, line, 0.0), axis=1, keepdims=True)
 
 
-def prepare_body(members, idx, wq, wk, wv, *outs):
+def prepare_body(choice, members, idx, wq, wk, wv, *outs):
     me, md = idx[0], idx[2]
     half = outs[0].shape[0]
     own = wq.shape[1] // members
     rows = pl.ds(pl.multiple_of(md * half, half), half)
-    for k in range(1, members):
+    for n, k in enumerate(choice):
         cols = pl.ds(pl.multiple_of((me ^ k) * own, own), own)
         for i, w in enumerate((wq, wk, wv)):
-            outs[k - 1][:, i * own : (i + 1) * own] = w[rows, cols]
+            outs[n][:, i * own : (i + 1) * own] = w[rows, cols]
 
 
 def project_body(members, experts, idx, *refs):
-    hs, sms = refs[:members], refs[members : 2 * members]
-    refs = refs[2 * members :]
+    hs = refs[:members]
+    refs = refs[members:]
     ws, got, peer = refs[:3], refs[3 : 2 + members], refs[2 + members : 1 + 2 * members]
     q0, k0, v, a, w, squares, gain, sems = refs[1 + 2 * members :]
     me, md = idx[0], idx[2]
-    length, total = hs[0].shape[0], a.shape[0]
+    total = a.shape[0]
+    length = total // members
     own = q0.shape[1]
     half = own // 2
     copies = []
@@ -325,11 +357,9 @@
     copies = [pltpu.make_async_copy(s, d, sems.at[i]) for i, (s, d) in enumerate(copies)]
     for c in copies:
         c.start()
+    place_gain(members, experts, length, 0, idx, hs, gain)
     for k in range(members):
-        cols = pl.ds(pl.multiple_of((me ^ k) * own, own), own)
-        gain[:, cols] = sms[k][experts : experts + 1, :].astype(F32)
-    for k in range(members):
-        h = hs[k][...].astype(F32)
+        h = hs[k][0:length, :].astype(F32)
         inv = lax.rsqrt(jnp.mean(h * h, axis=-1, keepdims=True) + EPSILON)
         rows = pl.ds(pl.multiple_of((me ^ k) * length, length), length)
         a[rows, :] = (h * inv * gain[...]).astype(BF16)
@@ -402,27 +432,40 @@
         outs[k][...] = dot(mixed[rows, :], wo[...]).astype(outs[k].dtype)
 
 
-def place_pieces(members, row, idx, pieces, out):
+def place_router(members, experts, length, idx, pieces, out):
     me = idx[0]
-    own = pieces[0].shape[1]
+    own = out.shape[1] // members
+    count = experts // members
     for k in range(members):
         cols = pl.ds(pl.multiple_of((me ^ k) * own, own), own)
-        out[:, cols] = pieces[k][row, :].astype(out.dtype)
+        for i in range(members):
+            part = pieces[k][length:, i * own : (i + 1) * own].astype(F32)
+            out[i * count : (i + 1) * count, cols] = part[0:count]
+
+
+def place_gain(members, experts, length, part, idx, pieces, out):
+    me = idx[0]
+    own = out.shape[1] // members
+    row = experts // members
+    for k in range(members):
+        cols = pl.ds(pl.multiple_of((me ^ k) * own, own), own)
+        value = pieces[k][length:, part * own : (part + 1) * own].astype(F32)
+        out[:, cols] = value[row : row + 1]
 
 
 def route_body(members, experts, idx, hidden, own, *refs):
     got, sms = refs[: members - 1], refs[members - 1 : 2 * members - 1]
     h1, packed, route, router, gain = refs[2 * members - 1 :]
-    place_pieces(members, slice(0, experts), idx, sms, router)
-    place_pieces(members, slice(experts + 1, experts + 2), idx, sms, gain)
     length = hidden.shape[0]
+    place_router(members, experts, length, idx, sms, router)
+    place_gain(members, experts, length, 1, idx, sms, gain)
     h = hidden[...].astype(F32) + own[...]
     for g in got:
         h = h + g[...].astype(F32)
     h1[...] = h
     inv = lax.rsqrt(jnp.mean(h * h, axis=-1, keepdims=True) + EPSILON)
     packed[0:length, :] = (h * inv * gain[...]).astype(BF16)
-    logits = dot_nt(router[...], packed[0:length, :])
+    logits = dot_nt(router[...].astype(BF16), packed[0:length, :])
     e = jnp.exp(logits - jnp.max(logits, axis=0, keepdims=True))
     r = e / jnp.sum(e, axis=0, keepdims=True)
     route[...] = r
@@ -435,10 +478,10 @@
     got, (route, h1, packed, grad_out) = refs[: planes - 1], refs[planes - 1 : planes + 3]
     sms = refs[planes + 3 : planes + 3 + members]
     grad, low, small, router, gain = refs[planes + 3 + members :]
-    place_pieces(members, slice(0, experts), idx, sms, router)
-    place_pieces(members, slice(experts + 1, experts + 2), idx, sms, gain)
     mz = idx[1]
     length = h1.shape[0]
+    place_router(members, experts, length, idx, sms, router)
+    place_gain(members, experts, length, 1, idx, sms, gain)
     total = own[...]
     spread = iota((experts, length), 0)
     grad_route = jnp.zeros((experts, length), F32)
@@ -455,7 +498,7 @@
             grad_route = grad_route + jnp.where(spread == z * members + s, part[s : s + 1], 0.0)
     r = route[...]
     dl = (r * (grad_route - jnp.sum(r * grad_route, axis=0, keepdims=True))).astype(BF16)
-    total = total + dot_tn(dl, router[...])
+    total = total + dot_tn(dl, router[...].astype(BF16))
     small[0:experts, :] = dot(dl, packed[0:length, :])
     h = h1[...]
     inv = lax.rsqrt(jnp.mean(h * h, axis=-1, keepdims=True) + EPSILON)
@@ -473,7 +516,7 @@
 def attend_back_body(members, scale, idx, lens, *refs):
     ds, squares = refs[:members], refs[members : 2 * members]
     wo, qr, kr, v, lse, q0, k0, cosine, sine, gq, gk = refs[2 * members : 2 * members + 11]
-    grads, dv, sq, sk, dots, gains, do, dkt, dvt, sems = refs[2 * members + 11 :]
+    dv, sq, sk, dots, gains, grads, do, dkt, dvt, sems = refs[2 * members + 11 :]
     me = idx[0]
     length = ds[0].shape[0]
     total, own = q0.shape
@@ -571,7 +614,7 @@
 def input_body(members, experts, idx, own, *refs):
     got, sms = refs[: members - 1], refs[members - 1 : 2 * members - 1]
     hidden, grad, out, line, gain = refs[2 * members - 1 :]
-    place_pieces(members, slice(experts, experts + 1), idx, sms, gain)
+    place_gain(members, experts, hidden.shape[0], 0, idx, sms, gain)
     total = own[...]
     for g in got:
         total = total + g[...].astype(F32)
@@ -583,9 +626,15 @@
     out[...] = grad[...] + (scaled - unit * jnp.mean(scaled * unit, axis=-1, keepdims=True)) * inv
 
 
-def output_grad_body(idx, mixed, grads, keep, away):
-    md = idx[2]
-    half = keep.shape[0]
+def output_grad_body(members, idx, mixed, *refs):
+    pieces, (keep, away, grads, sems) = refs[:members], refs[members:]
+    me, md = idx[0], idx[2]
+    length, half = pieces[0].shape[0], keep.shape[0]
+    pairs = []
+    for k in range(members):
+        rows = pl.ds(pl.multiple_of((me ^ k) * length, length), length)
+        pairs.append((pieces[k], grads.at[rows]))
+    copy_all(pairs, sems)
     for out, side in ((away, 1 - md), (keep, md)):
         cols = pl.ds(pl.multiple_of(side * half, half), half)
         out[...] = dot_tn(mixed[:, cols], grads[...]).astype(out.dtype)
@@ -685,6 +734,9 @@
     def exchange(pieces):
         return [pieces[0]] + [swap(pieces[k], k) for k in others]
 
+    def gate(values, others):
+        return list(lax.optimization_barrier((*values, *others))[: len(values)])
+
     def gather_plane(value):
         return exchange([value] * members)
 
@@ -698,18 +750,25 @@
     slots = (capacity + 3 + 15) // 16 * 16
     rows = members * slots
     whole = planes * rows
-    sms_rows = (experts + 2 + 15) // 16 * 16
-
-    hidden_pieces = gather_plane(hidden_in)
-    small = jnp.concatenate([w_router.T, attn_gain[None], mlp_gain[None]], axis=0)
-    small = gather_plane(jnp.pad(small, ((0, sms_rows - experts - 2), (0, 0))))
-    sent = call(
-        functools.partial(prepare_body, members),
-        (idx, w_query, w_key, w_value),
-        "svvv",
-        [((half, 3 * own), BF16)] * (members - 1),
-        moved=9 * own * D,
-    )
+
+    router_rows = experts // members
+    extra = w_router.T.reshape(members, router_rows, own).transpose(1, 0, 2).reshape(router_rows, D)
+    gains = jnp.concatenate([attn_gain, mlp_gain, jnp.zeros((D - 2 * own,), BF16)])[None]
+    extra = jnp.concatenate([extra, gains], axis=0)
+    extra = jnp.pad(extra, ((0, -extra.shape[0] % 16), (0, 0)))
+    small = gather_plane(jnp.concatenate([hidden_in, extra], axis=0))
+
+    def prepare(choice, after=()):
+        return call(
+            functools.partial(prepare_body, choice, members),
+            (idx, w_query, w_key, w_value),
+            "svvv",
+            [((half, 3 * own), BF16)] * len(choice),
+            after=after,
+        )
+
+    last = members - 1
+    sent = prepare(range(1, last)) + prepare([last], small[1:2])
     got = [swap(sent[k - 1], k) for k in others]
     peers = [swap_dp(g) for g in got]
 
@@ -720,17 +779,15 @@
 
     hit = jnp.any(expert_ids[:, :, None] == jnp.arange(experts, dtype=jnp.int32), axis=1)
     before = jnp.triu(jnp.ones((length, length), BF16))
-    rank = dot(hit.T.astype(BF16), before).astype(jnp.int32) - 1
-    place_z = gather_z(jnp.where(hit.T, rank, -1))
-    grads_z = gather_z(grad_out)
-
-    gate_mine, up_mine, down_mine = w_gate[0], w_up[0], w_down[0]
-    gate_peer, up_peer, down_peer = swap_dp(gate_mine), swap_dp(up_mine), swap_dp(down_mine)
+    rank = dot(hit.T.astype(BF16), before) - 1.0
+    place = jnp.pad(jnp.where(hit.T, rank, -1.0).astype(BF16), ((0, 0), (0, D - length)))
+    grads_z = lax.all_gather(jnp.concatenate([grad_out, place], axis=0), "expert")
+    places = grads_z[:, length:, :length].astype(F32)
 
     query_raw, key_raw, value_rows, attn_input, w_qkv, squares = call(
         functools.partial(project_body, members, experts),
-        (idx, *hidden_pieces, *small, w_query, w_key, w_value, *got, *peers),
-        "s" + "v" * (2 * members) + "a" * (1 + 2 * members),
+        (idx, *small, w_query, w_key, w_value, *got, *peers),
+        "s" + "v" * members + "a" * (1 + 2 * members),
         [
             ((total, own), F32),
             ((total, own), F32),
@@ -740,75 +797,94 @@
             ((8, total), F32),
         ],
         scratch=[pltpu.VMEM((1, D), F32), pltpu.SemaphoreType.DMA((1 + 2 * members,))],
-        flops=6 * total * D * own,
+        after=[cosine, sine, places],
     )
     squares = gather_plane(squares)
+
+    def dispatch(source, blocks, gated, after=()):
+        return call(
+            functools.partial(dispatch_body, blocks, gated, members, planes, capacity, slots),
+            (idx, places, source),
+            "sva",
+            [((len(blocks) * slots, D), BF16)] * members,
+            scratch=[
+                pltpu.VMEM((len(blocks), length + experts, D), BF16),
+                pltpu.SemaphoreType.DMA((len(blocks),)),
+            ],
+            after=after,
+        )
+
+    first_sent = dispatch(grads_z, [0], False, [value_rows])
+    first_grads = exchange(gate(first_sent, squares[1:]))
+    weights = [w_gate[0], w_up[0], w_down[0]]
+    weights = [w for pair in zip(weights, map(swap_dp, gate(weights, squares[1:]))) for w in pair]
     result = call(
         functools.partial(attend_body, members, scale),
         (idx, doc_lengths, query_raw, key_raw, value_rows, *squares, cosine, sine, gain_query, gain_key, w_output),
-        "ss" + "v" * (8 + members),
+        "ss" + "d" * (8 + members),
         [((length, D), F32)]
         + [((length, D), BF16)] * (members - 1)
         + [((total, own), BF16)] * 3
         + [((total, 128), F32)],
-        flops=8 * total * total * own + 2 * total * own * D,
-    )
-    partial = exchange(result[:members])
+        after=first_sent[:1],
+    )
+    partial = exchange(gate(result[:members], first_grads[1:]))
     query_heads, key_heads, mixed, log_total = result[members:]
     residual, packed, route = call(
         functools.partial(route_body, members, experts),
         (idx, hidden_in, *partial, *small),
         "s" + "v" * (1 + 2 * members),
         [((length, D), F32), ((length + experts, D), BF16), ((experts, length), F32)],
-        scratch=[pltpu.VMEM((experts, D), BF16), pltpu.VMEM((1, D), F32)],
-    )
-
-    def dispatch(source, j, gated, after=()):
-        return call(
-            functools.partial(dispatch_body, gated, members, capacity, slots),
-            (idx, place_z[j], source),
-            "svv",
-            [((slots, D), BF16)] * members,
-            flops=2 * members * slots * length * D,
+        scratch=[pltpu.VMEM((experts, D), F32), pltpu.VMEM((1, D), F32)],
+        after=weights[1::2],
+    )
+
+    input_z = lax.all_gather(packed, "expert")
+    turns = list(range(1, planes)) + [0]
+    chunks = [turns[: planes // 2], turns[planes // 2 :]]
+    spot = {j: (c, i) for c, chunk in enumerate(chunks) for i, j in enumerate(chunk)}
+    other_grads = exchange(dispatch(grads_z, turns[:-1], False, [residual]))
+    grad_rows = first_grads + other_grads
+    grad_spot = {j: (1, (j - 1) * slots) if j else (0, 0) for j in turns}
+    slot_rows, arrived, after = [], other_grads[1:], ()
+    for chunk in chunks:
+        sent = dispatch(input_z, chunk, True, after)
+        after = sent[:1]
+        slot_rows.append(exchange(gate(sent, arrived)))
+        arrived = slot_rows[-1][1:]
+    blocks_gm, blocks_dz, blocks_du, back = [], [], [], []
+    after = ()
+    for c, chunk in enumerate(chunks):
+        size = len(chunk) * rows
+        result = call(
+            functools.partial(expert_body, [grad_spot[j] for j in chunk], members, capacity, slots),
+            (idx, *slot_rows[c], *grad_rows, *weights),
+            "s" + "a" * (3 * members + 6),
+            [((len(chunk) * slots, D), BF16)] * members + [((size, inner), BF16)] * 3,
+            scratch=[
+                pltpu.VMEM((size, D), BF16),
+                pltpu.VMEM((size, D), BF16),
+                pltpu.VMEM((D, inner), BF16),
+                pltpu.VMEM((D, inner), BF16),
+                pltpu.VMEM((2, inner, D // 2), BF16),
+                pltpu.SemaphoreType.DMA((2 * members * len(chunk) + 6,)),
+            ],
+            vmem=58,
             after=after,
         )
-
-    input_z = gather_z(packed)
-    grad_pieces, slot_pieces, blocks_gm, blocks_dz, blocks_du, back = [], [], [], [], [], []
-    weights = (gate_mine, gate_peer, up_mine, up_peer, down_mine, down_peer)
-    order = [squares[1:], [residual]]
-    for j in range(planes):
-        pieces = exchange(dispatch(input_z[j], j, True))
-        slot_pieces += pieces
-        after = order[j] if j < 2 else back[j - 2][1:2]
-        grads = exchange(dispatch(grads_z[j], j, False, after))
-        grad_pieces += grads
-        result = call(
-            functools.partial(expert_body, members, capacity, slots, 0),
-            (idx, *pieces, *grads, *weights),
-            "s" + "a" * (2 * members) + "v" * 6,
-            [((slots, D), BF16)] * members + [((rows, inner), BF16)] * 3,
-            scratch=[
-                pltpu.VMEM((rows, D), BF16),
-                pltpu.VMEM((rows, D), BF16),
-                pltpu.SemaphoreType.DMA((2 * members,)),
-            ],
-            vmem=48,
-            flops=10 * rows * D * inner,
-        )
-        back.append(exchange(result[:members]))
-        blocks_gm.append(result[members])
-        blocks_dz.append(result[members + 1])
-        blocks_du.append(result[members + 2])
-
-    def collect(pieces, j, graded):
-        extra_rows = 16 if graded and j > 0 else 0
-        outs = [((length + extra_rows, D), F32 if j == 0 else BF16)]
+        after = result[:1]
+        back.append(exchange(gate(result[:members], arrived)))
+        arrived = back[-1][1:]
+        for blocks, block in zip((blocks_gm, blocks_dz, blocks_du), result[members:]):
+            blocks.append(block)
+
+    def collect(j, pieces, first, graded, after=()):
+        outs = [((length + (16 if graded and j > 0 else 0), D), F32 if j == 0 else BF16)]
         if graded and j == 0:
             outs.append(((16, length), F32))
         return call(
-            functools.partial(collect_body, graded, j > 0, members, capacity, slots),
-            (idx, place_z[j], *pieces),
+            functools.partial(collect_body, j, first, graded, j > 0, members, planes, capacity, slots),
+            (idx, places, *pieces),
             "sv" + "a" * members,
             outs,
             scratch=[
@@ -816,77 +892,118 @@
                 pltpu.VMEM((rows, length), BF16),
                 pltpu.SemaphoreType.DMA((members,)),
             ],
-            flops=2 * rows * length * D,
+            after=after,
         )
 
-    sums = [collect(back[j], j, True) for j in range(planes)]
+    order = [(j, k) for j in turns for k in range(members)]
+    row_spot = [(spot[j][0] * members + k, spot[j][1] * slots) for j, k in order]
+    grads_spot = [(grad_spot[j][0] * members + k, grad_spot[j][1]) for j, k in order]
+
+    def weight_grad(body, where, pieces, blocks, shape, after):
+        return call(
+            functools.partial(body, where, slots),
+            (idx, *pieces, *blocks),
+            "s" + "a" * (len(pieces) + len(blocks)),
+            [(shape, F32), (shape, BF16)],
+            scratch=[
+                pltpu.VMEM((whole, D), BF16),
+                pltpu.VMEM((whole, inner), BF16),
+                pltpu.SemaphoreType.DMA((len(where) + len(blocks),)),
+            ],
+            vmem=48,
+            after=after,
+        )
+
+    def outputs(blocks, after):
+        return call(
+            functools.partial(down_body, [(spot[j][0], spot[j][1] * rows) for j in blocks], members, slots),
+            (idx, *blocks_gm, *weights[4:]),
+            "s" + "v" * 4,
+            [((len(blocks) * slots, D), BF16)] * members,
+            after=after,
+        )
+
+    all_rows = [piece for pieces in slot_rows for piece in pieces]
+    quarter = planes // 4
+    out_chunks = [turns[:quarter], turns[quarter : 2 * quarter], turns[2 * quarter : -1], [0]]
+    sums, after = {}, ()
+    for j in chunks[0]:
+        sums[j] = collect(j, back[spot[j][0]], spot[j][1] * slots, True, after)
+        after = sums[j][:1]
+    half_d = D // 2
+    gate_part = weight_grad(row_grad_body, row_spot, all_rows, blocks_dz, (half_d, inner), after)
+    up_part = weight_grad(row_grad_body, row_spot, all_rows, blocks_du, (half_d, inner), gate_part[:1])
+    first_out = outputs(out_chunks[0], up_part[:1])
+    after = first_out[:1]
+    for j in chunks[1]:
+        sums[j] = collect(j, back[spot[j][0]], spot[j][1] * slots, True, after)
+        after = sums[j][:1]
+    later_out = [outputs(chunk, after) for chunk in out_chunks[1:]]
+    first_out = exchange(gate(first_out, back[1][1:]))
     returned = [return_z(sums[j][0], j) for j in range(1, planes)]
     grad_residual, grad_low, small_part = call(
         functools.partial(token_body, members, planes, experts),
         (idx, *sums[0], *returned, route, residual, packed, grad_out, *small),
         "s" + "v" * (2 + planes - 1 + 4 + members),
         [((length, D), F32), ((length, D), BF16), ((experts + 8, D), F32)],
-        scratch=[pltpu.VMEM((experts, D), BF16), pltpu.VMEM((1, D), F32)],
+        scratch=[pltpu.VMEM((experts, D), F32), pltpu.VMEM((1, D), F32)],
+        after=[*first_out[1:], *(out[0] for out in later_out)],
     )
     grad_all = gather_plane(grad_low)
-
-    expert_sum = residual
-    for first, last, after in ((0, planes // 2, [s[0] for s in sums[1:]]), (planes // 2, planes, grad_all[1:])):
-        span = last - first
-        weighted = call(
-            functools.partial(down_body, span, members, slots),
-            (idx, *blocks_gm[first:last], down_mine, down_peer),
-            "s" + "v" * (span + 2),
-            [((span * slots, D), BF16)] * members,
-            flops=2 * span * rows * D * inner,
+    def token_sums(c, pieces, after=()):
+        return [collect(j, pieces, i * slots, False, after)[0] for i, j in enumerate(out_chunks[c])]
+
+    def returns(c, values):
+        return [return_z(value, j) for j, value in zip(out_chunks[c], values)]
+
+    out_sums = token_sums(0, first_out)
+    out_parts = returns(0, out_sums)
+
+    output_keep, output_away = call(
+        functools.partial(output_grad_body, members),
+        (idx, mixed, *grad_all),
+        "sv" + "a" * members,
+        [((half, D), F32), ((half, D), BF16)],
+        scratch=[pltpu.VMEM((total, D), BF16), pltpu.SemaphoreType.DMA((members,))],
+        after=out_sums,
+    )
+    output_peer = swap_dp(output_away)
+    middle_out = exchange(gate(later_out[0], grad_all[1:]))
+    out_sums = token_sums(1, middle_out)
+
+    def split_z(keep, peer, parts, after=()):
+        height, width = keep.shape
+        return call(
+            functools.partial(split_body, planes, parts),
+            (idx, keep, peer),
+            "svv",
+            [((height // planes, width), F32)] + [((height // planes, width), BF16)] * (planes - 1),
             after=after,
         )
-        weighted = exchange(weighted)
-        for j in range(first, last):
-            at_row = (j - first) * slots
-            part = collect([w[at_row : at_row + slots] for w in weighted], j, False)[0]
-            if j > 0:
-                part = return_z(part, j).astype(F32)
-            expert_sum = expert_sum + part
-    block_out = expert_sum.astype(BF16)
-
-    half_d = D // 2
-
-    def row_grad(blocks):
+
+    def scatter_z(pieces):
+        return [pieces[0]] + [return_z(pieces[j], j) for j in range(1, planes)]
+
+    def add_z(pieces, holders, after=()):
+        height, width = pieces[0].shape
         return call(
-            functools.partial(row_grad_body, (len(slot_pieces), planes), slots),
-            (idx, *slot_pieces, *blocks),
-            "s" + "a" * (len(slot_pieces) + planes),
-            [((half_d, inner), F32), ((half_d, inner), BF16)],
-            scratch=[
-                pltpu.VMEM((whole, D), BF16),
-                pltpu.VMEM((whole, inner), BF16),
-                pltpu.SemaphoreType.DMA((len(slot_pieces) + planes,)),
-            ],
-            vmem=48,
-            flops=2 * whole * D * inner,
+            functools.partial(add_body, holders),
+            (idx, *pieces),
+            "s" + "v" * planes,
+            [((height // holders, width), BF16)] * holders,
+            after=after,
         )
 
-    grad_gate, away = row_grad(blocks_dz)
-    grad_gate = (grad_gate + swap_dp(away).astype(F32))[None]
-    grad_up, away = row_grad(blocks_du)
-    grad_up = (grad_up + swap_dp(away).astype(F32))[None]
-    grad_down, away = call(
-        functools.partial(col_grad_body, planes, members, slots),
-        (idx, *blocks_gm, *grad_pieces),
-        "s" + "a" * (planes + len(grad_pieces)),
-        [((inner, half_d), F32), ((inner, half_d), BF16)],
-        scratch=[
-            pltpu.VMEM((whole, inner), BF16),
-            pltpu.VMEM((whole, D), BF16),
-            pltpu.SemaphoreType.DMA((planes + planes * members,)),
-        ],
-        vmem=48,
-        flops=2 * whole * D * inner,
-    )
-    grad_down = (grad_down + swap_dp(away).astype(F32))[None]
-
-    grads, grad_value, scaled_query, scaled_key, dots, grad_gains = call(
+    def spread_z(pieces, count):
+        pieces = pieces + [swap_dp(p) for p in pieces]
+        return call(
+            functools.partial(spread_body, planes),
+            (idx, *pieces),
+            "s" + "v" * (2 * planes),
+            [((own, D), F32)] * count,
+        )
+
+    grad_value, scaled_query, scaled_key, dots, grad_gains = call(
         functools.partial(attend_back_body, members, scale),
         (
             idx,
@@ -905,9 +1022,8 @@
             gain_query,
             gain_key,
         ),
-        "ss" + "a" * members + "v" * (members + 11),
+        "ss" + "a" * members + "d" * (members + 11),
         [
-            ((total, D), BF16),
             ((total, own), BF16),
             ((total, own), F32),
             ((total, own), F32),
@@ -915,81 +1031,71 @@
             ((8, own), F32),
         ],
         scratch=[
+            pltpu.VMEM((total, D), BF16),
             pltpu.VMEM((total, own), BF16),
             pltpu.VMEM((total, HD), F32),
             pltpu.VMEM((total, HD), F32),
             pltpu.SemaphoreType.DMA((members,)),
         ],
-        flops=20 * total * total * own // 2,
+        after=[output_keep],
     )
     dots = gather_plane(dots)
+    output_piece = add_z(scatter_z(split_z(output_keep, output_peer, 1, [grad_value])), 1)[0]
+
     grad_raw, keep, away = call(
         functools.partial(project_back_body, members, planes),
         (idx, scaled_query, scaled_key, grad_value, query_raw, key_raw, attn_input, *squares, *dots),
-        "s" + "v" * (6 + 2 * members),
+        "s" + "d" * (6 + 2 * members),
         [((total, 3 * own), BF16), ((D // 2, 3 * own), F32), ((D // 2, 3 * own), BF16)],
         vmem=48,
-        flops=6 * total * D * own,
-    )
-
-    def scatter_z(keep, away, parts, holders):
-        height, width = keep.shape
-        pieces = call(
-            functools.partial(split_body, planes, parts),
-            (idx, keep, swap_dp(away)),
-            "svv",
-            [((height // planes, width), F32)] + [((height // planes, width), BF16)] * (planes - 1),
-        )
-        pieces = [pieces[0]] + [return_z(pieces[j], j) for j in range(1, planes)]
-        return call(
-            functools.partial(add_body, holders),
-            (idx, *pieces),
-            "s" + "v" * planes,
-            [((height // planes // holders, width), BF16)] * holders,
-        )
-
-    def spread_z(piece, count):
-        pieces = gather_z(piece)
-        pieces = pieces + [swap_dp(p) for p in pieces]
-        return call(
-            functools.partial(spread_body, planes),
-            (idx, *pieces),
-            "s" + "v" * (2 * planes),
-            [((own, D), F32)] * count,
-        )
-
-    summed = exchange(scatter_z(keep, away, members, members))
+        after=[*out_parts, *out_sums],
+    )
+
+    partial_sent = call(
+        functools.partial(input_back_body, members),
+        (idx, grad_raw, w_qkv),
+        "svv",
+        [((length, D), F32)] + [((length, D), BF16)] * (members - 1),
+    )
+
+    out_parts += returns(1, out_sums)
+    third_out = exchange(gate(later_out[1], dots[1:]))
+    third_sums = token_sums(2, third_out)
+    split = split_z(keep, swap_dp(away), members, [partial_sent[0], output_piece])
+    partial_sent = gate(partial_sent, split[1:2])
+    scattered = scatter_z(split)
+    summed = add_z(scattered, members, third_sums)
+    summed = exchange(summed)
     piece = call(
         functools.partial(merge_body, members),
         (idx, *summed),
         "s" + "v" * members,
         [((slab, 3 * D), BF16)],
     )[0]
-    grad_query, grad_key, grad_value_w = spread_z(piece, 3)
-
-    keep, away = call(
-        output_grad_body,
-        (idx, mixed, grads),
-        "svv",
-        [((half, D), F32), ((half, D), BF16)],
-        flops=2 * total * own * D,
-    )
-    grad_output = spread_z(scatter_z(keep, away, 1, 1)[0], 1)[0]
-
-    partial = call(
-        functools.partial(input_back_body, members),
-        (idx, grad_raw, w_qkv),
-        "svv",
-        [((length, D), F32)] + [((length, D), BF16)] * (members - 1),
-        flops=6 * total * D * own,
-    )
-    partial = exchange(partial)
+    output_pieces = gather_z(gate([output_piece], [piece])[0])
+    out_parts += returns(2, third_sums)
+    down_part = weight_grad(
+        col_grad_body, grads_spot, grad_rows, blocks_gm, (inner, half_d), [piece]
+    )
+    away = [*gate([gate_part[1], up_part[1]], [piece]), down_part[1]]
+    grad_gate, grad_up, grad_down = (
+        (part[0] + swap_dp(peer).astype(F32))[None]
+        for part, peer in zip((gate_part, up_part, down_part), away)
+    )
+    partial = exchange(partial_sent)
+    last_out = exchange(gate(later_out[2], partial[1:]))
+    last_sums = token_sums(3, last_out)
+    block_out = residual + last_sums[0]
+    for part in out_parts:
+        block_out = block_out + part.astype(F32)
+    block_out = block_out.astype(BF16)
     grad_in, line = call(
         functools.partial(input_body, members, experts),
         (idx, *partial, *small, hidden_in, grad_residual),
         "s" + "v" * (2 * members + 2),
         [((length, D), F32), ((8, D), F32)],
         scratch=[pltpu.VMEM((1, D), F32)],
+        after=[piece],
     )
 
     small_part = jnp.concatenate([small_part[: experts + 1], line[:1]], axis=0)
@@ -1003,6 +1109,9 @@
     small_total = at(stack, (0 - mz) % planes)
     for z in range(1, planes):
         small_total = small_total + at(stack, (z - mz) % planes)
+    output_sum = spread_z(output_pieces, 1)[0]
+    grad_query, grad_key, grad_value_w = spread_z(gather_z(piece), 3)
+
     return (
         block_out,
         grad_in,
@@ -1013,7 +1122,7 @@
         grad_query,
         grad_key,
         grad_value_w,
-        grad_output,
+        output_sum,
         small_total[:experts].T,
         grad_gate,
         grad_up,

time: 1070 us -> 904 us (0.84)
  waiting for transfers between devices: 551 us -> 400 us
  starting transfers between devices: 175 us -> 121 us
  local copies, waits for them, and re-layouts: 60.8 us -> 77.8 us
  between operations: 2.79 us -> 16.4 us
    ppermute x18 -> x9, waiting for transfers between devices: 157 us -> 50.5 us  [fetch_z(): lax.ppermute(value, 'expert', [(i, (i - j) % planes) for i in range(plane...]
    ppermute x72 -> x57, waiting for transfers between devices: 287 us -> 194 us  [swap(): return lax.ppermute(value, 'shard', [(i, i ^ k) for i in range(members)])]
    all_gather x0 -> x2, waiting for transfers between devices: none -> 54.4 us  [the longest x1 54.4 us: shards(): input_z = lax.all_gather(packed, 'expert')]
    ppermute x72 -> x57, starting transfers between devices: 79.4 us -> 52.9 us  [swap(): return lax.ppermute(value, 'shard', [(i, i ^ k) for i in range(members)])]
    unnamed x297 -> x342, local copies, waits for them, and re-layouts: 50.3 us -> 75.6 us
    ppermute x12, starting transfers between devices: 39.4 us -> 14.8 us  [return_z(): lax.ppermute(value, 'expert', [(i, (i + j) % planes) for i in range(plane...]
    ppermute x18 -> x9, starting transfers between devices: 27.8 us -> 8.48 us  [fetch_z(): lax.ppermute(value, 'expert', [(i, (i - j) % planes) for i in range(plane...]
    ppermute x20, starting transfers between devices: 28.6 us -> 44.5 us  [swap_dp(): return lax.ppermute(value, 'dp', [(0, 1), (1, 0)])]
  transfers between devices with their start and end apart: 122 -> 100, of which waited for: 41 -> 36; matrix products, arithmetic and copies ran while one was open for 3% -> 2% of each run, Pallas kernels for 24% -> 25%
where the time goes in v3:
time: 904 us; the launch traced here: 896 us
  waiting for transfers between devices  400 us (44%)
  Pallas kernels  258 us (29%)
  starting transfers between devices  121 us (13%)
  local copies, waits for them, and re-layouts  77.8 us (9%)
  other arithmetic  22.9 us (3%)
  between operations  16.4 us (2%)
    pallas_call x39, Pallas kernels, call(): pl.pallas_call(run, out_shape=[jax.ShapeDtypeStruct(shape, dtype) for sha...  258 us
    ppermute x57, waiting for transfers between devices, swap(): return lax.ppermute(value, 'shard', [(i, i ^ k) for i in range(members)])  194 us
    ppermute x12, waiting for transfers between devices, return_z(): lax.ppermute(value, 'expert', [(i, (i + j) % planes) for i in range(plane...  93.5 us
    unnamed x342, local copies, waits for them, and re-layouts  75.6 us
    all_gather x1, waiting for transfers between devices, shards(): input_z = lax.all_gather(packed, 'expert')  54.4 us
    ppermute x57, starting transfers between devices, swap(): return lax.ppermute(value, 'shard', [(i, i ^ k) for i in range(members)])  52.9 us
    ppermute x9, waiting for transfers between devices, fetch_z(): lax.ppermute(value, 'expert', [(i, (i - j) % planes) for i in range(plane...  50.5 us
    ppermute x20, starting transfers between devices, swap_dp(): return lax.ppermute(value, 'dp', [(0, 1), (1, 0)])  44.5 us
  transfers between devices with their start and end apart: 100, of which 36 were waited for; matrix products, arithmetic and copies ran while one was open for 2% of the time, Pallas kernels for 25%

profile of v3, /device:TPU:9, one launch (start us, length us, event | category | flops | bytes accessed | tf_op | source)
XLA Modules:
  0.0 896.2 jit_solution(16508336818739213763)
XLA Ops:
  22.7 8.0 collective-permute-done.refs_4_.refs_2_.refs_7_.refs_11_.refs_6_
  38.6 27.3 %collective-permute-done.3.refs_8_ = bf16[256,1536]{1,0:T(8,128)(2,1)S(1)} collective-permute-done((bf16[256,1536]{1,0:T(8,128)(2,1)}, bf16[256,1536]{1,0:T(8,128)(2,1)S(1)}, u32[]{:S(2)}, u32[]{:S(2)}) %collective-permute-start.3) | collective-permute-done | bytes 786464 | tf_op jit(solution)/shard_map/ppermute | solution.py:723
  68.5 18.2 %collective-permute-start.7 = (bf16[256,1536]{1,0:T(8,128)(2,1)}, bf16[256,1536]{1,0:T(8,128)(2,1)}, u32[]{:S(2)}, u32[]{:S(2)}) collective-permute-start(bf16[256,1536]{1,0:T(8,128)(2,1)} %collective-permute-done.4.refs_9_), channel_id=1, source_target_pairs={{0,16},{16,0},{1,17},{17,1},{2,18},{18,2},{3,19},{19,3},{4,20},{20... | collective-permute-start | bytes 2359304 | tf_op jit(solution)/shard_map/ppermute | solution.py:732
  94.4 12.1 %shard_map.265 = (f32[768,512]{1,0:T(8,128)S(1)}, f32[768,512]{1,0:T(8,128)S(1)}, bf16[768,512]{1,0:T(8,128)(2,1)S(1)}, bf16[768,2048]{1,0:T(8,128)(2,1)}, bf16[...) custom-call(s32[3]{0:T(128)S(1)} %pad_add_fusion.refs_0_, ...), custom_call_target="tpu_custom_call" | custom-call | flops 1000 | bytes 1000 | tf_op jit(solution)/shard_map/pallas_call | solution.py:80
  133.0 10.9 %shard_map.267 = (f32[192,2048]{1,0:T(8,128)S(1)}, bf16[192,2048]{1,0:T(8,128)(2,1)S(1)}, bf16[192,2048]{1,0:T(8,128)(2,1)S(1)}, bf16[192,2048]{1,0:T(8,128)(2,1...) custom-call(s32[3]{0:T(128)S(1)} %pad_add_fusion.refs_0_, ...), custom_call_target="tpu_custom_call" | custom-call | flops 1000 | bytes 1000 | tf_op jit(solution)/shard_map/pallas_call | solution.py:80
  150.3 17.8 %collective-permute-done.15.refs_3_ = bf16[192,2048]{1,0:T(8,128)(2,1)S(1)} collective-permute-done((bf16[192,2048]{1,0:T(8,128)(2,1)S(1)}, bf16[192,2048]{1,0:T(8,128)(2,1)S(1)}, u32[]{:S(2)}, u32[]{:S(2)}) %collective-permute-start.15) | collective-permute-done | bytes 786464 | tf_op jit(solution)/shard_map/ppermute | solution.py:723
  168.3 18.1 %collective-permute-done.17.refs_5_ = bf16[192,2048]{1,0:T(8,128)(2,1)S(1)} collective-permute-done((bf16[192,2048]{1,0:T(8,128)(2,1)S(1)}, bf16[192,2048]{1,0:T(8,128)(2,1)S(1)}, u32[]{:S(2)}, u32[]{:S(2)}) %collective-permute-start.17) | collective-permute-done | bytes 786464 | tf_op jit(solution)/shard_map/ppermute | solution.py:723
  207.0 54.4 %all-gather.7.cloned.1.call-done = bf16[832,2048]{1,0:T(8,128)(2,1)} async-done(((bf16[208,2048]{1,0:T(8,128)(2,1)}), bf16[832,2048]{1,0:T(8,128)(2,1)}) %all-gather.7.cloned.1.call-update) | async-done | bytes 3407888 | tf_op jit(solution)/shard_map/all_gather | solution.py:842
  279.8 13.0 %collective-permute-done.24.refs_2_ = bf16[256,2048]{1,0:T(8,128)(2,1)S(1)} collective-permute-done((bf16[256,2048]{1,0:T(8,128)(2,1)S(1)}, bf16[256,2048]{1,0:T(8,128)(2,1)S(1)}, u32[]{:S(2)}, u32[]{:S(2)}) %collective-permute-start.24) | collective-permute-done | bytes 1048608 | tf_op jit(solution)/shard_map/ppermute | solution.py:723
  292.9 23.3 %collective-permute-done.26.refs_4_ = bf16[256,2048]{1,0:T(8,128)(2,1)} collective-permute-done((bf16[256,2048]{1,0:T(8,128)(2,1)S(1)}, bf16[256,2048]{1,0:T(8,128)(2,1)}, u32[]{:S(2)}, u32[]{:S(2)}) %collective-permute-start.26) | collective-permute-done | bytes 1048608 | tf_op jit(solution)/shard_map/ppermute | solution.py:723
  318.8 33.5 %shard_map.271 = (bf16[256,2048]{1,0:T(8,128)(2,1)}, bf16[256,2048]{1,0:T(8,128)(2,1)}, bf16[256,2048]{1,0:T(8,128)(2,1)}, bf16[256,2048]{1,0:T(8,128)(2,1)}, bf...) custom-call(s32[3]{0:T(128)} %copy-done.96, bf16[256,2048]{1,0:T(8,128)(2,1)} %copy-done.18, ...), custom_call_target="tpu_custom_call" | custom-call | flops 1000 | bytes 1000 | tf_op jit(solution)/shard_map/pallas_call | solution.py:80
  352.3 8.1 collective-permute-done.29.refs_4_.refs_8_
  363.1 33.9 %shard_map.273 = (bf16[256,2048]{1,0:T(8,128)(2,1)}, bf16[256,2048]{1,0:T(8,128)(2,1)}, bf16[256,2048]{1,0:T(8,128)(2,1)}, bf16[256,2048]{1,0:T(8,128)(2,1)}, bf...) custom-call(s32[3]{0:T(128)} %copy-done.96, bf16[256,2048]{1,0:T(8,128)(2,1)} %copy-done.41, ...), custom_call_target="tpu_custom_call" | custom-call | flops 1000 | bytes 1000 | tf_op jit(solution)/shard_map/pallas_call | solution.py:80
  397.0 7.5 collective-permute-done.32.refs_5_
  421.3 15.3 %shard_map.276 = (f32[1024,1024]{1,0:T(8,128)}, bf16[1024,1024]{1,0:T(8,128)(2,1)}) custom-call(s32[3]{0:T(128)S(1)} %copy-done.97, bf16[256,2048]{1,0:T(8,128)(2,1)S(1)} %copy-done.19, bf16[256,2048]{1,0:T(8,128)(2,1)S(1)} %copy-done.38, bf16[256,2048]{1,0:T(8,128)(2,1)S(1)} %copy-done.40, bf16[256,2048]{1,0:T(8,128)(2,1)} %collective-permute-done.26.refs_4_, ...), custom_call_target="tpu_custom_call" | custom-call | flops 1000 | bytes 1000 | tf_op jit(solution)/shard_map/pallas_call | solution.py:80
  436.6 15.6 %shard_map.277 = (f32[1024,1024]{1,0:T(8,128)}, bf16[1024,1024]{1,0:T(8,128)(2,1)}) custom-call(s32[3]{0:T(128)S(1)} %copy-done.97, bf16[256,2048]{1,0:T(8,128)(2,1)S(1)} %copy-done.19, bf16[256,2048]{1,0:T(8,128)(2,1)S(1)} %copy-done.38, bf16[256,2048]{1,0:T(8,128)(2,1)S(1)} %copy-done.40, bf16[256,2048]{1,0:T(8,128)(2,1)} %collective-permute-done.26.refs_4_, ...), custom_call_target="tpu_custom_call" | custom-call | flops 1000 | bytes 1000 | tf_op jit(solution)/shard_map/pallas_call | solution.py:80
  478.7 16.0 %collective-permute-done.36.refs_3_ = bf16[208,2048]{1,0:T(8,128)(2,1)} collective-permute-done((bf16[208,2048]{1,0:T(8,128)(2,1)}, bf16[208,2048]{1,0:T(8,128)(2,1)}, u32[]{:S(2)}, u32[]{:S(2)}) %collective-permute-start.36) | collective-permute-done | bytes 852000 | tf_op jit(solution)/shard_map/ppermute | solution.py:729
  505.9 13.1 %collective-permute-done.44.refs_5_ = bf16[192,2048]{1,0:T(8,128)(2,1)S(1)} collective-permute-done((bf16[192,2048]{1,0:T(8,128)(2,1)S(1)}, bf16[192,2048]{1,0:T(8,128)(2,1)S(1)}, u32[]{:S(2)}, u32[]{:S(2)}) %collective-permute-start.44) | collective-permute-done | bytes 786464 | tf_op jit(solution)/shard_map/ppermute | solution.py:723
  519.0 16.1 %collective-permute-done.43.refs_4_ = bf16[192,2048]{1,0:T(8,128)(2,1)S(1)} collective-permute-done((bf16[192,2048]{1,0:T(8,128)(2,1)S(1)}, bf16[192,2048]{1,0:T(8,128)(2,1)S(1)}, u32[]{:S(2)}, u32[]{:S(2)}) %collective-permute-start.43) | collective-permute-done | bytes 786464 | tf_op jit(solution)/shard_map/ppermute | solution.py:723
  542.9 18.7 %shard_map.287 = (bf16[768,512]{1,0:T(8,128)(2,1)S(1)}, f32[768,512]{1,0:T(8,128)S(1)}, f32[768,512]{1,0:T(8,128)S(1)}, f32[8,768]{1,0:T(8,128)S(1)}, f32[8,512]{1,0:T(8,128)S(1)}) custom-call(s32[3]{0:T(128)S(1)} %copy-done.97, s32[1,4]{1,0:T(1,128)S(1)} %copy-done.145, bf16[192,2048]{1,0:T(8,128)(2,1)S(1)} %get-tuple-element.258.refs_2_, ...), custom_call_target="tpu_custom_call" | custom-call | flops 1000 | bytes 1000 | tf_op jit(solution)/shard_map/pallas_call | solution.py:80
  571.2 13.2 %shard_map.289 = (bf16[768,1536]{1,0:T(8,128)(2,1)}, f32[1024,1536]{1,0:T(8,128)}, bf16[1024,1536]{1,0:T(8,128)(2,1)}) custom-call(s32[3]{0:T(128)S(1)} %copy-done.97, f32[768,512]{1,0:T(8,128)S(1)} %copy-done.89, f32[768,512]{1,0:T(8,128)S(1)} %copy-done.91, bf16[768,512]{1,0:T(8,128)(2,1)S(1)} %copy-done.79, f32[768,512]{1,0:T(8,128)} %copy-done.20, ...), custom_call_target="tpu_custom_call" | custom-call | flops 1000 | bytes 1000 | tf_op jit(solution)/shard_map/pallas_call | solution.py:80
  587.6 6.8 collective-permute-done.53.refs_2_
  599.6 9.7 %shard_map.290 = (f32[192,2048]{1,0:T(8,128)S(1)}, bf16[192,2048]{1,0:T(8,128)(2,1)}, bf16[192,2048]{1,0:T(8,128)(2,1)}, bf16[192,2048]{1,0:T(8,128)(2,1)}) custom-call(s32[3]{0:T(128)S(1)} %copy-done.97, bf16[768,1536]{1,0:T(8,128)(2,1)S(1)} %copy-done.83, bf16[2048,1536]{1,0:T(8,128)(2,1)S(1)} %bitcast.72), custom_call_target="tpu_custom_call" | custom-call | flops 1000 | bytes 1000 | tf_op jit(solution)/shard_map/pallas_call | solution.py:80
  631.7 19.8 %collective-permute-done.65.refs_4_ = bf16[128,2048]{1,0:T(8,128)(2,1)S(1)} collective-permute-done((bf16[128,2048]{1,0:T(8,128)(2,1)S(1)}, bf16[128,2048]{1,0:T(8,128)(2,1)S(1)}, u32[]{:S(2)}, u32[]{:S(2)}) %collective-permute-start.65) | collective-permute-done | bytes 524320 | tf_op jit(solution)/shard_map/ppermute | solution.py:723
  653.9 23.2 %collective-permute-done.69.refs_3_ = bf16[256,1536]{1,0:T(8,128)(2,1)S(1)} collective-permute-done((bf16[256,1536]{1,0:T(8,128)(2,1)S(1)}, bf16[256,1536]{1,0:T(8,128)(2,1)S(1)}, u32[]{:S(2)}, u32[]{:S(2)}) %collective-permute-start.69) | collective-permute-done | bytes 786464 | tf_op jit(solution)/shard_map/ppermute | solution.py:729
  681.4 11.1 %collective-permute-done.70.refs_4_ = bf16[256,1536]{1,0:T(8,128)(2,1)S(1)} collective-permute-done((bf16[256,1536]{1,0:T(8,128)(2,1)S(1)}, bf16[256,1536]{1,0:T(8,128)(2,1)S(1)}, u32[]{:S(2)}, u32[]{:S(2)}) %collective-permute-start.70) | collective-permute-done | bytes 786464 | tf_op jit(solution)/shard_map/ppermute | solution.py:729
  735.8 20.1 %collective-permute-done.63 = bf16[192,2048]{1,0:T(8,128)(2,1)} collective-permute-done((bf16[192,2048]{1,0:T(8,128)(2,1)}, bf16[192,2048]{1,0:T(8,128)(2,1)}, u32[]{:S(2)}, u32[]{:S(2)}) %collective-permute-start.63) | collective-permute-done | bytes 786464 | tf_op jit(solution)/shard_map/ppermute | solution.py:729
  756.1 10.2 %collective-permute-done.67 = bf16[192,2048]{1,0:T(8,128)(2,1)} collective-permute-done((bf16[192,2048]{1,0:T(8,128)(2,1)}, bf16[192,2048]{1,0:T(8,128)(2,1)}, u32[]{:S(2)}, u32[]{:S(2)}) %collective-permute-start.67) | collective-permute-done | bytes 786464 | tf_op jit(solution)/shard_map/ppermute | solution.py:729
  774.5 15.0 %collective-permute-done.89.refs_3_ = bf16[64,2048]{1,0:T(8,128)(2,1)S(1)} collective-permute-done((bf16[64,2048]{1,0:T(8,128)(2,1)}, bf16[64,2048]{1,0:T(8,128)(2,1)S(1)}, u32[]{:S(2)}, u32[]{:S(2)}) %collective-permute-start.89) | collective-permute-done | bytes 262176 | tf_op jit(solution)/shard_map/ppermute | solution.py:726
  816.9 14.9 %shard_map.301 = (f32[1024,1024]{1,0:T(8,128)}, bf16[1024,1024]{1,0:T(8,128)(2,1)}) custom-call(s32[3]{0:T(128)S(1)} %copy-done.97, bf16[128,2048]{1,0:T(8,128)(2,1)S(1)} %copy-done.48, bf16[128,2048]{1,0:T(8,128)(2,1)S(1)} %copy-done.63, bf16[128,2048]{1,0:T(8,128)(2,1)S(1)} %copy-done.65, bf16[128,2048]{1,0:T(8,128)(2,1)S(1)} %copy-done.67, ...), custom_call_target="tpu_custom_call" | custom-call | flops 1000 | bytes 1000 | tf_op jit(solution)/shard_map/pallas_call | solution.py:80
  831.8 25.0 %collective-permute-done.82.refs_3_ = bf16[64,6144]{1,0:T(8,128)(2,1)} collective-permute-done((bf16[64,6144]{1,0:T(8,128)(2,1)S(1)}, bf16[64,6144]{1,0:T(8,128)(2,1)}, u32[]{:S(2)}, u32[]{:S(2)}) %collective-permute-start.82) | collective-permute-done | bytes 786464 | tf_op jit(solution)/shard_map/ppermute | solution.py:726
  869.7 7.2 shard_map.299
  (593 shorter events, 322.6 us)
Async XLA Ops:
  7.2 83.0 %all-gather.5.cloned.1.call-start = ((), (), s32[]{:S(2)}) async-start(), calls=%async_computation | async-start | bytes 4259840 | tf_op jit(solution)/shard_map/all_gather | solution.py:784
  10.4 251.0 %all-gather.7.cloned.1.call-start = ((), (), s32[]{:S(2)}) async-start(), calls=%async_computation.1 | async-start | bytes 4259840 | tf_op jit(solution)/shard_map/all_gather | solution.py:842
  12.0 79.0 %collective-permute-start.2 = (bf16[208,2048]{1,0:T(8,128)(2,1)S(1)}, bf16[208,2048]{1,0:T(8,128)(2,1)S(1)}, u32[]{:S(2)}, u32[]{:S(2)}) collective-permute-start(bf16[208,2048]{1,0:T(8,128)(2,1)S(1)} %pad_maximum_fusion.refs_1_.refs_6_.refs_10_.refs_5_), channel_id=1, source_target_pairs={{0,3},{1,2},{2,1},{3,0},{4,7},{5,6},{6,5},{7,4},{8,11},{9,10},{10,... | collective-permute-start | bytes 2555912 | tf_op jit(solution)/shard_map/ppermute | solution.py:723
  13.2 77.8 %collective-permute-start.1 = (bf16[208,2048]{1,0:T(8,128)(2,1)S(1)}, bf16[208,2048]{1,0:T(8,128)(2,1)}, u32[]{:S(2)}, u32[]{:S(2)}) collective-permute-start(bf16[208,2048]{1,0:T(8,128)(2,1)S(1)} %pad_maximum_fusion.refs_1_.refs_6_.refs_10_.refs_5_), channel_id=1, source_target_pairs={{0,2},{1,3},{2,0},{3,1},{4,6},{5,7},{6,4},{7,5},{8,10},{9,11},{10,... | collective-permute-start | bytes 2555912 | tf_op jit(solution)/shard_map/ppermute | solution.py:723
  20.1 45.8 %collective-permute-start.3 = (bf16[256,1536]{1,0:T(8,128)(2,1)}, bf16[256,1536]{1,0:T(8,128)(2,1)S(1)}, u32[]{:S(2)}, u32[]{:S(2)}) collective-permute-start(bf16[256,1536]{1,0:T(8,128)(2,1)} %get-tuple-element.171), channel_id=1, source_target_pairs={{0,1},{1,0},{2,3},{3,2},{4,5},{5,4},{6,7},{7,6},{8,9},{9,8},{10,11... | collective-permute-start | bytes 2359304 | tf_op jit(solution)/shard_map/ppermute | solution.py:723
  21.3 47.1 %collective-permute-start.4 = (bf16[256,1536]{1,0:T(8,128)(2,1)}, bf16[256,1536]{1,0:T(8,128)(2,1)}, u32[]{:S(2)}, u32[]{:S(2)}) collective-permute-start(bf16[256,1536]{1,0:T(8,128)(2,1)} %get-tuple-element.172), channel_id=1, source_target_pairs={{0,2},{1,3},{2,0},{3,1},{4,6},{5,7},{6,4},{7,5},{8,10},{9,11},{10,... | collective-permute-start | bytes 2359304 | tf_op jit(solution)/shard_map/ppermute | solution.py:723
  36.1 50.5 %collective-permute-start.5 = (bf16[256,1536]{1,0:T(8,128)(2,1)S(1)}, bf16[256,1536]{1,0:T(8,128)(2,1)}, u32[]{:S(2)}, u32[]{:S(2)}) collective-permute-start(bf16[256,1536]{1,0:T(8,128)(2,1)S(1)} %shard_map.264), channel_id=1, source_target_pairs={{0,3},{1,2},{2,1},{3,0},{4,7},{5,6},{6,5},{7,4},{8,11},{9,10},{10,... | collective-permute-start | bytes 2359304 | tf_op jit(solution)/shard_map/ppermute | solution.py:723
  115.7 70.6 %collective-permute-start.18 = (bf16[1024,1024]{1,0:T(8,128)(2,1)}, bf16[1024,1024]{1,0:T(8,128)(2,1)S(1)}, u32[]{:S(2)}, u32[]{:S(2)}) collective-permute-start(bf16[1024,1024]{1,0:T(8,128)(2,1)} %bitcast.11.refs_13_), channel_id=1, source_target_pairs={{0,16},{16,0},{1,17},{17,1},{2,18},{18,2},{3,19},{19,3},{4,20},{20... | collective-permute-start | bytes 6291464 | tf_op jit(solution)/shard_map/ppermute | solution.py:732
  118.5 67.9 %collective-permute-start.19 = (bf16[1024,1024]{1,0:T(8,128)(2,1)}, bf16[1024,1024]{1,0:T(8,128)(2,1)}, u32[]{:S(2)}, u32[]{:S(2)}) collective-permute-start(bf16[1024,1024]{1,0:T(8,128)(2,1)} %bitcast.12.refs_15_), channel_id=1, source_target_pairs={{0,16},{16,0},{1,17},{17,1},{2,18},{18,2},{3,19},{19,3},{4,20},{20... | collective-permute-start | bytes 6291464 | tf_op jit(solution)/shard_map/ppermute | solution.py:732
  124.6 61.8 %collective-permute-start.20 = (bf16[1024,1024]{1,0:T(8,128)(2,1)S(1)}, bf16[1024,1024]{1,0:T(8,128)(2,1)S(1)}, u32[]{:S(2)}, u32[]{:S(2)}) collective-permute-start(bf16[1024,1024]{1,0:T(8,128)(2,1)S(1)} %bitcast.61), channel_id=1, source_target_pairs={{0,16},{16,0},{1,17},{17,1},{2,18},{18,2},{3,19},{19,3},{4,20},{20... | collective-permute-start | bytes 6291464 | tf_op jit(solution)/shard_map/ppermute | solution.py:732
  204.3 61.8 %collective-permute-start.21 = (bf16[384,2048]{1,0:T(8,128)(2,1)}, bf16[384,2048]{1,0:T(8,128)(2,1)S(1)}, u32[]{:S(2)}, u32[]{:S(2)}) collective-permute-start(bf16[384,2048]{1,0:T(8,128)(2,1)} %get-tuple-element.201), channel_id=1, source_target_pairs={{0,1},{1,0},{2,3},{3,2},{4,5},{5,4},{6,7},{7,6},{8,9},{9,8},{10,11... | collective-permute-start | bytes 4718600 | tf_op jit(solution)/shard_map/ppermute | solution.py:723
  204.6 61.5 %collective-permute-start.22 = (bf16[384,2048]{1,0:T(8,128)(2,1)}, bf16[384,2048]{1,0:T(8,128)(2,1)}, u32[]{:S(2)}, u32[]{:S(2)}) collective-permute-start(bf16[384,2048]{1,0:T(8,128)(2,1)} %get-tuple-element.202), channel_id=1, source_target_pairs={{0,2},{1,3},{2,0},{3,1},{4,6},{5,7},{6,4},{7,5},{8,10},{9,11},{10,... | collective-permute-start | bytes 4718600 | tf_op jit(solution)/shard_map/ppermute | solution.py:723
  204.8 66.9 %collective-permute-start.23 = (bf16[384,2048]{1,0:T(8,128)(2,1)}, bf16[384,2048]{1,0:T(8,128)(2,1)}, u32[]{:S(2)}, u32[]{:S(2)}) collective-permute-start(bf16[384,2048]{1,0:T(8,128)(2,1)} %get-tuple-element.203), channel_id=1, source_target_pairs={{0,3},{1,2},{2,1},{3,0},{4,7},{5,6},{6,5},{7,4},{8,11},{9,10},{10,... | collective-permute-start | bytes 4718600 | tf_op jit(solution)/shard_map/ppermute | solution.py:723
  316.7 43.8 %collective-permute-start.29 = (bf16[256,2048]{1,0:T(8,128)(2,1)}, bf16[256,2048]{1,0:T(8,128)(2,1)}, u32[]{:S(2)}, u32[]{:S(2)}) collective-permute-start(bf16[256,2048]{1,0:T(8,128)(2,1)} %get-tuple-element.218), channel_id=1, source_target_pairs={{0,3},{1,2},{2,1},{3,0},{4,7},{5,6},{6,5},{7,4},{8,11},{9,10},{10,... | collective-permute-start | bytes 3145736 | tf_op jit(solution)/shard_map/ppermute | solution.py:723
  360.7 43.9 %collective-permute-start.32 = (bf16[256,2048]{1,0:T(8,128)(2,1)}, bf16[256,2048]{1,0:T(8,128)(2,1)S(1)}, u32[]{:S(2)}, u32[]{:S(2)}) collective-permute-start(bf16[256,2048]{1,0:T(8,128)(2,1)} %get-tuple-element.230), channel_id=1, source_target_pairs={{0,3},{1,2},{2,1},{3,0},{4,7},{5,6},{6,5},{7,4},{8,11},{9,10},{10,... | collective-permute-start | bytes 3145736 | tf_op jit(solution)/shard_map/ppermute | solution.py:723
  405.5 50.7 %collective-permute-start.33 = (bf16[256,2048]{1,0:T(8,128)(2,1)}, bf16[256,2048]{1,0:T(8,128)(2,1)S(1)}, u32[]{:S(2)}, u32[]{:S(2)}) collective-permute-start(bf16[256,2048]{1,0:T(8,128)(2,1)} %get-tuple-element.232), channel_id=1, source_target_pairs={{0,1},{1,0},{2,3},{3,2},{4,5},{5,4},{6,7},{7,6},{8,9},{9,8},{10,11... | collective-permute-start | bytes 3145736 | tf_op jit(solution)/shard_map/ppermute | solution.py:723
  405.7 50.6 %collective-permute-start.34 = (bf16[256,2048]{1,0:T(8,128)(2,1)}, bf16[256,2048]{1,0:T(8,128)(2,1)}, u32[]{:S(2)}, u32[]{:S(2)}) collective-permute-start(bf16[256,2048]{1,0:T(8,128)(2,1)} %get-tuple-element.233), channel_id=1, source_target_pairs={{0,2},{1,3},{2,0},{3,1},{4,6},{5,7},{6,4},{7,5},{8,10},{9,11},{10,... | collective-permute-start | bytes 3145736 | tf_op jit(solution)/shard_map/ppermute | solution.py:723
  405.7 50.6 %collective-permute-start.35 = (bf16[256,2048]{1,0:T(8,128)(2,1)}, bf16[256,2048]{1,0:T(8,128)(2,1)}, u32[]{:S(2)}, u32[]{:S(2)}) collective-permute-start(bf16[256,2048]{1,0:T(8,128)(2,1)} %get-tuple-element.234), channel_id=1, source_target_pairs={{0,3},{1,2},{2,1},{3,0},{4,7},{5,6},{6,5},{7,4},{8,11},{9,10},{10,... | collective-permute-start | bytes 3145736 | tf_op jit(solution)/shard_map/ppermute | solution.py:723
  421.3 73.5 %collective-permute-start.36 = (bf16[208,2048]{1,0:T(8,128)(2,1)}, bf16[208,2048]{1,0:T(8,128)(2,1)}, u32[]{:S(2)}, u32[]{:S(2)}) collective-permute-start(bf16[208,2048]{1,0:T(8,128)(2,1)} %shard_map.274.refs_6_), channel_id=1, source_target_pairs={{0,4},{4,8},{8,12},{12,0},{1,5},{5,9},{9,13},{13,1},{2,6},{6,10},{... | collective-permute-start | bytes 2555912 | tf_op jit(solution)/shard_map/ppermute | solution.py:729
  503.7 64.4 %collective-permute-start.48 = (bf16[192,2048]{1,0:T(8,128)(2,1)S(1)}, bf16[192,2048]{1,0:T(8,128)(2,1)S(1)}, u32[]{:S(2)}, u32[]{:S(2)}) collective-permute-start(bf16[192,2048]{1,0:T(8,128)(2,1)S(1)} %shard_map.285.refs_6_), channel_id=1, source_target_pairs={{0,4},{4,8},{8,12},{12,0},{1,5},{5,9},{9,13},{13,1},{2,6},{6,10},{... | collective-permute-start | bytes 2359304 | tf_op jit(solution)/shard_map/ppermute | solution.py:729
  625.9 51.2 %collective-permute-start.69 = (bf16[256,1536]{1,0:T(8,128)(2,1)S(1)}, bf16[256,1536]{1,0:T(8,128)(2,1)S(1)}, u32[]{:S(2)}, u32[]{:S(2)}) collective-permute-start(bf16[256,1536]{1,0:T(8,128)(2,1)S(1)} %get-tuple-element.308), channel_id=1, source_target_pairs={{0,8},{4,12},{8,0},{12,4},{1,9},{5,13},{9,1},{13,5},{2,10},{6,14},... | collective-permute-start | bytes 2359304 | tf_op jit(solution)/shard_map/ppermute | solution.py:729
  630.2 62.3 %collective-permute-start.70 = (bf16[256,1536]{1,0:T(8,128)(2,1)S(1)}, bf16[256,1536]{1,0:T(8,128)(2,1)S(1)}, u32[]{:S(2)}, u32[]{:S(2)}) collective-permute-start(bf16[256,1536]{1,0:T(8,128)(2,1)S(1)} %get-tuple-element.309), channel_id=1, source_target_pairs={{0,12},{4,0},{8,4},{12,8},{1,13},{5,1},{9,5},{13,9},{2,14},{6,2},{... | collective-permute-start | bytes 2359304 | tf_op jit(solution)/shard_map/ppermute | solution.py:729
  630.2 63.7 %collective-permute-start.68 = (bf16[256,1536]{1,0:T(8,128)(2,1)S(1)}, bf16[256,1536]{1,0:T(8,128)(2,1)S(1)}, u32[]{:S(2)}, u32[]{:S(2)}) collective-permute-start(bf16[256,1536]{1,0:T(8,128)(2,1)S(1)} %get-tuple-element.290), channel_id=1, source_target_pairs={{0,4},{4,8},{8,12},{12,0},{1,5},{5,9},{9,13},{13,1},{2,6},{6,10},{... | collective-permute-start | bytes 2359304 | tf_op jit(solution)/shard_map/ppermute | solution.py:729
  651.5 62.5 %collective-permute-start.57 = (bf16[192,2048]{1,0:T(8,128)(2,1)}, bf16[192,2048]{1,0:T(8,128)(2,1)}, u32[]{:S(2)}, u32[]{:S(2)}) collective-permute-start(bf16[192,2048]{1,0:T(8,128)(2,1)} %get-tuple-element.291), channel_id=1, source_target_pairs={{0,1},{1,0},{2,3},{3,2},{4,5},{5,4},{6,7},{7,6},{8,9},{9,8},{10,11... | collective-permute-start | bytes 2359304 | tf_op jit(solution)/shard_map/ppermute | solution.py:723
  652.5 61.6 %collective-permute-start.58 = (bf16[192,2048]{1,0:T(8,128)(2,1)}, bf16[192,2048]{1,0:T(8,128)(2,1)}, u32[]{:S(2)}, u32[]{:S(2)}) collective-permute-start(bf16[192,2048]{1,0:T(8,128)(2,1)} %get-tuple-element.292), channel_id=1, source_target_pairs={{0,2},{1,3},{2,0},{3,1},{4,6},{5,7},{6,4},{7,5},{8,10},{9,11},{10,... | collective-permute-start | bytes 2359304 | tf_op jit(solution)/shard_map/ppermute | solution.py:723
  705.6 50.4 %collective-permute-start.63 = (bf16[192,2048]{1,0:T(8,128)(2,1)}, bf16[192,2048]{1,0:T(8,128)(2,1)}, u32[]{:S(2)}, u32[]{:S(2)}) collective-permute-start(bf16[192,2048]{1,0:T(8,128)(2,1)} %shard_map.288.refs_16_), channel_id=1, source_target_pairs={{0,8},{4,12},{8,0},{12,4},{1,9},{5,13},{9,1},{13,5},{2,10},{6,14},... | collective-permute-start | bytes 2359304 | tf_op jit(solution)/shard_map/ppermute | solution.py:729
  709.7 56.7 %collective-permute-start.67 = (bf16[192,2048]{1,0:T(8,128)(2,1)}, bf16[192,2048]{1,0:T(8,128)(2,1)}, u32[]{:S(2)}, u32[]{:S(2)}) collective-permute-start(bf16[192,2048]{1,0:T(8,128)(2,1)} %shard_map.295.refs_5_), channel_id=1, source_target_pairs={{0,12},{4,0},{8,4},{12,8},{1,13},{5,1},{9,5},{13,9},{2,14},{6,2},{... | collective-permute-start | bytes 2359304 | tf_op jit(solution)/shard_map/ppermute | solution.py:729
  798.3 78.6 %collective-permute-start.95 = (bf16[1024,1024]{1,0:T(8,128)(2,1)}, bf16[1024,1024]{1,0:T(8,128)(2,1)}, u32[]{:S(2)}, u32[]{:S(2)}) collective-permute-start(bf16[1024,1024]{1,0:T(8,128)(2,1)} %get-tuple-element.324), channel_id=1, source_target_pairs={{0,16},{16,0},{1,17},{17,1},{2,18},{18,2},{3,19},{19,3},{4,20},{20... | collective-permute-start | bytes 6291464 | tf_op jit(solution)/shard_map/ppermute | solution.py:732
  799.0 57.8 %collective-permute-start.82 = (bf16[64,6144]{1,0:T(8,128)(2,1)S(1)}, bf16[64,6144]{1,0:T(8,128)(2,1)}, u32[]{:S(2)}, u32[]{:S(2)}) collective-permute-start(bf16[64,6144]{1,0:T(8,128)(2,1)S(1)} %shard_map.297.refs_11_.refs_1_), channel_id=1, source_target_pairs={{0,8},{4,12},{8,0},{12,4},{1,9},{5,13},{9,1},{13,5},{2,10},{6,14},... | collective-permute-start | bytes 2359304 | tf_op jit(solution)/shard_map/ppermute | solution.py:726
  803.6 57.6 %collective-permute-start.81 = (bf16[64,6144]{1,0:T(8,128)(2,1)S(1)}, bf16[64,6144]{1,0:T(8,128)(2,1)}, u32[]{:S(2)}, u32[]{:S(2)}) collective-permute-start(bf16[64,6144]{1,0:T(8,128)(2,1)S(1)} %shard_map.297.refs_11_.refs_1_), channel_id=1, source_target_pairs={{0,12},{4,0},{8,4},{12,8},{1,13},{5,1},{9,5},{13,9},{2,14},{6,2},{... | collective-permute-start | bytes 2359304 | tf_op jit(solution)/shard_map/ppermute | solution.py:726
  808.1 53.6 %collective-permute-start.87 = (bf16[64,6144]{1,0:T(8,128)(2,1)S(1)}, bf16[64,6144]{1,0:T(8,128)(2,1)}, u32[]{:S(2)}, u32[]{:S(2)}) collective-permute-start(bf16[64,6144]{1,0:T(8,128)(2,1)S(1)} %collective-permute-done.83.refs_4_), channel_id=1, source_target_pairs={{0,16},{16,0},{1,17},{17,1},{2,18},{18,2},{3,19},{19,3},{4,20},{20... | collective-permute-start | bytes 2359304 | tf_op jit(solution)/shard_map/ppermute | solution.py:732
  811.3 70.4 %collective-permute-start.96 = (bf16[1024,1024]{1,0:T(8,128)(2,1)}, bf16[1024,1024]{1,0:T(8,128)(2,1)}, u32[]{:S(2)}, u32[]{:S(2)}) collective-permute-start(bf16[1024,1024]{1,0:T(8,128)(2,1)} %get-tuple-element.325), channel_id=1, source_target_pairs={{0,16},{16,0},{1,17},{17,1},{2,18},{18,2},{3,19},{19,3},{4,20},{20... | collective-permute-start | bytes 6291464 | tf_op jit(solution)/shard_map/ppermute | solution.py:732
  (237 other events, 3782.0 us)
Sparse Core Ops, SparseCore 0:
  10.6 66.4 all-gather.4
  194.9 66.4 all-gather.6

commit v4 on v3

--- a/solution.py
+++ b/solution.py
@@ -925,7 +925,7 @@
 
     all_rows = [piece for pieces in slot_rows for piece in pieces]
     quarter = planes // 4
-    out_chunks = [turns[:quarter], turns[quarter : 2 * quarter], turns[2 * quarter : -1], [0]]
+    out_chunks = [turns[quarter : 2 * quarter], turns[:quarter], turns[2 * quarter : -1], [0]]
     sums, after = {}, ()
     for j in chunks[0]:
         sums[j] = collect(j, back[spot[j][0]], spot[j][1] * slots, True, after)

time: 904 us -> 887 us (0.981)
  waiting for transfers between devices: 400 us -> 383 us
    ppermute x12, waiting for transfers between devices: 93.5 us -> 70.5 us  [return_z(): lax.ppermute(value, 'expert', [(i, (i + j) % planes) for i in range(plane...]
  transfers between devices with their start and end apart: 100 -> 100, of which waited for: 36 -> 36; matrix products, arithmetic and copies ran while one was open for 2% -> 2% of each run, Pallas kernels for 25% -> 26%
where the time goes in v4:
time: 887 us; the launch traced here: 879 us
  waiting for transfers between devices  383 us (43%)
  Pallas kernels  258 us (29%)
  starting transfers between devices  121 us (14%)
  local copies, waits for them, and re-layouts  77.8 us (9%)
  other arithmetic  22.9 us (3%)
  between operations  16.4 us (2%)
    pallas_call x39, Pallas kernels, call(): pl.pallas_call(run, out_shape=[jax.ShapeDtypeStruct(shape, dtype) for sha...  258 us
    ppermute x57, waiting for transfers between devices, swap(): return lax.ppermute(value, 'shard', [(i, i ^ k) for i in range(members)])  194 us
    unnamed x342, local copies, waits for them, and re-layouts  75.6 us
    ppermute x12, waiting for transfers between devices, return_z(): lax.ppermute(value, 'expert', [(i, (i + j) % planes) for i in range(plane...  70.5 us
    ppermute x9, waiting for transfers between devices, fetch_z(): lax.ppermute(value, 'expert', [(i, (i - j) % planes) for i in range(plane...  56.4 us
    all_gather x1, waiting for transfers between devices, shards(): input_z = lax.all_gather(packed, 'expert')  54.4 us
    ppermute x57, starting transfers between devices, swap(): return lax.ppermute(value, 'shard', [(i, i ^ k) for i in range(members)])  53.3 us
    ppermute x20, starting transfers between devices, swap_dp(): return lax.ppermute(value, 'dp', [(0, 1), (1, 0)])  42.6 us
  transfers between devices with their start and end apart: 100, of which 36 were waited for; matrix products, arithmetic and copies ran while one was open for 2% of the time, Pallas kernels for 26%

profile of v4, /device:TPU:9, one launch (start us, length us, event | category | flops | bytes accessed | tf_op | source)
XLA Modules:
  0.0 879.2 jit_solution(6117077516872490673)
XLA Ops:
  22.7 8.0 collective-permute-done.refs_4_.refs_2_.refs_7_.refs_11_.refs_6_
  38.6 27.3 %collective-permute-done.3.refs_8_ = bf16[256,1536]{1,0:T(8,128)(2,1)S(1)} collective-permute-done((bf16[256,1536]{1,0:T(8,128)(2,1)}, bf16[256,1536]{1,0:T(8,128)(2,1)S(1)}, u32[]{:S(2)}, u32[]{:S(2)}) %collective-permute-start.3) | collective-permute-done | bytes 786464 | tf_op jit(solution)/shard_map/ppermute | solution.py:723
  68.5 18.2 %collective-permute-start.7 = (bf16[256,1536]{1,0:T(8,128)(2,1)}, bf16[256,1536]{1,0:T(8,128)(2,1)}, u32[]{:S(2)}, u32[]{:S(2)}) collective-permute-start(bf16[256,1536]{1,0:T(8,128)(2,1)} %collective-permute-done.4.refs_9_), channel_id=1, source_target_pairs={{0,16},{16,0},{1,17},{17,1},{2,18},{18,2},{3,19},{19,3},{4,20},{20... | collective-permute-start | bytes 2359304 | tf_op jit(solution)/shard_map/ppermute | solution.py:732
  94.4 12.1 %shard_map.265 = (f32[768,512]{1,0:T(8,128)S(1)}, f32[768,512]{1,0:T(8,128)S(1)}, bf16[768,512]{1,0:T(8,128)(2,1)S(1)}, bf16[768,2048]{1,0:T(8,128)(2,1)}, bf16[...) custom-call(s32[3]{0:T(128)S(1)} %pad_add_fusion.refs_0_, ...), custom_call_target="tpu_custom_call" | custom-call | flops 1000 | bytes 1000 | tf_op jit(solution)/shard_map/pallas_call | solution.py:80
  118.5 6.1 collective-permute-done.12.refs_6_.refs_2_
  133.0 10.9 %shard_map.267 = (f32[192,2048]{1,0:T(8,128)S(1)}, bf16[192,2048]{1,0:T(8,128)(2,1)S(1)}, bf16[192,2048]{1,0:T(8,128)(2,1)S(1)}, bf16[192,2048]{1,0:T(8,128)(2,1...) custom-call(s32[3]{0:T(128)S(1)} %pad_add_fusion.refs_0_, ...), custom_call_target="tpu_custom_call" | custom-call | flops 1000 | bytes 1000 | tf_op jit(solution)/shard_map/pallas_call | solution.py:80
  150.3 17.8 %collective-permute-done.15.refs_3_ = bf16[192,2048]{1,0:T(8,128)(2,1)S(1)} collective-permute-done((bf16[192,2048]{1,0:T(8,128)(2,1)S(1)}, bf16[192,2048]{1,0:T(8,128)(2,1)S(1)}, u32[]{:S(2)}, u32[]{:S(2)}) %collective-permute-start.15) | collective-permute-done | bytes 786464 | tf_op jit(solution)/shard_map/ppermute | solution.py:723
  168.3 18.1 %collective-permute-done.17.refs_5_ = bf16[192,2048]{1,0:T(8,128)(2,1)S(1)} collective-permute-done((bf16[192,2048]{1,0:T(8,128)(2,1)S(1)}, bf16[192,2048]{1,0:T(8,128)(2,1)S(1)}, u32[]{:S(2)}, u32[]{:S(2)}) %collective-permute-start.17) | collective-permute-done | bytes 786464 | tf_op jit(solution)/shard_map/ppermute | solution.py:723
  207.0 54.4 %all-gather.7.cloned.1.call-done = bf16[832,2048]{1,0:T(8,128)(2,1)} async-done(((bf16[208,2048]{1,0:T(8,128)(2,1)}), bf16[832,2048]{1,0:T(8,128)(2,1)}) %all-gather.7.cloned.1.call-update) | async-done | bytes 3407888 | tf_op jit(solution)/shard_map/all_gather | solution.py:842
  279.8 13.0 %collective-permute-done.24.refs_2_ = bf16[256,2048]{1,0:T(8,128)(2,1)S(1)} collective-permute-done((bf16[256,2048]{1,0:T(8,128)(2,1)S(1)}, bf16[256,2048]{1,0:T(8,128)(2,1)S(1)}, u32[]{:S(2)}, u32[]{:S(2)}) %collective-permute-start.24) | collective-permute-done | bytes 1048608 | tf_op jit(solution)/shard_map/ppermute | solution.py:723
  292.9 23.3 %collective-permute-done.26.refs_4_ = bf16[256,2048]{1,0:T(8,128)(2,1)} collective-permute-done((bf16[256,2048]{1,0:T(8,128)(2,1)S(1)}, bf16[256,2048]{1,0:T(8,128)(2,1)}, u32[]{:S(2)}, u32[]{:S(2)}) %collective-permute-start.26) | collective-permute-done | bytes 1048608 | tf_op jit(solution)/shard_map/ppermute | solution.py:723
  318.8 33.5 %shard_map.271 = (bf16[256,2048]{1,0:T(8,128)(2,1)}, bf16[256,2048]{1,0:T(8,128)(2,1)}, bf16[256,2048]{1,0:T(8,128)(2,1)}, bf16[256,2048]{1,0:T(8,128)(2,1)}, bf...) custom-call(s32[3]{0:T(128)} %copy-done.96, bf16[256,2048]{1,0:T(8,128)(2,1)} %copy-done.18, ...), custom_call_target="tpu_custom_call" | custom-call | flops 1000 | bytes 1000 | tf_op jit(solution)/shard_map/pallas_call | solution.py:80
  352.3 8.1 collective-permute-done.29.refs_4_.refs_8_
  363.1 33.9 %shard_map.273 = (bf16[256,2048]{1,0:T(8,128)(2,1)}, bf16[256,2048]{1,0:T(8,128)(2,1)}, bf16[256,2048]{1,0:T(8,128)(2,1)}, bf16[256,2048]{1,0:T(8,128)(2,1)}, bf...) custom-call(s32[3]{0:T(128)} %copy-done.96, bf16[256,2048]{1,0:T(8,128)(2,1)} %copy-done.41, ...), custom_call_target="tpu_custom_call" | custom-call | flops 1000 | bytes 1000 | tf_op jit(solution)/shard_map/pallas_call | solution.py:80
  397.0 7.5 collective-permute-done.32.refs_5_
  421.3 15.3 %shard_map.276 = (f32[1024,1024]{1,0:T(8,128)}, bf16[1024,1024]{1,0:T(8,128)(2,1)}) custom-call(s32[3]{0:T(128)S(1)} %copy-done.97, bf16[256,2048]{1,0:T(8,128)(2,1)S(1)} %copy-done.19, bf16[256,2048]{1,0:T(8,128)(2,1)S(1)} %copy-done.38, bf16[256,2048]{1,0:T(8,128)(2,1)S(1)} %copy-done.40, bf16[256,2048]{1,0:T(8,128)(2,1)} %collective-permute-done.26.refs_4_, ...), custom_call_target="tpu_custom_call" | custom-call | flops 1000 | bytes 1000 | tf_op jit(solution)/shard_map/pallas_call | solution.py:80
  436.6 15.6 %shard_map.277 = (f32[1024,1024]{1,0:T(8,128)}, bf16[1024,1024]{1,0:T(8,128)(2,1)}) custom-call(s32[3]{0:T(128)S(1)} %copy-done.97, bf16[256,2048]{1,0:T(8,128)(2,1)S(1)} %copy-done.19, bf16[256,2048]{1,0:T(8,128)(2,1)S(1)} %copy-done.38, bf16[256,2048]{1,0:T(8,128)(2,1)S(1)} %copy-done.40, bf16[256,2048]{1,0:T(8,128)(2,1)} %collective-permute-done.26.refs_4_, ...), custom_call_target="tpu_custom_call" | custom-call | flops 1000 | bytes 1000 | tf_op jit(solution)/shard_map/pallas_call | solution.py:80
  478.7 16.0 %collective-permute-done.36.refs_3_ = bf16[208,2048]{1,0:T(8,128)(2,1)} collective-permute-done((bf16[208,2048]{1,0:T(8,128)(2,1)}, bf16[208,2048]{1,0:T(8,128)(2,1)}, u32[]{:S(2)}, u32[]{:S(2)}) %collective-permute-start.36) | collective-permute-done | bytes 852000 | tf_op jit(solution)/shard_map/ppermute | solution.py:729
  503.7 15.3 %collective-permute-done.44.refs_5_ = bf16[192,2048]{1,0:T(8,128)(2,1)S(1)} collective-permute-done((bf16[192,2048]{1,0:T(8,128)(2,1)S(1)}, bf16[192,2048]{1,0:T(8,128)(2,1)S(1)}, u32[]{:S(2)}, u32[]{:S(2)}) %collective-permute-start.44) | collective-permute-done | bytes 786464 | tf_op jit(solution)/shard_map/ppermute | solution.py:723
  519.0 16.1 %collective-permute-done.43.refs_4_ = bf16[192,2048]{1,0:T(8,128)(2,1)S(1)} collective-permute-done((bf16[192,2048]{1,0:T(8,128)(2,1)S(1)}, bf16[192,2048]{1,0:T(8,128)(2,1)S(1)}, u32[]{:S(2)}, u32[]{:S(2)}) %collective-permute-start.43) | collective-permute-done | bytes 786464 | tf_op jit(solution)/shard_map/ppermute | solution.py:723
  542.9 18.7 %shard_map.287 = (bf16[768,512]{1,0:T(8,128)(2,1)S(1)}, f32[768,512]{1,0:T(8,128)S(1)}, f32[768,512]{1,0:T(8,128)S(1)}, f32[8,768]{1,0:T(8,128)S(1)}, f32[8,512]{1,0:T(8,128)S(1)}) custom-call(s32[3]{0:T(128)S(1)} %copy-done.97, s32[1,4]{1,0:T(1,128)S(1)} %copy-done.145, bf16[192,2048]{1,0:T(8,128)(2,1)S(1)} %get-tuple-element.258.refs_2_, ...), custom_call_target="tpu_custom_call" | custom-call | flops 1000 | bytes 1000 | tf_op jit(solution)/shard_map/pallas_call | solution.py:80
  571.2 13.2 %shard_map.289 = (bf16[768,1536]{1,0:T(8,128)(2,1)}, f32[1024,1536]{1,0:T(8,128)}, bf16[1024,1536]{1,0:T(8,128)(2,1)}) custom-call(s32[3]{0:T(128)S(1)} %copy-done.97, f32[768,512]{1,0:T(8,128)S(1)} %copy-done.89, f32[768,512]{1,0:T(8,128)S(1)} %copy-done.91, bf16[768,512]{1,0:T(8,128)(2,1)S(1)} %copy-done.79, f32[768,512]{1,0:T(8,128)} %copy-done.20, ...), custom_call_target="tpu_custom_call" | custom-call | flops 1000 | bytes 1000 | tf_op jit(solution)/shard_map/pallas_call | solution.py:80
  587.6 6.8 collective-permute-done.53.refs_2_
  599.6 9.7 %shard_map.290 = (f32[192,2048]{1,0:T(8,128)S(1)}, bf16[192,2048]{1,0:T(8,128)(2,1)}, bf16[192,2048]{1,0:T(8,128)(2,1)}, bf16[192,2048]{1,0:T(8,128)(2,1)}) custom-call(s32[3]{0:T(128)S(1)} %copy-done.97, bf16[768,1536]{1,0:T(8,128)(2,1)S(1)} %copy-done.83, bf16[2048,1536]{1,0:T(8,128)(2,1)S(1)} %bitcast.72), custom_call_target="tpu_custom_call" | custom-call | flops 1000 | bytes 1000 | tf_op jit(solution)/shard_map/pallas_call | solution.py:80
  631.7 19.8 %collective-permute-done.65.refs_4_ = bf16[128,2048]{1,0:T(8,128)(2,1)S(1)} collective-permute-done((bf16[128,2048]{1,0:T(8,128)(2,1)S(1)}, bf16[128,2048]{1,0:T(8,128)(2,1)S(1)}, u32[]{:S(2)}, u32[]{:S(2)}) %collective-permute-start.65) | collective-permute-done | bytes 524320 | tf_op jit(solution)/shard_map/ppermute | solution.py:723
  653.9 23.2 %collective-permute-done.69.refs_3_ = bf16[256,1536]{1,0:T(8,128)(2,1)S(1)} collective-permute-done((bf16[256,1536]{1,0:T(8,128)(2,1)S(1)}, bf16[256,1536]{1,0:T(8,128)(2,1)S(1)}, u32[]{:S(2)}, u32[]{:S(2)}) %collective-permute-start.69) | collective-permute-done | bytes 786464 | tf_op jit(solution)/shard_map/ppermute | solution.py:729
  681.4 11.1 %collective-permute-done.70.refs_4_ = bf16[256,1536]{1,0:T(8,128)(2,1)S(1)} collective-permute-done((bf16[256,1536]{1,0:T(8,128)(2,1)S(1)}, bf16[256,1536]{1,0:T(8,128)(2,1)S(1)}, u32[]{:S(2)}, u32[]{:S(2)}) %collective-permute-start.70) | collective-permute-done | bytes 786464 | tf_op jit(solution)/shard_map/ppermute | solution.py:729
  736.4 7.4 collective-permute-done.67
  756.8 15.7 %collective-permute-done.89.refs_3_ = bf16[64,2048]{1,0:T(8,128)(2,1)S(1)} collective-permute-done((bf16[64,2048]{1,0:T(8,128)(2,1)}, bf16[64,2048]{1,0:T(8,128)(2,1)S(1)}, u32[]{:S(2)}, u32[]{:S(2)}) %collective-permute-start.89) | collective-permute-done | bytes 262176 | tf_op jit(solution)/shard_map/ppermute | solution.py:726
  799.9 14.9 %shard_map.301 = (f32[1024,1024]{1,0:T(8,128)}, bf16[1024,1024]{1,0:T(8,128)(2,1)}) custom-call(s32[3]{0:T(128)S(1)} %copy-done.97, bf16[128,2048]{1,0:T(8,128)(2,1)S(1)} %copy-done.48, bf16[128,2048]{1,0:T(8,128)(2,1)S(1)} %copy-done.63, bf16[128,2048]{1,0:T(8,128)(2,1)S(1)} %copy-done.65, bf16[128,2048]{1,0:T(8,128)(2,1)S(1)} %copy-done.67, ...), custom_call_target="tpu_custom_call" | custom-call | flops 1000 | bytes 1000 | tf_op jit(solution)/shard_map/pallas_call | solution.py:80
  814.8 25.0 %collective-permute-done.82.refs_3_ = bf16[64,6144]{1,0:T(8,128)(2,1)} collective-permute-done((bf16[64,6144]{1,0:T(8,128)(2,1)S(1)}, bf16[64,6144]{1,0:T(8,128)(2,1)}, u32[]{:S(2)}, u32[]{:S(2)}) %collective-permute-start.82) | collective-permute-done | bytes 786464 | tf_op jit(solution)/shard_map/ppermute | solution.py:726
  852.7 7.2 shard_map.299
  (593 shorter events, 319.7 us)
Async XLA Ops:
  7.2 83.0 %all-gather.5.cloned.1.call-start = ((), (), s32[]{:S(2)}) async-start(), calls=%async_computation | async-start | bytes 4259840 | tf_op jit(solution)/shard_map/all_gather | solution.py:784
  10.4 251.0 %all-gather.7.cloned.1.call-start = ((), (), s32[]{:S(2)}) async-start(), calls=%async_computation.1 | async-start | bytes 4259840 | tf_op jit(solution)/shard_map/all_gather | solution.py:842
  12.0 79.0 %collective-permute-start.2 = (bf16[208,2048]{1,0:T(8,128)(2,1)S(1)}, bf16[208,2048]{1,0:T(8,128)(2,1)S(1)}, u32[]{:S(2)}, u32[]{:S(2)}) collective-permute-start(bf16[208,2048]{1,0:T(8,128)(2,1)S(1)} %pad_maximum_fusion.refs_1_.refs_6_.refs_10_.refs_5_), channel_id=1, source_target_pairs={{0,3},{1,2},{2,1},{3,0},{4,7},{5,6},{6,5},{7,4},{8,11},{9,10},{10,... | collective-permute-start | bytes 2555912 | tf_op jit(solution)/shard_map/ppermute | solution.py:723
  13.2 77.8 %collective-permute-start.1 = (bf16[208,2048]{1,0:T(8,128)(2,1)S(1)}, bf16[208,2048]{1,0:T(8,128)(2,1)}, u32[]{:S(2)}, u32[]{:S(2)}) collective-permute-start(bf16[208,2048]{1,0:T(8,128)(2,1)S(1)} %pad_maximum_fusion.refs_1_.refs_6_.refs_10_.refs_5_), channel_id=1, source_target_pairs={{0,2},{1,3},{2,0},{3,1},{4,6},{5,7},{6,4},{7,5},{8,10},{9,11},{10,... | collective-permute-start | bytes 2555912 | tf_op jit(solution)/shard_map/ppermute | solution.py:723
  20.1 45.8 %collective-permute-start.3 = (bf16[256,1536]{1,0:T(8,128)(2,1)}, bf16[256,1536]{1,0:T(8,128)(2,1)S(1)}, u32[]{:S(2)}, u32[]{:S(2)}) collective-permute-start(bf16[256,1536]{1,0:T(8,128)(2,1)} %get-tuple-element.171), channel_id=1, source_target_pairs={{0,1},{1,0},{2,3},{3,2},{4,5},{5,4},{6,7},{7,6},{8,9},{9,8},{10,11... | collective-permute-start | bytes 2359304 | tf_op jit(solution)/shard_map/ppermute | solution.py:723
  21.3 47.1 %collective-permute-start.4 = (bf16[256,1536]{1,0:T(8,128)(2,1)}, bf16[256,1536]{1,0:T(8,128)(2,1)}, u32[]{:S(2)}, u32[]{:S(2)}) collective-permute-start(bf16[256,1536]{1,0:T(8,128)(2,1)} %get-tuple-element.172), channel_id=1, source_target_pairs={{0,2},{1,3},{2,0},{3,1},{4,6},{5,7},{6,4},{7,5},{8,10},{9,11},{10,... | collective-permute-start | bytes 2359304 | tf_op jit(solution)/shard_map/ppermute | solution.py:723
  36.1 50.5 %collective-permute-start.5 = (bf16[256,1536]{1,0:T(8,128)(2,1)S(1)}, bf16[256,1536]{1,0:T(8,128)(2,1)}, u32[]{:S(2)}, u32[]{:S(2)}) collective-permute-start(bf16[256,1536]{1,0:T(8,128)(2,1)S(1)} %shard_map.264), channel_id=1, source_target_pairs={{0,3},{1,2},{2,1},{3,0},{4,7},{5,6},{6,5},{7,4},{8,11},{9,10},{10,... | collective-permute-start | bytes 2359304 | tf_op jit(solution)/shard_map/ppermute | solution.py:723
  115.7 70.6 %collective-permute-start.18 = (bf16[1024,1024]{1,0:T(8,128)(2,1)}, bf16[1024,1024]{1,0:T(8,128)(2,1)S(1)}, u32[]{:S(2)}, u32[]{:S(2)}) collective-permute-start(bf16[1024,1024]{1,0:T(8,128)(2,1)} %bitcast.11.refs_13_), channel_id=1, source_target_pairs={{0,16},{16,0},{1,17},{17,1},{2,18},{18,2},{3,19},{19,3},{4,20},{20... | collective-permute-start | bytes 6291464 | tf_op jit(solution)/shard_map/ppermute | solution.py:732
  118.5 67.9 %collective-permute-start.19 = (bf16[1024,1024]{1,0:T(8,128)(2,1)}, bf16[1024,1024]{1,0:T(8,128)(2,1)}, u32[]{:S(2)}, u32[]{:S(2)}) collective-permute-start(bf16[1024,1024]{1,0:T(8,128)(2,1)} %bitcast.12.refs_15_), channel_id=1, source_target_pairs={{0,16},{16,0},{1,17},{17,1},{2,18},{18,2},{3,19},{19,3},{4,20},{20... | collective-permute-start | bytes 6291464 | tf_op jit(solution)/shard_map/ppermute | solution.py:732
  124.6 61.8 %collective-permute-start.20 = (bf16[1024,1024]{1,0:T(8,128)(2,1)S(1)}, bf16[1024,1024]{1,0:T(8,128)(2,1)S(1)}, u32[]{:S(2)}, u32[]{:S(2)}) collective-permute-start(bf16[1024,1024]{1,0:T(8,128)(2,1)S(1)} %bitcast.61), channel_id=1, source_target_pairs={{0,16},{16,0},{1,17},{17,1},{2,18},{18,2},{3,19},{19,3},{4,20},{20... | collective-permute-start | bytes 6291464 | tf_op jit(solution)/shard_map/ppermute | solution.py:732
  204.3 61.8 %collective-permute-start.21 = (bf16[384,2048]{1,0:T(8,128)(2,1)}, bf16[384,2048]{1,0:T(8,128)(2,1)S(1)}, u32[]{:S(2)}, u32[]{:S(2)}) collective-permute-start(bf16[384,2048]{1,0:T(8,128)(2,1)} %get-tuple-element.201), channel_id=1, source_target_pairs={{0,1},{1,0},{2,3},{3,2},{4,5},{5,4},{6,7},{7,6},{8,9},{9,8},{10,11... | collective-permute-start | bytes 4718600 | tf_op jit(solution)/shard_map/ppermute | solution.py:723
  204.6 61.5 %collective-permute-start.22 = (bf16[384,2048]{1,0:T(8,128)(2,1)}, bf16[384,2048]{1,0:T(8,128)(2,1)}, u32[]{:S(2)}, u32[]{:S(2)}) collective-permute-start(bf16[384,2048]{1,0:T(8,128)(2,1)} %get-tuple-element.202), channel_id=1, source_target_pairs={{0,2},{1,3},{2,0},{3,1},{4,6},{5,7},{6,4},{7,5},{8,10},{9,11},{10,... | collective-permute-start | bytes 4718600 | tf_op jit(solution)/shard_map/ppermute | solution.py:723
  204.8 66.9 %collective-permute-start.23 = (bf16[384,2048]{1,0:T(8,128)(2,1)}, bf16[384,2048]{1,0:T(8,128)(2,1)}, u32[]{:S(2)}, u32[]{:S(2)}) collective-permute-start(bf16[384,2048]{1,0:T(8,128)(2,1)} %get-tuple-element.203), channel_id=1, source_target_pairs={{0,3},{1,2},{2,1},{3,0},{4,7},{5,6},{6,5},{7,4},{8,11},{9,10},{10,... | collective-permute-start | bytes 4718600 | tf_op jit(solution)/shard_map/ppermute | solution.py:723
  273.3 42.8 %collective-permute-start.26 = (bf16[256,2048]{1,0:T(8,128)(2,1)S(1)}, bf16[256,2048]{1,0:T(8,128)(2,1)}, u32[]{:S(2)}, u32[]{:S(2)}) collective-permute-start(bf16[256,2048]{1,0:T(8,128)(2,1)S(1)} %get-tuple-element.207), channel_id=1, source_target_pairs={{0,3},{1,2},{2,1},{3,0},{4,7},{5,6},{6,5},{7,4},{8,11},{9,10},{10,... | collective-permute-start | bytes 3145736 | tf_op jit(solution)/shard_map/ppermute | solution.py:723
  316.7 43.8 %collective-permute-start.29 = (bf16[256,2048]{1,0:T(8,128)(2,1)}, bf16[256,2048]{1,0:T(8,128)(2,1)}, u32[]{:S(2)}, u32[]{:S(2)}) collective-permute-start(bf16[256,2048]{1,0:T(8,128)(2,1)} %get-tuple-element.218), channel_id=1, source_target_pairs={{0,3},{1,2},{2,1},{3,0},{4,7},{5,6},{6,5},{7,4},{8,11},{9,10},{10,... | collective-permute-start | bytes 3145736 | tf_op jit(solution)/shard_map/ppermute | solution.py:723
  360.7 43.9 %collective-permute-start.32 = (bf16[256,2048]{1,0:T(8,128)(2,1)}, bf16[256,2048]{1,0:T(8,128)(2,1)S(1)}, u32[]{:S(2)}, u32[]{:S(2)}) collective-permute-start(bf16[256,2048]{1,0:T(8,128)(2,1)} %get-tuple-element.230), channel_id=1, source_target_pairs={{0,3},{1,2},{2,1},{3,0},{4,7},{5,6},{6,5},{7,4},{8,11},{9,10},{10,... | collective-permute-start | bytes 3145736 | tf_op jit(solution)/shard_map/ppermute | solution.py:723
  405.5 50.7 %collective-permute-start.33 = (bf16[256,2048]{1,0:T(8,128)(2,1)}, bf16[256,2048]{1,0:T(8,128)(2,1)S(1)}, u32[]{:S(2)}, u32[]{:S(2)}) collective-permute-start(bf16[256,2048]{1,0:T(8,128)(2,1)} %get-tuple-element.232), channel_id=1, source_target_pairs={{0,1},{1,0},{2,3},{3,2},{4,5},{5,4},{6,7},{7,6},{8,9},{9,8},{10,11... | collective-permute-start | bytes 3145736 | tf_op jit(solution)/shard_map/ppermute | solution.py:723
  405.7 50.6 %collective-permute-start.34 = (bf16[256,2048]{1,0:T(8,128)(2,1)}, bf16[256,2048]{1,0:T(8,128)(2,1)}, u32[]{:S(2)}, u32[]{:S(2)}) collective-permute-start(bf16[256,2048]{1,0:T(8,128)(2,1)} %get-tuple-element.233), channel_id=1, source_target_pairs={{0,2},{1,3},{2,0},{3,1},{4,6},{5,7},{6,4},{7,5},{8,10},{9,11},{10,... | collective-permute-start | bytes 3145736 | tf_op jit(solution)/shard_map/ppermute | solution.py:723
  405.7 50.6 %collective-permute-start.35 = (bf16[256,2048]{1,0:T(8,128)(2,1)}, bf16[256,2048]{1,0:T(8,128)(2,1)}, u32[]{:S(2)}, u32[]{:S(2)}) collective-permute-start(bf16[256,2048]{1,0:T(8,128)(2,1)} %get-tuple-element.234), channel_id=1, source_target_pairs={{0,3},{1,2},{2,1},{3,0},{4,7},{5,6},{6,5},{7,4},{8,11},{9,10},{10,... | collective-permute-start | bytes 3145736 | tf_op jit(solution)/shard_map/ppermute | solution.py:723
  418.6 42.0 %collective-permute-start.37 = (bf16[208,2048]{1,0:T(8,128)(2,1)}, bf16[208,2048]{1,0:T(8,128)(2,1)}, u32[]{:S(2)}, u32[]{:S(2)}) collective-permute-start(bf16[208,2048]{1,0:T(8,128)(2,1)} %shard_map.275.refs_11_), channel_id=1, source_target_pairs={{0,8},{4,12},{8,0},{12,4},{1,9},{5,13},{9,1},{13,5},{2,10},{6,14},... | collective-permute-start | bytes 2555912 | tf_op jit(solution)/shard_map/ppermute | solution.py:729
  421.3 73.5 %collective-permute-start.36 = (bf16[208,2048]{1,0:T(8,128)(2,1)}, bf16[208,2048]{1,0:T(8,128)(2,1)}, u32[]{:S(2)}, u32[]{:S(2)}) collective-permute-start(bf16[208,2048]{1,0:T(8,128)(2,1)} %shard_map.274.refs_6_), channel_id=1, source_target_pairs={{0,4},{4,8},{8,12},{12,0},{1,5},{5,9},{9,13},{13,1},{2,6},{6,10},{... | collective-permute-start | bytes 2555912 | tf_op jit(solution)/shard_map/ppermute | solution.py:729
  503.7 64.4 %collective-permute-start.48 = (bf16[192,2048]{1,0:T(8,128)(2,1)S(1)}, bf16[192,2048]{1,0:T(8,128)(2,1)S(1)}, u32[]{:S(2)}, u32[]{:S(2)}) collective-permute-start(bf16[192,2048]{1,0:T(8,128)(2,1)S(1)} %shard_map.285.refs_6_), channel_id=1, source_target_pairs={{0,8},{4,12},{8,0},{12,4},{1,9},{5,13},{9,1},{13,5},{2,10},{6,14},... | collective-permute-start | bytes 2359304 | tf_op jit(solution)/shard_map/ppermute | solution.py:729
  625.9 51.2 %collective-permute-start.69 = (bf16[256,1536]{1,0:T(8,128)(2,1)S(1)}, bf16[256,1536]{1,0:T(8,128)(2,1)S(1)}, u32[]{:S(2)}, u32[]{:S(2)}) collective-permute-start(bf16[256,1536]{1,0:T(8,128)(2,1)S(1)} %get-tuple-element.308), channel_id=1, source_target_pairs={{0,8},{4,12},{8,0},{12,4},{1,9},{5,13},{9,1},{13,5},{2,10},{6,14},... | collective-permute-start | bytes 2359304 | tf_op jit(solution)/shard_map/ppermute | solution.py:729
  630.2 62.3 %collective-permute-start.70 = (bf16[256,1536]{1,0:T(8,128)(2,1)S(1)}, bf16[256,1536]{1,0:T(8,128)(2,1)S(1)}, u32[]{:S(2)}, u32[]{:S(2)}) collective-permute-start(bf16[256,1536]{1,0:T(8,128)(2,1)S(1)} %get-tuple-element.309), channel_id=1, source_target_pairs={{0,12},{4,0},{8,4},{12,8},{1,13},{5,1},{9,5},{13,9},{2,14},{6,2},{... | collective-permute-start | bytes 2359304 | tf_op jit(solution)/shard_map/ppermute | solution.py:729
  630.2 63.7 %collective-permute-start.68 = (bf16[256,1536]{1,0:T(8,128)(2,1)S(1)}, bf16[256,1536]{1,0:T(8,128)(2,1)S(1)}, u32[]{:S(2)}, u32[]{:S(2)}) collective-permute-start(bf16[256,1536]{1,0:T(8,128)(2,1)S(1)} %get-tuple-element.290), channel_id=1, source_target_pairs={{0,4},{4,8},{8,12},{12,0},{1,5},{5,9},{9,13},{13,1},{2,6},{6,10},{... | collective-permute-start | bytes 2359304 | tf_op jit(solution)/shard_map/ppermute | solution.py:729
  651.5 62.5 %collective-permute-start.57 = (bf16[192,2048]{1,0:T(8,128)(2,1)}, bf16[192,2048]{1,0:T(8,128)(2,1)}, u32[]{:S(2)}, u32[]{:S(2)}) collective-permute-start(bf16[192,2048]{1,0:T(8,128)(2,1)} %get-tuple-element.291), channel_id=1, source_target_pairs={{0,1},{1,0},{2,3},{3,2},{4,5},{5,4},{6,7},{7,6},{8,9},{9,8},{10,11... | collective-permute-start | bytes 2359304 | tf_op jit(solution)/shard_map/ppermute | solution.py:723
  652.5 61.6 %collective-permute-start.58 = (bf16[192,2048]{1,0:T(8,128)(2,1)}, bf16[192,2048]{1,0:T(8,128)(2,1)}, u32[]{:S(2)}, u32[]{:S(2)}) collective-permute-start(bf16[192,2048]{1,0:T(8,128)(2,1)} %get-tuple-element.292), channel_id=1, source_target_pairs={{0,2},{1,3},{2,0},{3,1},{4,6},{5,7},{6,4},{7,5},{8,10},{9,11},{10,... | collective-permute-start | bytes 2359304 | tf_op jit(solution)/shard_map/ppermute | solution.py:723
  778.2 81.6 %collective-permute-start.95 = (bf16[1024,1024]{1,0:T(8,128)(2,1)}, bf16[1024,1024]{1,0:T(8,128)(2,1)}, u32[]{:S(2)}, u32[]{:S(2)}) collective-permute-start(bf16[1024,1024]{1,0:T(8,128)(2,1)} %get-tuple-element.324), channel_id=1, source_target_pairs={{0,16},{16,0},{1,17},{17,1},{2,18},{18,2},{3,19},{19,3},{4,20},{20... | collective-permute-start | bytes 6291464 | tf_op jit(solution)/shard_map/ppermute | solution.py:732
  778.9 60.9 %collective-permute-start.82 = (bf16[64,6144]{1,0:T(8,128)(2,1)S(1)}, bf16[64,6144]{1,0:T(8,128)(2,1)}, u32[]{:S(2)}, u32[]{:S(2)}) collective-permute-start(bf16[64,6144]{1,0:T(8,128)(2,1)S(1)} %shard_map.297.refs_11_.refs_1_), channel_id=1, source_target_pairs={{0,8},{4,12},{8,0},{12,4},{1,9},{5,13},{9,1},{13,5},{2,10},{6,14},... | collective-permute-start | bytes 2359304 | tf_op jit(solution)/shard_map/ppermute | solution.py:726
  785.1 59.1 %collective-permute-start.81 = (bf16[64,6144]{1,0:T(8,128)(2,1)S(1)}, bf16[64,6144]{1,0:T(8,128)(2,1)}, u32[]{:S(2)}, u32[]{:S(2)}) collective-permute-start(bf16[64,6144]{1,0:T(8,128)(2,1)S(1)} %shard_map.297.refs_11_.refs_1_), channel_id=1, source_target_pairs={{0,12},{4,0},{8,4},{12,8},{1,13},{5,1},{9,5},{13,9},{2,14},{6,2},{... | collective-permute-start | bytes 2359304 | tf_op jit(solution)/shard_map/ppermute | solution.py:726
  791.1 53.6 %collective-permute-start.87 = (bf16[64,6144]{1,0:T(8,128)(2,1)S(1)}, bf16[64,6144]{1,0:T(8,128)(2,1)}, u32[]{:S(2)}, u32[]{:S(2)}) collective-permute-start(bf16[64,6144]{1,0:T(8,128)(2,1)S(1)} %collective-permute-done.83.refs_4_), channel_id=1, source_target_pairs={{0,16},{16,0},{1,17},{17,1},{2,18},{18,2},{3,19},{19,3},{4,20},{20... | collective-permute-start | bytes 2359304 | tf_op jit(solution)/shard_map/ppermute | solution.py:732
  794.3 70.4 %collective-permute-start.96 = (bf16[1024,1024]{1,0:T(8,128)(2,1)}, bf16[1024,1024]{1,0:T(8,128)(2,1)}, u32[]{:S(2)}, u32[]{:S(2)}) collective-permute-start(bf16[1024,1024]{1,0:T(8,128)(2,1)} %get-tuple-element.325), channel_id=1, source_target_pairs={{0,16},{16,0},{1,17},{17,1},{2,18},{18,2},{3,19},{19,3},{4,20},{20... | collective-permute-start | bytes 6291464 | tf_op jit(solution)/shard_map/ppermute | solution.py:732
  (237 other events, 3694.4 us)
Sparse Core Ops, SparseCore 0:
  10.6 66.4 all-gather.4
  194.9 66.4 all-gather.6
